TPU v7x, 32 devices: a whole 2x2x4 slice. The times are simulated.
32 devices in a mesh: seq: 16 (over z, x, core), heads: 2 (over y).
Axes of the slice: x: 2, y: 2, z: 4, core: 2. Of those that a mesh axis runs over, the one named last changes fastest.
Arguments:
- inputs: float32 [50176, 512], P('seq'), may hold values from -6 to 6
- w_qkv: float32 [3, 512, 512], P(None, 'seq', 'heads'), may hold values from -0.25 to 0.25
- w_proj: float32 [512, 512], P('heads', 'seq'), may hold values from -3 to 3
- w_fc1: float32 [512, 2048], P('seq', 'heads'), may hold values from -0.25 to 0.25
- w_fc2: float32 [2048, 512], P('heads', 'seq'), may hold values from -0.125 to 0.125
- gains: float32 [2, 512], replicated, may hold values from 0.1 to 1.9
- shifts: float32 [4, 512], replicated, may hold values from -3 to 3
- rel_table: float32 [16, 2535], P('heads'), may hold values from -4 to 4
- region: int32 [50176], P('seq'), may hold values from 0 to 2
- pos_index: int32 [392, 392], replicated, may hold values from 0 to 2534
- out_grad: float32 [50176, 512], P('seq'), may hold values from -6 to 6
Outputs:
- output: float32 [50176, 512], P('seq')
- d_inputs: float32 [50176, 512], P('seq')
- d_qkv: float32 [3, 512, 512], P(None, 'seq', 'heads')
- d_proj: float32 [512, 512], P('heads', 'seq')
- d_fc1: float32 [512, 2048], P('seq', 'heads')
- d_fc2: float32 [2048, 512], P('heads', 'seq')
- d_gains: float32 [2, 512], replicated
- d_shifts: float32 [4, 512], replicated
- d_table: float32 [16, 2535], P('heads')
All inputs are finite; a program needn't handle non-finite values.
Results may differ from a plain program's by a relative error of at most 0.012.
The roundings to bfloat16 on the way count: a program that leaves them out, or rounds other values in their place, can miss the bound.
Values may be sent and summed in bfloat16 or wider, within the bound.
A program may use at most 320 MiB of HBM per device.

v0:
```python
import jax
import jax.numpy as jnp
from jax import lax
from jax.sharding import PartitionSpec as P

WT = 8
WH = 7
WW = 7
WIN = 392
SHIFT = 196
TABLE = 2535


eps_norm = 1e-05
fill_value = -100.0
highest = lax.Precision.HIGHEST


def shifted(block, axis, distance):
    devices = range(lax.axis_size(axis))
    route = [((i - distance) % len(devices), i) for i in devices]
    return lax.ppermute(block, axis, route)


def normalize(rows_in, gain_vec, shift_vec):
    row_mean = jnp.mean(rows_in, axis=-1, keepdims=True)
    centred = rows_in - row_mean
    variance = jnp.mean(centred * centred, axis=-1, keepdims=True)
    return centred * lax.rsqrt(variance + eps_norm) * gain_vec + shift_vec


def gelu_exact(values):
    return jax.nn.gelu(values, approximate=False)


def pair_blocks():
    return 4


def index_parts(block_index):
    inner_count = (2 * WH - 1) * (2 * WW - 1)
    outer_count = 2 * WT - 1
    inner_index = block_index % inner_count
    outer_index = block_index // inner_count
    inner_hot = (inner_index[:, None] == jnp.arange(inner_count, dtype=jnp.int32)[None, :]).astype(
        jnp.float32
    )
    outer_hot = (outer_index[:, None] == jnp.arange(outer_count, dtype=jnp.int32)[None, :]).astype(
        jnp.float32
    )
    return (inner_hot, outer_hot)


def table_lookup(table, pos_index):
    heads_here = table.shape[0]
    inner_count = (2 * WH - 1) * (2 * WW - 1)
    outer_count = 2 * WT - 1
    table_three = table.reshape(heads_here, outer_count, inner_count)
    count_blocks = pair_blocks()
    index_rows = pos_index.reshape(count_blocks, WIN * WIN // count_blocks)

    def lookup_block(block_index):
        inner_hot, outer_hot = index_parts(block_index)
        picked = jnp.einsum("pl,hol->pho", inner_hot, table_three, precision=highest)
        return jnp.einsum("pho,po->hp", picked, outer_hot, precision=highest)

    looked = lax.map(lookup_block, index_rows)
    return jnp.transpose(looked, (1, 0, 2)).reshape(heads_here, WIN, WIN)


def table_gradient(summed, pos_index):
    heads_here = summed.shape[0]
    count_blocks = pair_blocks()
    per_block = WIN * WIN // count_blocks
    index_rows = pos_index.reshape(count_blocks, per_block)
    summed_rows = jnp.transpose(summed.reshape(heads_here, count_blocks, per_block), (1, 0, 2))

    def scatter_block(piece):
        block_index, block_grad = piece
        inner_hot, outer_hot = index_parts(block_index)
        weighted = block_grad[:, :, None] * outer_hot[None]
        return jnp.einsum("hpo,pl->hol", weighted, inner_hot, precision=highest)

    pieces = lax.map(scatter_block, (index_rows, summed_rows))
    return jnp.sum(pieces, axis=0).reshape(heads_here, TABLE)


def gather_seq(qkv_low, proj_low, fc1_low, fc2_low):
    return (
        lax.all_gather(qkv_low, "seq", axis=1, tiled=True),
        lax.all_gather(proj_low, "seq", axis=1, tiled=True),
        lax.all_gather(fc1_low, "seq", axis=0, tiled=True),
        lax.all_gather(fc2_low, "seq", axis=1, tiled=True),
    )


def sum_heads(values):
    return lax.psum(values, "heads")


def grads_to_owners(g_one, g_two, g_three, g_four):
    return (
        lax.psum_scatter(g_one, "seq", scatter_dimension=1, tiled=True),
        lax.psum_scatter(g_two, "seq", scatter_dimension=1, tiled=True),
        lax.psum_scatter(g_three, "seq", scatter_dimension=0, tiled=True),
        lax.psum_scatter(g_four, "seq", scatter_dimension=1, tiled=True),
    )


def small_sum(g_one, g_two, g_three):
    return lax.psum((g_one, g_two, g_three), "seq")


def pull_next(values):
    incoming = shifted(values[:SHIFT], "seq", -1)
    return jnp.concatenate([values[SHIFT:], incoming], axis=0)


def push_prev_low(values):
    trailing = shifted(values[values.shape[0] - SHIFT :], "seq", 1)
    return jnp.concatenate([trailing, values[: values.shape[0] - SHIFT]], axis=0)


def push_prev_full(values):
    trailing = shifted(values[values.shape[0] - SHIFT :].astype(jnp.bfloat16), "seq", 1).astype(
        jnp.float32
    )
    return jnp.concatenate([trailing, values[: values.shape[0] - SHIFT]], axis=0)


def scores_of(q_rows, k_rows, pos_bias, labels, score_scale):
    raw_scores = (
        jnp.einsum("wqhd,wkhd->whqk", q_rows, k_rows, preferred_element_type=jnp.float32)
        * score_scale
    )
    same_region = labels[:, :, None] == labels[:, None, :]
    return raw_scores + pos_bias[None] + jnp.where(same_region, 0.0, fill_value)[:, None]


def attend(rolled, qkv_w, table, labels, pos_index):
    heads_here = table.shape[0]
    tok_count = rolled.shape[0]
    windows = tok_count // WIN
    head_size = qkv_w.shape[2] // heads_here
    score_scale = head_size ** (-0.5)
    qkv = jnp.einsum("td,cde->cte", rolled, qkv_w, preferred_element_type=jnp.float32).astype(
        jnp.bfloat16
    )
    blocks = qkv.reshape(3, windows, WIN, heads_here, head_size)
    pos_bias = table_lookup(table, pos_index)
    scores = scores_of(blocks[0], blocks[1], pos_bias, labels, score_scale)
    row_max = jnp.max(scores, axis=-1, keepdims=True)
    shifted_exp = jnp.exp(scores - row_max)
    row_total = jnp.sum(shifted_exp, axis=-1, keepdims=True)
    log_total = row_max + jnp.log(row_total)
    probs_low = (shifted_exp / row_total).astype(jnp.bfloat16)
    attn_mixed = jnp.einsum(
        "whqk,wkhd->wqhd", probs_low, blocks[2], preferred_element_type=jnp.float32
    )
    attn_mixed = attn_mixed.astype(jnp.bfloat16).reshape(tok_count, heads_here * head_size)
    return (blocks, pos_bias, log_total, probs_low, attn_mixed)


def attend_back(
    g_branch, proj_w, qkv_w, rolled, blocks, pos_bias, labels, log_total, probs_low, pos_index
):
    q_rows, k_rows, v_rows = (blocks[0], blocks[1], blocks[2])
    windows, heads_here, head_size = (q_rows.shape[0], q_rows.shape[2], q_rows.shape[3])
    tok_count = rolled.shape[0]
    score_scale = head_size ** (-0.5)
    g_mixed = jnp.dot(g_branch, proj_w.T, preferred_element_type=jnp.float32).astype(jnp.bfloat16)
    g_mixed = g_mixed.reshape(windows, WIN, heads_here, head_size)
    scores = scores_of(q_rows, k_rows, pos_bias, labels, score_scale)
    attn_probs = jnp.exp(scores - log_total)
    g_probs = jnp.einsum("wqhd,wkhd->whqk", g_mixed, v_rows, preferred_element_type=jnp.float32)
    row_inner = jnp.sum(g_probs * attn_probs, axis=-1, keepdims=True)
    g_scores = (attn_probs * (g_probs - row_inner)).astype(jnp.bfloat16)
    g_value = jnp.einsum("whqk,wqhd->wkhd", probs_low, g_mixed, preferred_element_type=jnp.float32)
    g_query = (
        jnp.einsum("whqk,wkhd->wqhd", g_scores, k_rows, preferred_element_type=jnp.float32)
        * score_scale
    )
    g_key = (
        jnp.einsum("whqk,wqhd->wkhd", g_scores, q_rows, preferred_element_type=jnp.float32)
        * score_scale
    )
    g_qkv = (
        jnp.stack([g_query, g_key, g_value])
        .astype(jnp.bfloat16)
        .reshape(3, tok_count, heads_here * head_size)
    )
    summed = jnp.sum(g_scores.astype(jnp.float32), axis=0).reshape(heads_here, WIN * WIN)
    g_table = table_gradient(summed, pos_index)
    g_wqkv = jnp.einsum("td,cte->cde", rolled, g_qkv, preferred_element_type=jnp.float32)
    g_rolled_part = jnp.einsum("cte,cde->td", g_qkv, qkv_w, preferred_element_type=jnp.float32)
    return (g_wqkv, g_table, g_rolled_part)


def mlp_forward(normed_two, fc1_w, fc2_w):
    hidden = jnp.dot(normed_two, fc1_w, preferred_element_type=jnp.float32)
    active, gelu_pull = jax.vjp(gelu_exact, hidden)
    active_low = active.astype(jnp.bfloat16)
    partial_value = jnp.dot(active_low, fc2_w, preferred_element_type=jnp.float32)
    return (active_low, gelu_pull, partial_value)


def mlp_back(top_grad, active_low, normed_two, gelu_pull, fc1_w, fc2_w):
    g_fc2 = jnp.dot(active_low.T, top_grad, preferred_element_type=jnp.float32)
    g_active = jnp.dot(top_grad, fc2_w.T, preferred_element_type=jnp.float32)
    g_hidden = gelu_pull(g_active)[0].astype(jnp.bfloat16)
    g_fc1 = jnp.dot(normed_two.T, g_hidden, preferred_element_type=jnp.float32)
    g_normed_part = jnp.dot(g_hidden, fc1_w.T, preferred_element_type=jnp.float32)
    return (g_fc2, g_fc1, g_normed_part)


def body(
    inputs, w_qkv, w_proj, w_fc1, w_fc2, gains, shifts, rel_table, region, pos_index, out_grad
):
    tok_count = inputs.shape[0]
    qkv_low = w_qkv.astype(jnp.bfloat16)
    proj_low = w_proj.astype(jnp.bfloat16)
    fc1_low = w_fc1.astype(jnp.bfloat16)
    fc2_low = w_fc2.astype(jnp.bfloat16)
    normed_one = normalize(inputs, gains[0], shifts[0]).astype(jnp.bfloat16)
    qkv_w, proj_w, fc1_w, fc2_w = gather_seq(qkv_low, proj_low, fc1_low, fc2_low)
    rolled = pull_next(normed_one)
    labels = region.reshape(tok_count // WIN, WIN)
    blocks, pos_bias, log_total, probs_low, attn_mixed = attend(
        rolled, qkv_w, rel_table, labels, pos_index
    )
    partial_value = jnp.dot(attn_mixed, proj_w, preferred_element_type=jnp.float32)
    branch = (sum_heads(partial_value) + shifts[2]).astype(jnp.bfloat16)
    middle = inputs + push_prev_low(branch).astype(jnp.float32)
    normed_two = normalize(middle, gains[1], shifts[1]).astype(jnp.bfloat16)
    active_low, gelu_pull, partial_up = mlp_forward(normed_two, fc1_w, fc2_w)
    output = middle + sum_heads(partial_up) + shifts[3]
    qkv_w, proj_w, fc1_w, fc2_w = gather_seq(qkv_low, proj_low, fc1_low, fc2_low)
    top_grad = out_grad.astype(jnp.bfloat16)
    g_fc2, g_fc1, g_normed_part = mlp_back(
        top_grad, active_low, normed_two, gelu_pull, fc1_w, fc2_w
    )
    g_normed_two = sum_heads(g_normed_part)
    unused_two, norm_pull_two = jax.vjp(normalize, middle, gains[1], shifts[1])
    g_ln_two, g_gain_two, g_shift_two = norm_pull_two(g_normed_two)
    g_middle = out_grad + g_ln_two
    g_branch = pull_next(g_middle.astype(jnp.bfloat16))
    g_proj = jnp.dot(attn_mixed.T, g_branch, preferred_element_type=jnp.float32)
    g_wqkv, g_table, g_rolled_part = attend_back(
        g_branch, proj_w, qkv_w, rolled, blocks, pos_bias, labels, log_total, probs_low, pos_index
    )
    g_rolled = sum_heads(g_rolled_part)
    g_first = push_prev_full(g_rolled)
    unused_one, norm_pull_one = jax.vjp(normalize, inputs, gains[0], shifts[0])
    g_ln_one, g_gain_one, g_shift_one = norm_pull_one(g_first)
    g_inputs = g_middle + g_ln_one
    d_qkv, d_proj, d_fc1, d_fc2 = grads_to_owners(g_wqkv, g_proj, g_fc1, g_fc2)
    g_gains = jnp.stack([g_gain_one, g_gain_two])
    g_shifts = jnp.stack(
        [
            g_shift_one,
            g_shift_two,
            jnp.sum(g_branch.astype(jnp.float32), axis=0),
            jnp.sum(top_grad.astype(jnp.float32), axis=0),
        ]
    )
    d_table, d_gains, d_shifts = small_sum(g_table, g_gains, g_shifts)
    return (output, g_inputs, d_qkv, d_proj, d_fc1, d_fc2, d_gains, d_shifts, d_table)


def solution(mesh):
    placed = (
        P("seq", None),
        P(None, "seq", "heads"),
        P("heads", "seq"),
        P("seq", "heads"),
        P("heads", "seq"),
        P(),
        P(),
        P("heads", None),
        P("seq"),
        P(),
        P("seq", None),
    )
    return jax.shard_map(
        body,
        mesh=mesh,
        in_specs=placed,
        out_specs=(
            P("seq", None),
            P("seq", None),
            P(None, "seq", "heads"),
            P("heads", "seq"),
            P("seq", "heads"),
            P("heads", "seq"),
            P(),
            P(),
            P("heads", None),
        ),
        check_vma=False,
    )
```

profile of v0, /device:TPU:0, one launch (start us, length us, event | category | flops | bytes accessed | tf_op | source)
XLA Modules:
  0.0 1676.8 jit_solution(2849051259127982260)
XLA Ops:
  14.2 4.1 multiply_reduce_fusion.6
  22.3 6.0 collective-permute-start
  29.2 113.7 %while.24 = (s32[]{:T(128)}, f32[4,8,38416]{2,1,0:T(8,128)}, s32[4,38416]{1,0:T(4,128)S(1)}, f32[8,15,169]{2,1,0:T(8,128)S(1)}, s32[]{:T(128)}) while((s32[]{:T(128)}, f32[4,8,38416]{2,1,0:T(8,128)}, s32[4,38416]{1,0:T(4,128)S(1)}, f32[8,15,169]{2,1,0:T(8,128)S(1)}, s32[]{:T(128)}) %tuple.89), condition=%wide.region_3.4_spmd, body=%wide.region_2.3_spmd.sunk | while | flops 9365936128 | bytes 9996113 | solution.py:67
  31.4 25.1 %fusion.111 = f32[38416,8]{0,1:T(8,128)S(1)} fusion(f32[8,15,169]{2,1,0:T(8,128)S(1)} %get-tuple-element.313, s32[38416]{0:T(1024)S(1)} %get-tuple-element.290, f32[38416,15]{0,1:T(8,128)S(1)} %fusion.110), kind=kOutput, calls=%fused_computation.24.clone.1 | convolution fusion | flops 9364322304 | bytes 3769056 | tf_op jit(solution)/shard_map/while/body/eval_jaxpr/pl,hol->pho/dot_general | solution.py:64
  59.8 25.1 %fusion.111 = f32[38416,8]{0,1:T(8,128)S(1)} fusion(f32[8,15,169]{2,1,0:T(8,128)S(1)} %get-tuple-element.313, s32[38416]{0:T(1024)S(1)} %get-tuple-element.290, f32[38416,15]{0,1:T(8,128)S(1)} %fusion.110), kind=kOutput, calls=%fused_computation.24.clone.1 | convolution fusion | flops 9364322304 | bytes 3769056 | tf_op jit(solution)/shard_map/while/body/eval_jaxpr/pl,hol->pho/dot_general | solution.py:64
  88.2 25.1 %fusion.111 = f32[38416,8]{0,1:T(8,128)S(1)} fusion(f32[8,15,169]{2,1,0:T(8,128)S(1)} %get-tuple-element.313, s32[38416]{0:T(1024)S(1)} %get-tuple-element.290, f32[38416,15]{0,1:T(8,128)S(1)} %fusion.110), kind=kOutput, calls=%fused_computation.24.clone.1 | convolution fusion | flops 9364322304 | bytes 3769056 | tf_op jit(solution)/shard_map/while/body/eval_jaxpr/pl,hol->pho/dot_general | solution.py:64
  116.6 25.1 %fusion.111 = f32[38416,8]{0,1:T(8,128)S(1)} fusion(f32[8,15,169]{2,1,0:T(8,128)S(1)} %get-tuple-element.313, s32[38416]{0:T(1024)S(1)} %get-tuple-element.290, f32[38416,15]{0,1:T(8,128)S(1)} %fusion.110), kind=kOutput, calls=%fused_computation.24.clone.1 | convolution fusion | flops 9364322304 | bytes 3769056 | tf_op jit(solution)/shard_map/while/body/eval_jaxpr/pl,hol->pho/dot_general | solution.py:64
  146.4 21.6 %all_gather.16 = bf16[3,512,256]{2,1,0:T(8,128)(2,1)} all-gather(bf16[3,32,256]{2,1,0:T(8,128)(2,1)S(1)} %convert_element_type.86), channel_id=1, replica_groups=mesh['seq'=16,'heads'=2] {'seq'}, dimensions={1}, use_global_device_ids=true | all-gather | bytes 835584 | tf_op jit(solution)/shard_map/all_gather | solution.py:90
  173.9 7.6 add.186
  181.5 8.2 copy.95
  189.7 19.3 %all_gather.17 = bf16[256,512]{0,1:T(8,128)(2,1)S(1)} all-gather(bf16[256,32]{0,1:T(8,128)(2,1)S(1)} %convert_element_type.92), channel_id=1, replica_groups=mesh['seq'=16,'heads'=2] {'seq'}, dimensions={1}, use_global_device_ids=true | all-gather | bytes 278528 | tf_op jit(solution)/shard_map/all_gather | solution.py:91
  218.0 5.8 squeeze.17
  226.1 6.1 squeeze.19
  232.2 4.0 copy.90
  236.2 6.9 squeeze.18
  243.1 26.3 %fusion.68 = (f32[8,8,392]{2,1,0:T(8,128)S(1)}, f32[8,8,392,392]{2,3,1,0:T(8,128)}) fusion(f32[8,392,392]{1,2,0:T(8,128)} %compare_select_fusion, f32[8,392,392]{1,2,0:T(8,128)} %copy.95, bf16[8,392,8,32]{1,0,3,2:T(8,128)(2,1)S(1)} %squeeze.19, bf16[8,392,8,32]{1,0,3,2:T(8,128)(2,1)} %squeeze.18), kind=kOutput, calls=%fused_computation.137 | convolution fusion | flops 668720640 | bytes 52484096 | tf_op jit(solution)/shard_map/wqhd,wkhd->whqk/dot_general | solution.py:133
  269.4 16.9 %fusion.26 = f32[8,8,392]{2,1,0:T(8,128)S(1)} fusion(f32[8,8,392,392]{2,3,1,0:T(8,128)} %get-tuple-element.230, f32[8,8,392]{2,1,0:T(8,128)S(1)} %get-tuple-element.229), kind=kLoop, calls=%fused_computation.41 | loop fusion | flops 19643904 | bytes 39538688 | tf_op jit(solution)/shard_map/reduce_sum | solution.py:154
  286.2 26.6 %divide_convert_fusion = bf16[8,8,392,392]{2,3,1,0:T(8,128)(2,1)} fusion(f32[8,8,392,392]{2,3,1,0:T(8,128)} %get-tuple-element.230, f32[8,8,392]{2,1,0:T(8,128)S(1)} %fusion.26, f32[8,8,392]{2,1,0:T(8,128)S(1)} %get-tuple-element.229), kind=kLoop, calls=%fused_computation.38 | loop fusion | flops 29503488 | bytes 59207680 | tf_op jit(solution)/shard_map/convert_element_type | solution.py:156
  312.9 12.8 convert_bitcast_fusion.1
  328.2 4.0 reshape.262
  336.9 152.7 %all-reduce.9.cloned.1.call-done = f32[3136,512]{1,0:T(8,128)} async-done(((f32[3136,512]{1,0:T(8,128)}), f32[3136,512]{1,0:T(8,128)}) %all-reduce.9.cloned.1.call-update) | async-done | bytes 6422544 | tf_op jit(solution)/shard_map/psum | solution.py:98
  494.4 7.0 collective-permute-done.1
  501.4 4.1 fusion.64
  509.7 34.6 %multiply_convert_fusion.1 = (bf16[3136,1024]{1,0:T(8,128)(2,1)}, f32[3136,1024]{1,0:T(8,128)}, f32[3136,1024]{1,0:T(8,128)}) fusion(bf16[512,1024]{1,0:T(8,128)(2,1)} %all-gather.3.cloned.1.call-done, f32[3136,512]{1,0:T(8,128)} %copy-done.1, f32[512]{0:T(512)S(1)} %bitcast.154, f32[512]{0:T(512)S(1)} %bitcast.141, f32[3136]{0:T(1024)S(1)} %fusion.50, ...), kind=kOutput, calls=%fused_computation.45 | convolution fusion | flops 3505094656 | bytes 39612928 | tf_op jit(solution)/shard_map/dot_general | solution.py:200
  544.3 16.5 add_convert_fusion
  560.8 8.4 fusion.71
  569.3 153.4 %all-reduce.11.cloned.1.call-done = f32[3136,512]{1,0:T(8,128)} async-done(((f32[3136,512]{1,0:T(8,128)}), f32[3136,512]{1,0:T(8,128)}) %all-reduce.11.cloned.1.call-update) | async-done | bytes 6422544 | tf_op jit(solution)/shard_map/psum | solution.py:98
  722.7 9.0 multiply_reduce_fusion.1
  731.8 6.1 fusion.62
  740.6 4.1 collective-permute-start.2
  751.2 5.7 reshape.263
  756.9 14.4 convert_bitcast_fusion
  771.2 33.9 %multiply_reduce_fusion = (f32[8,8,392]{2,1,0:T(8,128)S(1)}, f32[8,8,392,392]{2,3,1,0:T(8,128)}) fusion(f32[8,8,392,392]{2,3,1,0:T(8,128)} %get-tuple-element.230, f32[8,8,392]{2,1,0:T(8,128)S(1)} %log_add_fusion, bf16[8,392,8,32]{1,0,3,2:T(8,128)(2,1)S(1)} %copy-done.9, bf16[8,392,8,32]{1,0,3,2:T(8,128)(2,1)} %reshape.263), kind=kOutput, calls=%fused_computation.36 | convolution fusion | flops 658886144 | bytes 82087936 | tf_op jit(solution)/shard_map/wqhd,wkhd->whqk/dot_general | solution.py:175
  805.1 47.7 %convert_reduce_fusion = (f32[8,392,392]{1,2,0:T(8,128)}, bf16[8,8,392,392]{2,3,1,0:T(8,128)(2,1)}) fusion(f32[8,8,392,392]{2,3,1,0:T(8,128)} %get-tuple-element.233, f32[8,8,392]{2,1,0:T(8,128)S(1)} %get-tuple-element.232, f32[8,8,392,392]{2,3,1,0:T(8,128)} %get-tuple-element.230, f32[8,8,392]{2,1,0:T(8,128)S(1)} %log_add_fusion), kind=kLoop, calls=%fused_computation.34 | loop fusion | flops 57777664 | bytes 103462912 | tf_op jit(solution)/shard_map/reduce_sum | solution.py:192
  852.9 14.6 fusion.35
  867.5 14.3 fusion.34
  890.2 8.0 copy.115
  898.2 7.9 reshape_reshape.3
  906.1 4.3 copy.104
  910.4 4.9 stack.28
  928.0 145.2 %while.25 = (s32[]{:T(128)}, f32[4,8,15,169]{3,2,1,0:T(8,128)}, f32[4,8,38416]{2,0,1:T(4,128)}, s32[4,38416]{1,0:T(4,128)S(1)}, s32[]{:T(128)}) while((s32[]{:T(128)}, f32[4,8,15,169]{3,2,1,0:T(8,128)}, f32[4,8,38416]{2,0,1:T(4,128)}, s32[4,38416]{1,0:T(4,128)S(1)}, s32[]{:T(128)}) %tuple.117), condition=%wide.region_32.33_spmd, body=%wide.region_31.32_spmd.sunk | while | flops 9361633280 | bytes 50667124 | solution.py:84
  935.2 9.2 fusion.115
  944.5 20.1 %fusion.116 = f32[4,8,15,169]{3,2,1,0:T(8,128)} fusion(f32[4,8,15,169]{3,2,1,0:T(8,128)} %get-tuple-element.321, s32[]{:T(128)S(6)} %copy.171, s32[38416]{0:T(1024)S(1)} %get-tuple-element.298, f32[8,38416,15]{1,2,0:T(8,128)} %fusion.115), kind=kOutput, calls=%fused_computation.11.clone.3 | convolution fusion | flops 9355409408 | bytes 20011076 | tf_op jit(solution)/shard_map/while/body/eval_jaxpr/hpo,pl->hol/dot_general | solution.py:82
  971.4 9.2 fusion.115
  980.7 20.1 %fusion.116 = f32[4,8,15,169]{3,2,1,0:T(8,128)} fusion(f32[4,8,15,169]{3,2,1,0:T(8,128)} %get-tuple-element.321, s32[]{:T(128)S(6)} %copy.171, s32[38416]{0:T(1024)S(1)} %get-tuple-element.298, f32[8,38416,15]{1,2,0:T(8,128)} %fusion.115), kind=kOutput, calls=%fused_computation.11.clone.3 | convolution fusion | flops 9355409408 | bytes 20011076 | tf_op jit(solution)/shard_map/while/body/eval_jaxpr/hpo,pl->hol/dot_general | solution.py:82
  1007.6 9.2 fusion.115
  1016.9 20.1 %fusion.116 = f32[4,8,15,169]{3,2,1,0:T(8,128)} fusion(f32[4,8,15,169]{3,2,1,0:T(8,128)} %get-tuple-element.321, s32[]{:T(128)S(6)} %copy.171, s32[38416]{0:T(1024)S(1)} %get-tuple-element.298, f32[8,38416,15]{1,2,0:T(8,128)} %fusion.115), kind=kOutput, calls=%fused_computation.11.clone.3 | convolution fusion | flops 9355409408 | bytes 20011076 | tf_op jit(solution)/shard_map/while/body/eval_jaxpr/hpo,pl->hol/dot_general | solution.py:82
  1043.8 9.2 fusion.115
  1053.1 20.1 %fusion.116 = f32[4,8,15,169]{3,2,1,0:T(8,128)} fusion(f32[4,8,15,169]{3,2,1,0:T(8,128)} %get-tuple-element.321, s32[]{:T(128)S(6)} %copy.171, s32[38416]{0:T(1024)S(1)} %get-tuple-element.298, f32[8,38416,15]{1,2,0:T(8,128)} %fusion.115), kind=kOutput, calls=%fused_computation.11.clone.3 | convolution fusion | flops 9355409408 | bytes 20011076 | tf_op jit(solution)/shard_map/while/body/eval_jaxpr/hpo,pl->hol/dot_general | solution.py:82
  1075.0 6.3 fusion.46
  1083.3 8.7 fusion.70
  1092.0 4.6 convolution_bitcast_fusion.1
  1097.3 10.1 fusion.59
  1107.5 9.8 fusion.56
  1119.0 4.7 fusion.47
  1126.1 55.3 %all-reduce.13.cloned.1.call-done = (f32[3,512,256]{2,0,1:T(4,128)}, f32[8,2535]{1,0:T(8,128)}) async-done(((f32[3,512,256]{2,0,1:T(4,128)}, f32[8,2535]{1,0:T(8,128)}), (f32[3,512,256]{2,0,1:T(4,128)}, f32[8,2535]{1,0:T(8,128)})) %all-reduce.13.cloned.1.call-update) | async-done | bytes 1654000
  1183.0 295.4 %all-reduce.15.cloned.1.call-done = (f32[3136,512]{1,0:T(8,128)}, f32[3136,512]{1,0:T(8,128)}) async-done(((f32[3136,512]{1,0:T(8,128)}, f32[3136,512]{1,0:T(8,128)}), (f32[3136,512]{1,0:T(8,128)}, f32[3136,512]{1,0:T(8,128)})) %all-reduce.15.cloned.1.call-update) | async-done | bytes 12845072 | tf_op jit(solution)/shard_map/psum | solution.py:98
  1479.6 9.2 add_add_fusion.5
  1492.7 4.5 multiply_reduce_fusion.2
  1497.2 5.7 fusion.61
  1503.1 10.1 convert_reduce_fusion.1
  1513.2 62.0 %all-reduce.1 = (f32[2,512]{1,0:T(2,128)}, f32[4,512]{1,0:T(4,128)}) all-reduce(f32[2,512]{1,0:T(2,128)S(1)} %pad_maximum_fusion.10, f32[4,512]{1,0:T(4,128)S(1)} %pad_maximum_fusion.9), channel_id=1, replica_groups=mesh['seq'=16,'heads'=2] {'seq'}, use_global_device_ids=true, to_apply=%region_23.24 | all-reduce | flops 3072 | bytes 24576 | tf_op jit(solution)/shard_map/psum | solution.py:111
  1575.2 34.5 %reduce-scatter.8.cloned.1.call-done = f32[1024,32]{0,1:T(8,128)} async-done(((f32[1024,512]{0,1:T(8,128)}), f32[1024,32]{0,1:T(8,128)}) %reduce-scatter.8.cloned.1.call-update) | async-done | bytes 131088 | tf_op jit(solution)/shard_map/reduce_scatter | solution.py:106
  1609.6 58.8 %reduce-scatter.4.cloned.1.call-done = f32[256,32]{0,1:T(8,128)} async-done(((f32[256,512]{0,1:T(8,128)}), f32[256,32]{0,1:T(8,128)}) %reduce-scatter.4.cloned.1.call-update) | async-done | bytes 32784 | tf_op jit(solution)/shard_map/reduce_scatter | solution.py:104
  (274 shorter events, 133.2 us)
Async XLA Ops:
  8.0 481.6 %all-reduce.9.cloned.1.call-start = ((), (), s32[]{:S(2)}) async-start(), calls=%async_computation.3 | async-start | bytes 12845056 | tf_op jit(solution)/shard_map/psum | solution.py:98
  9.4 8.9 copy-start.48
  14.2 4.7 copy-start
  14.2 6.4 copy-start.29
  18.3 10.0 copy-start.53
  18.3 10.1 copy-start.45
  18.3 10.1 copy-start.46
  18.3 10.3 copy-start.27
  22.3 186.8 %collective-permute-start = (bf16[196,512]{1,0:T(8,128)(2,1)S(1)}, bf16[196,512]{1,0:T(8,128)(2,1)}, u32[]{:S(2)}, u32[]{:S(2)}) collective-permute-start(bf16[196,512]{1,0:T(8,128)(2,1)S(1)} %slice.78), channel_id=1, source_target_pairs={{2,0},{4,2},{6,4},{8,6},{10,8},{12,10},{14,12},{16,14},{18,16},{20... | collective-permute-start | bytes 602120 | tf_op jit(solution)/shard_map/ppermute | solution.py:22
  142.9 27.5 %copy-start.4 = (s32[4,38416]{1,0:T(4,128)}, s32[4,38416]{1,0:T(4,128)S(1)}, u32[]{:S(2)}) copy-start(s32[4,38416]{1,0:T(4,128)S(1)} %get-tuple-element.357) | copy-start | bytes 1843972
  142.9 25.2 %copy-start.11 = (bf16[3136,512]{1,0:T(8,128)(2,1)S(1)}, bf16[3136,512]{1,0:T(8,128)(2,1)}, u32[]{:S(2)}) copy-start(bf16[3136,512]{1,0:T(8,128)(2,1)} %copy-done.10) | copy-start | bytes 9633796
  142.9 27.5 %copy-start.50 = (f32[256,32]{0,1:T(8,128)S(1)}, f32[256,32]{0,1:T(8,128)}, u32[]{:S(2)}) copy-start(f32[256,32]{0,1:T(8,128)} %param.17) | copy-start | bytes 98308
  142.9 27.5 %copy-start.16 = (f32[4,8,38416]{2,1,0:T(8,128)S(1)}, f32[4,8,38416]{2,1,0:T(8,128)}, u32[]{:S(2)}) copy-start(f32[4,8,38416]{2,1,0:T(8,128)} %get-tuple-element.121) | copy-start | bytes 14751748
  181.5 27.5 %copy-start.17 = (bf16[2940,512]{1,0:T(8,128)(2,1)S(1)}, bf16[2940,512]{1,0:T(8,128)(2,1)}, u32[]{:S(2)}) copy-start(bf16[2940,512]{1,0:T(8,128)(2,1)} %slice.77) | copy-start | bytes 9031684
  209.0 123.2 %copy-start.25 = (bf16[256,512]{0,1:T(8,128)(2,1)}, bf16[256,512]{0,1:T(8,128)(2,1)S(1)}, u32[]{:S(2)}) copy-start(bf16[256,512]{0,1:T(8,128)(2,1)S(1)} %all_gather.17) | copy-start | bytes 786436
  232.2 37.2 %copy-start.6 = (bf16[8,392,8,32]{1,0,3,2:T(8,128)(2,1)}, bf16[8,392,8,32]{1,0,3,2:T(8,128)(2,1)S(1)}, u32[]{:S(2)}) copy-start(bf16[8,392,8,32]{1,0,3,2:T(8,128)(2,1)S(1)} %squeeze.19) | copy-start | bytes 4816900
  269.4 16.9 %copy-start.18 = (f32[8,8,392]{2,1,0:T(8,128)}, f32[8,8,392]{2,1,0:T(8,128)S(1)}, u32[]{:S(2)}) copy-start(f32[8,8,392]{2,1,0:T(8,128)S(1)} %get-tuple-element.229) | copy-start | bytes 301060
  286.2 26.6 %copy-start.23 = (f32[8,8,392]{2,1,0:T(8,128)}, f32[8,8,392]{2,1,0:T(8,128)S(1)}, u32[]{:S(2)}) copy-start(f32[8,8,392]{2,1,0:T(8,128)S(1)} %fusion.26) | copy-start | bytes 301060
  286.2 26.6 %copy-start.8 = (bf16[8,392,8,32]{1,0,3,2:T(8,128)(2,1)S(1)}, bf16[8,392,8,32]{1,0,3,2:T(8,128)(2,1)}, u32[]{:S(2)}) copy-start(bf16[8,392,8,32]{1,0,3,2:T(8,128)(2,1)} %squeeze.17) | copy-start | bytes 4816900
  332.3 157.3 %copy-start.57 = (f32[1,512]{1,0:T(1,128)S(1)}, f32[1,512]{1,0:T(1,128)}, u32[]{:S(2)}) copy-start(f32[1,512]{1,0:T(1,128)} %get-tuple-element.224) | copy-start | bytes 6148
  336.1 157.3 %copy-start.44 = (f32[1024,32]{0,1:T(8,128)S(1)}, f32[1024,32]{0,1:T(8,128)}, u32[]{:S(2)}) copy-start(f32[1024,32]{0,1:T(8,128)} %param.19) | copy-start | bytes 393220
  336.1 173.6 %all-gather.3.cloned.1.call-start = ((), (), s32[]{:S(2)}) async-start(), calls=%async_computation.4 | async-start | bytes 1114112 | tf_op jit(solution)/shard_map/all_gather | solution.py:92
  336.9 207.5 %all-gather.5.cloned.1.call-start = ((), (), s32[]{:S(2)}) async-start(), calls=%async_computation.5 | async-start | bytes 1114112 | tf_op jit(solution)/shard_map/all_gather | solution.py:93
  493.4 8.0 collective-permute-start.1
  494.1 228.6 %all-reduce.11.cloned.1.call-start = ((), (), s32[]{:S(2)}) async-start(), calls=%async_computation.6 | async-start | bytes 12845056 | tf_op jit(solution)/shard_map/psum | solution.py:98
  505.5 4.2 copy-start.51
  505.5 226.2 %copy-start.31 = (f32[3136]{0:T(1024)}, f32[3136]{0:T(1024)S(1)}, u32[]{:S(2)}) copy-start(f32[3136]{0:T(1024)S(1)} %broadcast_multiply_fusion) | copy-start | bytes 37636
  509.7 222.1 %copy-start.39 = (f32[3136]{0:T(1024)}, f32[3136]{0:T(1024)S(1)}, u32[]{:S(2)}) copy-start(f32[3136]{0:T(1024)S(1)} %fusion.50) | copy-start | bytes 37636
  544.3 16.5 copy-start.61
  569.3 612.1 %all-reduce.13.cloned.1.call-start = ((), (), s32[]{:S(2)}) async-start(), calls=%async_computation.10 | async-start | bytes 4358144
  722.7 9.1 copy-start.3
  722.7 15.3 slice-start.4
  731.8 6.2 slice-start.5
  738.0 6.7 copy-start.19
  738.0 6.7 copy-start.24
  740.6 8.1 copy-start.26
  740.6 7.4 collective-permute-start.2
  756.9 14.4 copy-start.9
  852.9 14.6 copy-start.7
  867.5 14.3 copy-start.14
  906.1 13.0 copy-start.13
  915.3 12.7 copy-start.5
  1075.0 8.2 copy-start.60
  1083.2 395.3 %all-reduce.15.cloned.1.call-start = ((), (), s32[]{:S(2)}) async-start(), calls=%async_computation.11 | async-start | bytes 25690112 | tf_op jit(solution)/shard_map/psum | solution.py:98
  1083.2 8.7 copy-start.20
  1083.2 8.7 copy-start.21
  1083.2 8.7 copy-start.22
  1083.3 8.7 copy-start.28
  1096.6 478.5 %reduce-scatter.6.cloned.1.call-start = ((), (), s32[]{:S(2)}) async-start(), calls=%async_computation.8 | async-start | bytes 2228224 | tf_op jit(solution)/shard_map/reduce_scatter | solution.py:105
  1107.5 10.2 copy-start.62
  1107.5 11.4 copy-start.36
  1107.5 502.1 %reduce-scatter.8.cloned.1.call-start = ((), (), s32[]{:S(2)}) async-start(), calls=%async_computation.9 | async-start | bytes 2228224 | tf_op jit(solution)/shard_map/reduce_scatter | solution.py:106
  1117.4 551.1 %reduce-scatter.4.cloned.1.call-start = ((), (), s32[]{:S(2)}) async-start(), calls=%async_computation.7 | async-start | bytes 557056 | tf_op jit(solution)/shard_map/reduce_scatter | solution.py:104
  1118.9 360.6 %copy-start.55 = (f32[1,512]{1,0:T(1,128)S(1)}, f32[1,512]{1,0:T(1,128)}, u32[]{:S(2)}) copy-start(f32[1,512]{1,0:T(1,128)} %get-tuple-element.223) | copy-start | bytes 6148
  1119.0 373.6 %slice-start = ((s8[6422528]{0:T(1024)(128)(4,1)}), s8[2228224]{0:T(1024)(128)(4,1)S(1)}, s32[]{:S(2)}) async-start(s8[6422528]{0:T(1024)(128)(4,1)} %bitcast.129), calls=%async_computation.12 | async-start | bytes 4456448
  1479.5 13.0 collective-permute-start.3
  1479.6 13.0 slice-start.1
  1492.7 4.5 copy-start.42
  1492.7 10.3 slice-start.2
  1497.2 5.8 copy-start.54
  1497.2 5.8 slice-start.3
  1497.2 5.8 copy-start.38
  1503.0 10.2 copy-start.56
  1503.0 165.4 %copy-start.47 = (f32[8,2535]{1,0:T(8,128)S(1)}, f32[8,2535]{1,0:T(8,128)}, u32[]{:S(2)}) copy-start(f32[8,2535]{1,0:T(8,128)} %get-tuple-element.338) | copy-start | bytes 243364
  (18 other events, 47.1 us)
Sparse Core Ops, SparseCore 0:
  336.2 153.3 all-reduce.8
  569.4 153.2 all-reduce.10
Sparse Core Ops, SparseCore 1:
  339.6 35.4 all-gather.2
  494.2 38.2 all-gather.4
  1083.2 98.1 all-reduce.12
  1184.0 294.4 all-reduce.14
  1482.8 61.5 reduce-scatter.5
  1549.1 60.5 reduce-scatter.7
  1613.6 54.8 reduce-scatter.3
where the time goes:
time: 1680 us
  waiting for transfers between devices  760 us (45%)
  matrix products  410 us (24%)
  other arithmetic  222 us (13%)
  local copies, waits for them, and re-layouts  153 us (9%)
  blocking collectives  103 us (6%)
  between operations  17.5 us (1%)
    psum x3, waiting for transfers between devices, sum_heads(): return lax.psum(values, 'heads')  602 us
    dot_general x4, matrix products, lookup_block(): jnp.einsum('pl,hol->pho', inner_hot, table_three, precision=highest)  100 us
    dot_general x4, matrix products, scatter_block(): return jnp.einsum('hpo,pl->hol', weighted, inner_hot, precision=highest)  80.5 us
    psum x1, blocking collectives, small_sum(): return lax.psum((g_one, g_two, g_three), 'seq')  62 us
    reduce_scatter x1, waiting for transfers between devices, grads_to_owners(): lax.psum_scatter(g_two, 'seq', scatter_dimension=1, tiled=True)  58.8 us
    unnamed x10, waiting for transfers between devices  55.4 us
    reduce_sum x1, other arithmetic, attend_back(): jnp.sum(g_scores.astype(jnp.float32), axis=0).reshape(heads_here, WIN * WIN)  47.7 us
    dot_general x4, other arithmetic, scatter_block(): return jnp.einsum('hpo,pl->hol', weighted, inner_hot, precision=highest)  36.9 us
  transfers between devices with their start and end apart: 13, of which 8 were waited for; matrix products, arithmetic and copies ran while one was open for 16% of the time, Pallas kernels for 0%

commit v1 on v0

v1 whole, which is shorter than its diff:
```python
import functools
import math

import jax, jax.numpy as jnp
from jax import lax
from jax.experimental import pallas as pl
from jax.experimental.pallas import tpu as pltpu
from jax.sharding import PartitionSpec as P

BF=jnp.bfloat16; F32=jnp.float32
HD=32; GROUP=128; PER=4
EPS=1e-5
SQ=math.sqrt(32.0)
CEXP=math.log2(math.e)/SQ
MASK=100.0*SQ

def mm(a,b):
    return lax.dot_general(a,b,(((1,),(0,)),((),())),preferred_element_type=F32)
def mm_nt(a,b):
    return lax.dot_general(a,b,(((1,),(1,)),((),())),preferred_element_type=F32)

def norm_stats(v):
    mean=jnp.mean(v,axis=-1,keepdims=True)
    c=v-mean
    var=jnp.mean(c*c,axis=-1,keepdims=True)
    rstd=lax.rsqrt(var+EPS)
    return c*rstd, rstd

def norm_back(gy,xhat,rstd,gain):
    gx=gy*gain
    m1=jnp.mean(gx,axis=-1,keepdims=True)
    m2=jnp.mean(gx*xhat,axis=-1,keepdims=True)
    return rstd*(gx-m1-xhat*m2)

P0=0.3275911
A1,A2,A3,A4,A5=0.254829592,-0.284496736,1.421413741,-1.453152027,1.061405429
def gelu_both(x):
    e=jnp.exp2(x*x*(-0.5*math.log2(math.e)))
    t=1.0/(1.0+(P0/math.sqrt(2.0))*jnp.abs(x))
    poly=t*(0.5*A1+t*(0.5*A2+t*(0.5*A3+t*(0.5*A4+t*(0.5*A5)))))
    half=poly*e
    phi=jnp.where(x>=0,1.0-half,half)
    return x*phi, phi+x*e*(1.0/math.sqrt(2.0*math.pi))

def kernel_a(nheads, x_ref,og_ref,labc_ref,labr_ref,bias_ref,wqkv_ref,projT_ref,fc1_ref,fc2T_ref,gains_ref,shifts_ref,
             delta_ref,gln2_ref,qkv_ref,g_ref,gT_ref,D_ref,P_hbm,dfc1_ref,dfc2T_ref,dprojT_ref,small_ref,
             qT_s,vT_s,OT_s,P_s,afc1,afc2,aproj,sem,xn2_s,xn2T_s,tg_s,tgT_s,up_s,gn2_s):
    w=pl.program_id(0); nw=pl.num_programs(0)
    D=x_ref.shape[-1]; WIN=x_ref.shape[-2]; FF=fc1_ref.shape[1]
    groups=nheads//PER
    x=x_ref[0]
    xhat,_=norm_stats(x)
    xn=(xhat*gains_ref[0:1,:]+shifts_ref[0:1,:]).astype(BF)
    for c in range(3):
        y=mm(xn,wqkv_ref[:,c*D:(c+1)*D]).astype(BF)
        qkv_ref[0,c]=y
        if c==0: qT_s[...]=y.T
        if c==2: vT_s[...]=y.T
    labc=labc_ref[0]; labr=labr_ref[0]
    lane=lax.broadcasted_iota(jnp.int32,(WIN,GROUP),1)
    oh=jnp.where((labc==lane)|((labc+3)==lane),1.0,0.0).astype(BF)
    hi=564.0
    lo=MASK-564.0
    sub=lax.broadcasted_iota(jnp.int32,(GROUP,WIN),0)
    nm=jnp.where(sub<3,jnp.where(sub!=labr,-hi,0.0),jnp.where(sub<6,jnp.where(sub-3!=labr,-lo,0.0),0.0)).astype(BF)
    hl=lane//HD

    def group(gi,_):
        slot=gi%2
        step=w*groups+gi
        @pl.when(step>=2)
        def _():
            pltpu.make_async_copy(P_s.at[slot],P_hbm.at[0,pl.ds(0,PER)],sem.at[slot]).wait()
        o=pl.multiple_of(gi*GROUP,GROUP)
        qTg=jnp.concatenate([qT_s[pl.ds(o,GROUP),:],nm],axis=0)
        kg=qkv_ref[0,1,:,pl.ds(o,GROUP)]
        for hh in range(PER):
            kh=jnp.concatenate([jnp.where(hl==hh,kg,jnp.zeros_like(kg)),oh],axis=1)
            t=mm(kh,qTg)+bias_ref[gi*PER+hh]
            m=jnp.max(t,axis=0,keepdims=True)
            e=jnp.exp2((t-m)*CEXP)
            l=jnp.sum(e,axis=0,keepdims=True)
            p=(e*(1.0/l)).astype(BF)
            P_s[slot,hh]=p
            OT_s[pl.ds(o+hh*HD,HD),:]=mm(vT_s[pl.ds(o+hh*HD,HD),:],p)
        pltpu.make_async_copy(P_s.at[slot],P_hbm.at[w,pl.ds(gi*PER,PER)],sem.at[slot]).start()
        return 0
    lax.fori_loop(0,groups,group,0)

    attn=OT_s[...].astype(BF).T
    branch=(mm_nt(attn,projT_ref[...])+shifts_ref[2:3,:]).astype(BF).astype(F32)
    middle=x+branch
    xhat2,rstd2=norm_stats(middle)
    xn2=(xhat2*gains_ref[1:2,:]+shifts_ref[1:2,:]).astype(BF)
    og=og_ref[0]
    tg=og.astype(BF)
    xn2_s[...]=xn2; xn2T_s[...]=xn2.T; tg_s[...]=tg; tgT_s[...]=tg.T
    up_s[...]=jnp.zeros_like(up_s); gn2_s[...]=jnp.zeros_like(gn2_s)
    CH=min(512,FF)
    @pl.when(w==0)
    def _():
        afc1[...]=jnp.zeros_like(afc1); afc2[...]=jnp.zeros_like(afc2); aproj[...]=jnp.zeros_like(aproj)
        small_ref[...]=jnp.zeros_like(small_ref)
    def chunk(c,_):
        o=pl.multiple_of(c*CH,CH)
        f1=fc1_ref[:,pl.ds(o,CH)]; f2=fc2T_ref[:,pl.ds(o,CH)]
        hid=mm(xn2_s[...],f1)
        act,dact=gelu_both(hid)
        a=act.astype(BF)
        up_s[...]+=mm_nt(a,f2)
        gh=(mm(tg_s[...],f2)*dact).astype(BF)
        gn2_s[...]+=mm_nt(gh,f1)
        afc1[:,pl.ds(o,CH)]+=mm(xn2T_s[...],gh)
        afc2[:,pl.ds(o,CH)]+=mm(tgT_s[...],a)
        return 0
    lax.fori_loop(0,FF//CH,chunk,0)
    delta_ref[0]=(branch+up_s[...]+shifts_ref[3:4,:]).astype(BF)
    gn2=gn2_s[...]
    gln2=norm_back(gn2,xhat2,rstd2,gains_ref[1:2,:])
    gln2_ref[0]=gln2
    gb=(og+gln2).astype(BF)
    aproj[...]+=mm(gb.T,attn)
    g=mm(gb,projT_ref[...]).astype(BF)
    g_ref[0]=g
    gT=g.T
    gT_ref[0]=gT
    prod=gT.astype(F32)*OT_s[...]
    D_ref[0]=jnp.sum(prod.reshape(nheads,HD,WIN),axis=1)
    small_ref[1:2,:]+=jnp.sum(gn2*xhat2,axis=0,keepdims=True)
    small_ref[3:4,:]+=jnp.sum(gn2,axis=0,keepdims=True)
    small_ref[4:5,:]+=jnp.sum(gb.astype(F32),axis=0,keepdims=True)
    small_ref[5:6,:]+=jnp.sum(tg.astype(F32),axis=0,keepdims=True)
    @pl.when(w==nw-1)
    def _():
        dfc1_ref[...]=afc1[...].astype(BF); dfc2T_ref[...]=afc2[...].astype(BF); dprojT_ref[...]=aproj[...].astype(BF)
        for s in range(2):
            pltpu.make_async_copy(P_s.at[s],P_hbm.at[0,pl.ds(0,PER)],sem.at[s]).wait()

def full(shape,**kw):
    return pl.BlockSpec(shape,lambda w:(0,)*len(shape),**kw)
def per(shape):
    return pl.BlockSpec((1,)+shape,lambda w:(w,)+(0,)*len(shape))
ONE=pl.Buffered(1)

def call_a(x,og,labc,labr,bias,wqkv,projT,fc1,fc2T,gains,shifts):
    nW,WIN,D=x.shape; FF=fc1.shape[1]; NH=bias.shape[0]
    sd=jax.ShapeDtypeStruct
    outs=[sd((nW,WIN,D),BF),sd((nW,WIN,D),F32),sd((nW,3,WIN,D),BF),sd((nW,WIN,D),BF),sd((nW,D,WIN),BF),sd((nW,NH,WIN),F32),
          sd((nW,NH,WIN,WIN),BF),sd((D,FF),BF),sd((D,FF),BF),sd((D,D),BF),sd((8,D),F32)]
    return pl.pallas_call(functools.partial(kernel_a,NH),grid=(nW,),
      in_specs=[per((WIN,D)),per((WIN,D)),per((WIN,1)),per((1,WIN)),full((NH,WIN,WIN),pipeline_mode=ONE),
        full((D,3*D),pipeline_mode=ONE),full((D,D),pipeline_mode=ONE),full((D,FF),pipeline_mode=ONE),full((D,FF),pipeline_mode=ONE),
        full(gains.shape),full(shifts.shape)],
      out_specs=[per((WIN,D)),per((WIN,D)),per((3,WIN,D)),per((WIN,D)),per((D,WIN)),per((NH,WIN)),pl.BlockSpec(memory_space=pl.ANY),
        full((D,FF)),full((D,FF)),full((D,D)),full((8,D))],
      out_shape=outs,
      scratch_shapes=[pltpu.VMEM((D,WIN),BF),pltpu.VMEM((D,WIN),BF),pltpu.VMEM((D,WIN),F32),pltpu.VMEM((2,PER,WIN,WIN),BF),
        pltpu.VMEM((D,FF),F32),pltpu.VMEM((D,FF),F32),pltpu.VMEM((D,D),F32),pltpu.SemaphoreType.DMA((2,)),
        pltpu.VMEM((WIN,D),BF),pltpu.VMEM((D,WIN),BF),pltpu.VMEM((WIN,D),BF),pltpu.VMEM((D,WIN),BF),pltpu.VMEM((WIN,D),F32),pltpu.VMEM((WIN,D),F32)],
      compiler_params=pltpu.CompilerParams(vmem_limit_bytes=62*1024*1024,dimension_semantics=("arbitrary",)),
      name="kernel_a")(x,og,labc,labr,bias,wqkv,projT,fc1,fc2T,gains,shifts)

def kernel_b(nheads,x_ref,gln2_ref,qkv_ref,g_ref,gT_ref,D_ref,P_ref,wqkv_ref,gains_ref,shifts_ref,
             dd_ref,dqkv_ref,G_hbm,small_ref, G_s,aq,kT_s,gq_s,gqT_s,sem):
    w=pl.program_id(0); nw=pl.num_programs(0)
    D=x_ref.shape[-1]; WIN=x_ref.shape[-2]
    groups=nheads//PER
    @pl.when(w==0)
    def _():
        aq[...]=jnp.zeros_like(aq); G_s[...]=jnp.zeros_like(G_s); small_ref[...]=jnp.zeros_like(small_ref)
    kT_s[...]=qkv_ref[0,1].T
    lane=lax.broadcasted_iota(jnp.int32,(WIN,GROUP),1)
    hl=lane//HD
    def group(gi,_):
        o=pl.multiple_of(gi*GROUP,GROUP)
        gTg=gT_ref[0,pl.ds(o,GROUP),:]
        vg=qkv_ref[0,2,:,pl.ds(o,GROUP)]
        qg=qkv_ref[0,0,:,pl.ds(o,GROUP)]
        gg=g_ref[0,:,pl.ds(o,GROUP)]
        dv=jnp.zeros((WIN,GROUP),F32); dk=jnp.zeros((WIN,GROUP),F32)
        zero=jnp.zeros_like(vg)
        for hh in range(PER):
            h=gi*PER+hh
            p=P_ref[0,h]
            dp=mm(jnp.where(hl==hh,vg,zero),gTg)
            ds=p.astype(F32)*(dp-D_ref[0,pl.ds(h,1),:])
            for c in range(G_s.shape[0]):
                wd=min(128,WIN-c*128)
                G_s[c,pl.ds(pl.multiple_of(h*WIN,8),WIN),:wd]+=ds[:,c*128:c*128+wd]
            dsl=ds.astype(BF)
            dv+=mm(p,jnp.where(hl==hh,gg,zero))
            dk+=mm(dsl,jnp.where(hl==hh,qg,zero))
            gqT_s[pl.ds(o+hh*HD,HD),:]=mm(kT_s[pl.ds(o+hh*HD,HD),:],dsl)
        gq_s[1,:,pl.ds(o,GROUP)]=(dk*(1.0/SQ)).astype(BF)
        gq_s[2,:,pl.ds(o,GROUP)]=dv.astype(BF)
        return 0
    lax.fori_loop(0,groups,group,0)
    gq_s[0]=(gqT_s[...]*(1.0/SQ)).astype(BF).T
    x=x_ref[0]
    xhat,rstd=norm_stats(x)
    xn=(xhat*gains_ref[0:1,:]+shifts_ref[0:1,:]).astype(BF)
    xnT=xn.T
    gr=jnp.zeros((WIN,D),F32)
    for c in range(3):
        gc=gq_s[c]
        gr=gr+mm_nt(gc,wqkv_ref[:,c*D:(c+1)*D])
        aq[:,c*D:(c+1)*D]+=mm(xnT,gc)
    dd_ref[0]=(gln2_ref[0]+norm_back(gr,xhat,rstd,gains_ref[0:1,:])).astype(BF)
    small_ref[0:1,:]+=jnp.sum(gr*xhat,axis=0,keepdims=True)
    small_ref[2:3,:]+=jnp.sum(gr,axis=0,keepdims=True)
    @pl.when(w==nw-1)
    def _():
        dqkv_ref[...]=aq[...].astype(BF)
        cp=pltpu.make_async_copy(G_s,G_hbm,sem); cp.start(); cp.wait()

def call_b(x,gln2,qkv,g,gT,Dd,Pp,wqkv,gains,shifts):
    nW,WIN,D=x.shape; NH=Dd.shape[1]
    sd=jax.ShapeDtypeStruct
    return pl.pallas_call(functools.partial(kernel_b,NH),grid=(nW,),
      in_specs=[per((WIN,D)),per((WIN,D)),per((3,WIN,D)),per((WIN,D)),per((D,WIN)),per((NH,WIN)),per((NH,WIN,WIN)),
        full((D,3*D),pipeline_mode=ONE),full(gains.shape),full(shifts.shape)],
      out_specs=[per((WIN,D)),full((D,3*D)),pl.BlockSpec(memory_space=pl.ANY),full((8,D))],
      out_shape=[sd((nW,WIN,D),BF),sd((D,3*D),BF),sd((-(-WIN//128),NH*WIN,128),F32),sd((8,D),F32)],
      scratch_shapes=[pltpu.VMEM((-(-WIN//128),NH*WIN,128),F32),pltpu.VMEM((D,3*D),F32),pltpu.VMEM((D,WIN),BF),pltpu.VMEM((3,WIN,D),BF),pltpu.VMEM((D,WIN),F32),pltpu.SemaphoreType.DMA],
      compiler_params=pltpu.CompilerParams(vmem_limit_bytes=62*1024*1024,dimension_semantics=("arbitrary",)),
      name="kernel_b")(x,gln2,qkv,g,gT,Dd,Pp,wqkv,gains,shifts)

FIX=8191.0

def pack_table(table):
    NH,T=table.shape
    n=-(-T//128)
    q=jnp.round(jnp.clip(table,-4.0,4.0)*FIX).astype(jnp.int32)
    q=jnp.pad(q,((0,0),(0,n*128-T)))
    q=q.reshape(NH//2,2,n,128)
    return (q[:,0]*65536)|(q[:,1]&65535)

def kernel_p(pos_ref,tab_ref,bias_ref):
    npair,n,_=tab_ref.shape
    WIN=bias_ref.shape[-1]
    tiles=-(-WIN//128)
    def row(r,_):
        r8=pl.multiple_of(r*8,8)
        for c in range(tiles):
            width=min(128,WIN-c*128)
            idx=pos_ref[pl.ds(r8,8),c*128:(c+1)*128]
            lo=idx&127; hi=idx>>7
            masks=[hi==k for k in range(n)]
            for p in range(npair):
                acc=jnp.zeros((8,128),jnp.int32)
                for k in range(n):
                    src=jnp.broadcast_to(tab_ref[p,k:k+1,:],(8,128))
                    acc=jnp.where(masks[k],jnp.take_along_axis(src,lo,axis=1),acc)
                a=(acc>>16).astype(F32)*(SQ/FIX)
                b=((acc<<16)>>16).astype(F32)*(SQ/FIX)
                bias_ref[2*p,pl.ds(r8,8),c*128:c*128+width]=a[:,:width]
                bias_ref[2*p+1,pl.ds(r8,8),c*128:c*128+width]=b[:,:width]
        return 0
    lax.fori_loop(0,bias_ref.shape[1]//8,row,0)

def call_p(posT_pad,tab,WIN):
    NH=tab.shape[0]*2
    return pl.pallas_call(kernel_p,out_shape=jax.ShapeDtypeStruct((NH,WIN,WIN),F32),
      compiler_params=pltpu.CompilerParams(vmem_limit_bytes=40*1024*1024),name="kernel_p")(posT_pad,tab)

def kernel_c(NH,G_ref,hi_ref,lo_ref,out_ref):
    WIN=hi_ref.shape[0]; LW=G_ref.shape[0]*128
    nh=out_ref.shape[0]//NH
    out_ref[...]=jnp.zeros_like(out_ref)
    def rows(r,_):
        r8=pl.multiple_of(r*8,8)
        hi8=hi_ref[pl.ds(r8,8),:]; lo8=lo_ref[pl.ds(r8,8),:]
        tot=jnp.zeros(out_ref.shape,F32)
        iota=lax.broadcasted_iota(jnp.int32,(256,LW),0).astype(F32).astype(BF)
        for k in range(8):
            g=jnp.concatenate([G_ref[c,pl.ds(r8+k,NH,stride=WIN),:] for c in range(LW//128)],axis=1)
            hr=hi8[k:k+1,:]; lr=lo8[k:k+1,:].astype(F32).astype(BF)
            A=jnp.concatenate([jnp.where(hr==m,g,0.0) for m in range(nh)],axis=0).astype(BF)
            oh=jnp.where(iota==lr,jnp.ones((),BF),jnp.zeros((),BF))
            tot=tot+lax.dot_general(A,oh,(((1,),(1,)),((),())),preferred_element_type=F32)
        out_ref[...]+=tot
        return 0
    lax.fori_loop(0,WIN//8,rows,0)

def call_c(G,posT,T,NH):
    WIN=posT.shape[0]; nt=G.shape[0]
    nh=-(-T//256)
    pp=jnp.pad(posT,((0,0),(0,nt*128-WIN)),constant_values=nh*256)
    hi=pp>>8; lo=pp&255
    o=pl.pallas_call(functools.partial(kernel_c,NH),out_shape=jax.ShapeDtypeStruct((nh*NH,256),F32),
      compiler_params=pltpu.CompilerParams(vmem_limit_bytes=40*1024*1024),name="kernel_c")(G,hi,lo)
    return o.reshape(nh,NH,256).transpose(1,0,2).reshape(NH,nh*256)[:,:T]


def gathered(piece,names,nseq,nheads):
    full=lax.all_gather(piece,names,axis=0,tiled=False)
    return full.reshape((nseq,nheads)+piece.shape)

def natural(block):
    s,h,r,c=block.shape
    return block.transpose(0,2,1,3).reshape(s*r,h*c)

def owners(grad,nseq,nheads):
    r,c=grad.shape
    return grad.reshape(nseq,r//nseq,nheads,c//nheads).transpose(0,2,1,3).reshape(nseq*nheads,r//nseq,c//nheads)

def from_next(rows):
    n=lax.axis_size("seq")
    return lax.ppermute(rows,"seq",[(i,(i-1)%n) for i in range(n)])

def to_next(rows):
    n=lax.axis_size("seq")
    return lax.ppermute(rows,"seq",[(i,(i+1)%n) for i in range(n)])

def spread(rows):
    n=lax.axis_size("heads")
    flat=rows.reshape(-1,rows.shape[-1])
    if n==2:
        other=lax.ppermute(flat,"heads",[(0,1),(1,0)])
        me=lax.axis_index("heads")
        return jnp.where(me==0,jnp.concatenate([flat,other]),jnp.concatenate([other,flat]))
    return lax.all_gather(flat,"heads",axis=0,tiled=True)

def place(rows,base,shift):
    full=spread(rows)
    keep=full.shape[0]-shift
    moved=jnp.concatenate([to_next(full[keep:]),full[:keep]])
    return base+moved.astype(F32)

def body(inputs,w_qkv,w_proj,w_fc1,w_fc2,gains,shifts,rel_table,region,pos_index,out_grad):
    nseq=lax.axis_size("seq"); nheads=lax.axis_size("heads"); me=lax.axis_index("heads")
    names=("seq","heads")
    tok,D=inputs.shape; WIN=pos_index.shape[0]; shift=WIN//2; T=rel_table.shape[1]
    nW=tok//WIN//nheads
    rows=w_qkv.shape[1]; cq=w_qkv.shape[2]; cf=w_fc1.shape[1]
    wcat=jnp.concatenate([w_qkv[0],w_qkv[1],w_qkv[2],w_proj.T,w_fc1,w_fc2.T],axis=1).astype(BF)
    table=lax.all_gather(rel_table,"heads",axis=0,tiled=True)
    NH=table.shape[0]
    full_w=gathered(wcat,names,nseq,nheads)
    cut=[natural(full_w[...,i*cq:(i+1)*cq]) for i in range(4)]
    wqkv=jnp.concatenate(cut[:3],axis=1); projT=cut[3]
    fc1=natural(full_w[...,4*cq:4*cq+cf]); fc2T=natural(full_w[...,4*cq+cf:])
    posT=pos_index.T
    wide=-(-WIN//128)*128
    bias=call_p(jnp.pad(posT,((0,0),(0,wide-WIN))),pack_table(table),WIN)
    start=me*nW*WIN
    def mine(v):
        ext=jnp.concatenate([v,from_next(v[:shift])])
        return lax.dynamic_slice_in_dim(ext,start+shift,nW*WIN,0).reshape(nW,WIN,-1)
    x=mine(inputs); og=mine(out_grad)
    lab=lax.dynamic_slice_in_dim(region,start,nW*WIN,0).reshape(nW,WIN)
    delta,gln2,qkv,g,gT,Dd,Pp,dfc1,dfc2T,dprojT,sm_a=call_a(x,og,lab[:,:,None],lab[:,None,:],bias,wqkv,projT,fc1,fc2T,gains,shifts)
    pieces=jnp.concatenate([owners(dprojT,nseq,nheads),owners(dfc1,nseq,nheads),owners(dfc2T,nseq,nheads)],axis=2)
    red_a=lax.psum_scatter(pieces,names,scatter_dimension=0,tiled=False).astype(F32)
    output=place(delta,inputs,shift)
    dd,dqkv,G,sm_b=call_b(x,gln2,qkv,g,gT,Dd,Pp,wqkv,gains,shifts)
    red_q=lax.psum_scatter(jnp.concatenate([owners(dqkv[:,c*D:(c+1)*D],nseq,nheads) for c in range(3)],axis=2),names,scatter_dimension=0,tiled=False).astype(F32)
    d_inputs=place(dd,out_grad,shift)
    tab=call_c(G,posT,T,NH)
    tab,small=lax.psum((tab,sm_a+sm_b),names)
    d_qkv=red_q.reshape(rows,3,cq).transpose(1,0,2)
    d_proj=red_a[:,:cq].T; d_fc1=red_a[:,cq:cq+cf]; d_fc2=red_a[:,cq+cf:].T
    nl=rel_table.shape[0]
    d_table=lax.dynamic_slice_in_dim(tab,me*nl,nl,0)
    return (output,d_inputs,d_qkv,d_proj,d_fc1,d_fc2,small[0:2],small[2:6],d_table)

def solution(mesh):
    placed=(P("seq",None),P(None,"seq","heads"),P("heads","seq"),P("seq","heads"),P("heads","seq"),P(),P(),P("heads",None),P("seq"),P(),P("seq",None))
    return jax.shard_map(body,mesh=mesh,in_specs=placed,
        out_specs=(P("seq",None),P("seq",None),P(None,"seq","heads"),P("heads","seq"),P("seq","heads"),P("heads","seq"),P(),P(),P("heads",None)),
        check_vma=False)
```

time: 1680 us -> 644 us (0.38)
  waiting for transfers between devices: 760 us -> 192 us
  matrix products: 410 us -> 0 us
  Pallas kernels: 0 us -> 220 us
  other arithmetic: 222 us -> 32.7 us
  local copies, waits for them, and re-layouts: 153 us -> 63.7 us
    psum x3 -> x1, waiting for transfers between devices: 602 us -> 0.01 us  [body(): tab, small = lax.psum((tab, sm_a + sm_b), names)]
    dot_general x26 -> x0, matrix products: 410 us -> none  [the longest x4 100 us: lookup_block(): jnp.einsum('pl,hol->pho', inner_hot, table_three, precision=highest)]
    pallas_call x0 -> x4, Pallas kernels: none -> 220 us  [the longest x1 89.4 us: call_a(): pl.pallas_call(functools.partial(kernel_a, NH), grid=(nW,), in_specs=[per...]
    reduce_sum x16 -> x0, other arithmetic: 120 us -> none  [the longest x1 47.7 us: attend_back(): jnp.sum(g_scores.astype(jnp.float32), axis=0).reshape(heads_here, WIN * WIN)]
    reduce_scatter x3 -> x2, waiting for transfers between devices: 93.3 us -> 189 us  [the longest x1 110 us: body(): lax.psum_scatter(pieces, names, scatter_dimension=0, tiled=False)]
    unnamed x10 -> x4, waiting for transfers between devices: 55.4 us -> 0.07 us
    psum x1, blocking collectives: 62 us -> 103 us  [body(): tab, small = lax.psum((tab, sm_a + sm_b), names)]
    dot_general x4 -> x0, other arithmetic: 36.9 us -> none  [scatter_block(): return jnp.einsum('hpo,pl->hol', weighted, inner_hot, precision=highest)]
  transfers between devices with their start and end apart: 13 -> 10, of which waited for: 8 -> 5; matrix products, arithmetic and copies ran while one was open for 16% -> 8% of each run, Pallas kernels for 0% -> 6%
where the time goes in v1:
time: 644 us; the launch traced here: 643 us
  Pallas kernels  220 us (34%)
  waiting for transfers between devices  192 us (30%)
  blocking collectives  109 us (17%)
  local copies, waits for them, and re-layouts  63.7 us (10%)
  other arithmetic  32.7 us (5%)
  between operations  14.2 us (2%)
  starting transfers between devices  11.2 us (2%)
    reduce_scatter x1, waiting for transfers between devices, body(): lax.psum_scatter(pieces, names, scatter_dimension=0, tiled=False)  110 us
    psum x1, blocking collectives, body(): tab, small = lax.psum((tab, sm_a + sm_b), names)  103 us
    pallas_call x1, Pallas kernels, call_a(): pl.pallas_call(functools.partial(kernel_a, NH), grid=(nW,), in_specs=[per...  89.4 us
    reduce_scatter x1, waiting for transfers between devices, body(): lax.psum_scatter(jnp.concatenate([owners(dqkv[:, c * D:(c + 1) * D], nseq...  78.8 us
    pallas_call x1, Pallas kernels, call_b(): pl.pallas_call(functools.partial(kernel_b, NH), grid=(nW,), in_specs=[per...  51.1 us
    pallas_call x1, Pallas kernels, call_c(): pl.pallas_call(functools.partial(kernel_c, NH), out_shape=jax.ShapeDtypeS...  41.7 us
    pallas_call x1, Pallas kernels, call_p(): pl.pallas_call(kernel_p, out_shape=jax.ShapeDtypeStruct((NH, WIN, WIN), F...  37.4 us
    unnamed x58, local copies, waits for them, and re-layouts  31.2 us
  transfers between devices with their start and end apart: 10, of which 5 were waited for; matrix products, arithmetic and copies ran while one was open for 8% of the time, Pallas kernels for 6%

profile of v1, /device:TPU:0, one launch (start us, length us, event | category | flops | bytes accessed | tf_op | source)
XLA Modules:
  0.0 642.7 jit_solution(12424145576850621729)
XLA Ops:
  7.2 0.9 convert.25
  8.2 0.8 constant_dynamic-update-slice_fusion
  8.9 0.9 bitcast_dynamic-update-slice_fusion.1
  9.8 0.9 bitcast_dynamic-update-slice_fusion
  10.8 0.7 copy-done.8
  11.5 1.0 slice.81
  12.5 5.5 collective-permute-start
  18.0 1.0 slice.82
  19.0 0.7 collective-permute-start.1
  19.8 2.3 copy.49
  22.1 6.3 all_gather.7
  28.5 1.8 pad_and_fusion
  30.3 1.6 broadcast_in_dim_reshape.8.labc_ref
  31.9 0.7 broadcast_in_dim_reshape.7.labr_ref
  32.6 37.4 %kernel_p.1.bias_ref = f32[16,392,392]{2,1,0:T(8,128)S(1)} custom-call(s32[392,512]{1,0:T(8,128)S(1)} %get-tuple-element.68.pos_ref, s32[8,20,128]{2,1,0:T(8,128)S(1)} %fusion.4.tab_ref), custom_call_target="tpu_custom_call" | custom-call | tf_op jit(solution)/shard_map/kernel_p/pallas_call | solution.py:263
  70.0 4.7 copy-done
  74.7 4.9 fusion.1
  79.6 3.0 fusion
  82.6 1.7 all-gather.2.cloned.1.call-done
  84.3 1.7 fusion.7
  86.1 2.7 fusion.6
  89.4 1.0 constant_dynamic-update-slice_fusion.6
  92.2 0.9 copy.78
  93.1 2.2 copy.73
  95.2 1.9 copy.79
  97.1 2.2 copy.74
  99.3 1.9 copy.80
  101.2 0.9 constant_dynamic-update-slice_fusion.5
  102.1 0.8 constant_dynamic-update-slice_fusion.4.wqkv_ref
  102.9 89.4 %kernel_a.1 = (bf16[4,392,512]{2,1,0:T(8,128)(2,1)}, f32[4,392,512]{2,1,0:T(8,128)}, bf16[4,3,392,512]{3,2,1,0:T(8,128)(2,1)}, bf16[4,392,512]{2,1,0:T(8,128)(2,...) custom-call(f32[4,392,512]{2,1,0:T(8,128)} %bitcast.87, ...), custom_call_target="tpu_custom_call" | custom-call | tf_op jit(solution)/shard_map/kernel_a/pallas_call | solution.py:150
  192.3 51.1 %kernel_b.1 = (bf16[4,392,512]{2,1,0:T(8,128)(2,1)}, bf16[512,1536]{1,0:T(8,128)(2,1)}, f32[4,6272,128]{2,1,0:T(8,128)}, f32[8,512]{1,0:T(8,128)}) custom-call(f32[4,392,512]{2,1,0:T(8,128)} %bitcast.88, f32[4,392,512]{2,1,0:T(8,128)} %get-tuple-element.25.gln2_ref, bf16[4,3,392,512]{3,2,1,0:T(8,128)(2,1)} %get-tuple-element.26.qkv_ref, ...), custom_call_target="tpu_custom_call" | custom-call | tf_op jit(solution)/shard_map/kernel_b/pallas_call | solution.py:219
  243.4 2.4 fusion.8
  246.1 1.2 reshape.199
  247.3 0.9 copy.60
  248.2 1.2 reshape.201
  249.3 0.9 copy.61
  250.2 4.6 copy-done.1
  254.9 41.7 %kernel_c.1 = f32[160,256]{1,0:T(8,128)S(1)} custom-call(f32[4,6272,128]{2,1,0:T(8,128)S(1)} %copy-done.1, s32[392,512]{1,0:T(8,128)S(1)} %get-tuple-element.67.hi_ref, s32[392,512]{1,0:T(8,128)S(1)} %get-tuple-element.66.lo_ref), custom_call_target="tpu_custom_call" | custom-call | tf_op jit(solution)/shard_map/kernel_c/pallas_call | solution.py:290
  296.6 0.7 copy.81
  297.4 2.4 pad_maximum_fusion.1
  299.8 3.3 reshape.205
  303.1 2.0 copy.63
  305.1 3.4 reshape.207
  308.4 2.0 copy.64
  310.7 1.4 copy-done.3
  312.0 3.6 pad_maximum_fusion
  315.6 1.4 copy-done.6
  317.0 1.5 collective-permute-start.4
  319.1 103.0 %psum.14 = f32[8,512]{1,0:T(8,128)S(1)} all-reduce(f32[8,512]{1,0:T(8,128)S(1)} %add.44), channel_id=1, replica_groups=mesh['seq'=16,'heads'=2] {'seq','heads'}, use_global_device_ids=true, to_apply=%region_2.3 | all-reduce | flops 4096 | bytes 32768 | tf_op jit(solution)/shard_map/psum | solution.py:360
  423.3 1.5 constant_dynamic-slice_fusion
  424.8 2.4 maximum_select_fusion.1
  427.4 2.5 maximum_select_fusion
  430.1 1.4 copy-done.2
  431.6 2.7 collective-permute-start.3
  434.3 0.9 collective-permute-done.5
  435.2 3.9 convert_add_fusion
  439.1 0.8 collective-permute-done.3
  439.9 3.9 convert_add_fusion.1
  443.7 78.8 %reduce-scatter.3.cloned.1.call-done = bf16[1,32,768]{2,1,0:T(8,128)(2,1)} async-done(((bf16[32,32,768]{2,1,0:T(8,128)(2,1)}), bf16[1,32,768]{2,1,0:T(8,128)(2,1)}) %reduce-scatter.3.cloned.1.call-update) | async-done | bytes 49168 | tf_op jit(solution)/shard_map/reduce_scatter | solution.py:357
  522.5 0.8 reshape.212
  523.4 0.7 copy.66
  524.1 109.8 %reduce-scatter.5.cloned.1.call-done = bf16[1,32,2304]{2,1,0:T(8,128)(2,1)} async-done(((bf16[32,32,2304]{2,1,0:T(8,128)(2,1)}), bf16[1,32,2304]{2,1,0:T(8,128)(2,1)}) %reduce-scatter.5.cloned.1.call-update) | async-done | bytes 147472 | tf_op jit(solution)/shard_map/reduce_scatter | solution.py:354
  633.9 0.9 bitcast_convert_fusion
  634.8 0.7 slice_bitcast_fusion
  (78 shorter events, 6.1 us)
Async XLA Ops:
  7.2 14.9 %copy-start.9 = (f32[8,2535]{1,0:T(8,128)S(1)}, f32[8,2535]{1,0:T(8,128)}, u32[]{:S(2)}) copy-start(f32[8,2535]{1,0:T(8,128)} %param.18) | copy-start | bytes 243364
  7.2 77.2 %all-gather.2.cloned.1.call-start = ((), (), s32[]{:S(2)}) async-start(), calls=%async_computation.2 | async-start | bytes 6488064 | tf_op jit(solution)/shard_map/all_gather | solution.py:296
  10.8 0.7 copy-start.8
  11.4 411.8 %all-reduce.5.cloned.1.call-start = ((), (), s32[]{:S(2)}) async-start(), calls=%async_computation.5 | async-start | bytes 327680 | tf_op jit(solution)/shard_map/psum | solution.py:360
  12.5 62.1 %collective-permute-start = (f32[196,512]{1,0:T(8,128)S(1)}, f32[196,512]{1,0:T(8,128)}, u32[]{:S(2)}, u32[]{:S(2)}) collective-permute-start(f32[196,512]{1,0:T(8,128)S(1)} %slice.81), channel_id=1, source_target_pairs={{0,30},{2,0},{4,2},{6,4},{8,6},{10,8},{12,10},{14,12},{16,14},{18,... | collective-permute-start | bytes 1204232 | tf_op jit(solution)/shard_map/ppermute | solution.py:309
  19.0 11.2 %copy-start.12 = (s32[3136]{0:T(1024)S(1)}, s32[3136]{0:T(1024)}, u32[]{:S(2)}) copy-start(s32[3136]{0:T(1024)} %param.19) | copy-start | bytes 37636
  19.0 60.5 %collective-permute-start.1 = (f32[196,512]{1,0:T(8,128)S(1)}, f32[196,512]{1,0:T(8,128)}, u32[]{:S(2)}, u32[]{:S(2)}) collective-permute-start(f32[196,512]{1,0:T(8,128)S(1)} %slice.82), channel_id=1, source_target_pairs={{0,30},{2,0},{4,2},{6,4},{8,6},{10,8},{12,10},{14,12},{16,14},{18,... | collective-permute-start | bytes 1204232 | tf_op jit(solution)/shard_map/ppermute | solution.py:309
  32.6 47.0 %slice-start = ((s8[6422528]{0:T(1024)(128)(4,1)}), s8[4194304]{0:T(1024)(128)(4,1)S(1)}, s32[]{:S(2)}) async-start(s8[6422528]{0:T(1024)(128)(4,1)} %bitcast.89), calls=%async_computation.6 | async-start | bytes 8388608
  32.6 47.0 %slice-start.1 = ((s8[6422528]{0:T(1024)(128)(4,1)}), s8[2228224]{0:T(1024)(128)(4,1)S(1)}, s32[]{:S(2)}) async-start(s8[6422528]{0:T(1024)(128)(4,1)} %bitcast.89), calls=%async_computation.7 | async-start | bytes 4456448
  70.0 4.7 copy-start
  250.2 4.7 copy-start.1
  254.9 42.5 %copy-start.4 = (bf16[16,32,2,256]{3,1,2,0:T(8,128)(2,1)S(1)}, bf16[16,32,2,256]{3,1,2,0:T(8,128)(2,1)}, u32[]{:S(2)}) copy-start(bf16[16,32,2,256]{3,1,2,0:T(8,128)(2,1)} %copy.60) | copy-start | bytes 1572868
  297.3 225.3 %reduce-scatter.3.cloned.1.call-start = ((), (), s32[]{:S(2)}) async-start(), calls=%async_computation.3 | async-start | bytes 1622016 | tf_op jit(solution)/shard_map/reduce_scatter | solution.py:357
  299.7 334.2 %reduce-scatter.5.cloned.1.call-start = ((), (), s32[]{:S(2)}) async-start(), calls=%async_computation.4 | async-start | bytes 4866048 | tf_op jit(solution)/shard_map/reduce_scatter | solution.py:354
  305.1 5.4 copy-start.7
  310.4 1.6 copy-start.3
  315.6 1.4 copy-start.6
  315.6 2.9 copy-start.5
  315.6 3.5 copy-start.10
  315.6 3.5 copy-start.11
  317.0 107.8 %collective-permute-start.4 = (bf16[1568,512]{1,0:T(8,128)(2,1)S(1)}, bf16[1568,512]{1,0:T(8,128)(2,1)}, u32[]{:S(2)}, u32[]{:S(2)}) collective-permute-start(bf16[1568,512]{1,0:T(8,128)(2,1)S(1)} %bitcast.122), channel_id=1, source_target_pairs={{0,1},{1,0},{2,3},{3,2},{4,5},{5,4},{6,7},{7,6},{8,9},{9,8},{10,11... | collective-permute-start | bytes 4816904 | tf_op jit(solution)/shard_map/ppermute | solution.py:319
  318.5 108.9 %collective-permute-start.2 = (bf16[1568,512]{1,0:T(8,128)(2,1)S(1)}, bf16[1568,512]{1,0:T(8,128)(2,1)}, u32[]{:S(2)}, u32[]{:S(2)}) collective-permute-start(bf16[1568,512]{1,0:T(8,128)(2,1)S(1)} %bitcast.120), channel_id=1, source_target_pairs={{0,1},{1,0},{2,3},{3,2},{4,5},{5,4},{6,7},{7,6},{8,9},{9,8},{10,11... | collective-permute-start | bytes 4816904 | tf_op jit(solution)/shard_map/ppermute | solution.py:319
  427.3 7.9 %collective-permute-start.5 = (bf16[196,512]{1,0:T(8,128)(2,1)S(1)}, bf16[196,512]{1,0:T(8,128)(2,1)S(1)}, u32[]{:S(2)}, u32[]{:S(2)}) collective-permute-start(bf16[196,512]{1,0:T(8,128)(2,1)S(1)} %slice.120), channel_id=1, source_target_pairs={{0,2},{2,4},{4,6},{6,8},{8,10},{10,12},{12,14},{14,16},{16,18},{18... | collective-permute-start | bytes 602120 | tf_op jit(solution)/shard_map/ppermute | solution.py:313
  427.4 7.9 %slice-start.2 = ((s8[6422528]{0:T(1024)(128)(4,1)}), s8[4194304]{0:T(1024)(128)(4,1)S(1)}, s32[]{:S(2)}) async-start(s8[6422528]{0:T(1024)(128)(4,1)} %bitcast.91), calls=%async_computation.8 | async-start | bytes 8388608
  429.8 1.7 copy-start.2
  429.9 5.4 slice-start.3
  430.1 9.8 %slice-start.4 = ((s8[6422528]{0:T(1024)(128)(4,1)}), s8[4194304]{0:T(1024)(128)(4,1)S(1)}, s32[]{:S(2)}) async-start(s8[6422528]{0:T(1024)(128)(4,1)} %bitcast.93), calls=%async_computation.10 | async-start | bytes 8388608
  431.6 8.3 %slice-start.5 = ((s8[6422528]{0:T(1024)(128)(4,1)}), s8[2228224]{0:T(1024)(128)(4,1)S(1)}, s32[]{:S(2)}) async-start(s8[6422528]{0:T(1024)(128)(4,1)} %bitcast.93), calls=%async_computation.11 | async-start | bytes 4456448
  431.6 8.3 %slice-start.6 = ((bf16[3136,512]{1,0:T(8,128)(2,1)}), bf16[2940,512]{1,0:T(8,128)(2,1)S(1)}, s32[]{:S(2)}) async-start(bf16[3136,512]{1,0:T(8,128)(2,1)} %copy-done.2), calls=%async_computation.12 | async-start | bytes 6029312 | tf_op jit(solution)/shard_map/slice | solution.py:327
  431.6 8.2 %collective-permute-start.3 = (bf16[196,512]{1,0:T(8,128)(2,1)S(1)}, bf16[196,512]{1,0:T(8,128)(2,1)S(1)}, u32[]{:S(2)}, u32[]{:S(2)}) collective-permute-start(bf16[196,512]{1,0:T(8,128)(2,1)S(1)} %slice.118), channel_id=1, source_target_pairs={{0,2},{2,4},{4,6},{6,8},{8,10},{10,12},{12,14},{14,16},{16,18},{18... | collective-permute-start | bytes 602120 | tf_op jit(solution)/shard_map/ppermute | solution.py:313
Sparse Core Ops, SparseCore 0:
  11.6 72.7 all-gather.1
  297.4 120.7 all-reduce.4
  423.4 99.0 reduce-scatter.2
  527.9 105.9 reduce-scatter.4

commit v2 on v1

v2 whole, which is shorter than its diff:
```python
import functools
import math

import jax, jax.numpy as jnp
from jax import lax
from jax.experimental import pallas as pl
from jax.experimental.pallas import tpu as pltpu
from jax.sharding import PartitionSpec as P

BF=jnp.bfloat16; F32=jnp.float32
HD=32; GROUP=128; PER=4
EPS=1e-5
SQ=math.sqrt(32.0)
CEXP=math.log2(math.e)/SQ
MASK=100.0*SQ

def mm(a,b):
    return lax.dot_general(a,b,(((1,),(0,)),((),())),preferred_element_type=F32)
def mm_nt(a,b):
    return lax.dot_general(a,b,(((1,),(1,)),((),())),preferred_element_type=F32)

def norm_stats(v):
    mean=jnp.mean(v,axis=-1,keepdims=True)
    c=v-mean
    var=jnp.mean(c*c,axis=-1,keepdims=True)
    rstd=lax.rsqrt(var+EPS)
    return c*rstd, rstd

def norm_back(gy,xhat,rstd,gain):
    gx=gy*gain
    m1=jnp.mean(gx,axis=-1,keepdims=True)
    m2=jnp.mean(gx*xhat,axis=-1,keepdims=True)
    return rstd*(gx-m1-xhat*m2)

P0=0.3275911
A1,A2,A3,A4,A5=0.254829592,-0.284496736,1.421413741,-1.453152027,1.061405429
def gelu_both(x):
    e=jnp.exp2(x*x*(-0.5*math.log2(math.e)))
    t=1.0/(1.0+(P0/math.sqrt(2.0))*jnp.abs(x))
    poly=t*(0.5*A1+t*(0.5*A2+t*(0.5*A3+t*(0.5*A4+t*(0.5*A5)))))
    half=poly*e
    phi=jnp.where(x>=0,1.0-half,half)
    return x*phi, phi+x*e*(1.0/math.sqrt(2.0*math.pi))

def kernel_a(nheads,x_ref,og_ref,labc_ref,labr_ref,bias_ref,W_ref,gains_ref,shifts_ref,
             delta_ref,gln2_ref,qkv_ref,g_ref,gT_ref,D_ref,P_hbm,dcat_ref,small_ref,
             qT_s,vT_s,OT_s,P_s,acc,sem,xn2_s,xn2T_s,tg_s,tgT_s,up_s,gn2_s):
    w=pl.program_id(0); nw=pl.num_programs(0)
    D=x_ref.shape[-1]; WIN=x_ref.shape[-2]
    parts=W_ref.shape[0]; cq=D//parts; cf=(W_ref.shape[2]-4*cq)//2
    groups=nheads//PER
    x=x_ref[0]
    xhat,_=norm_stats(x)
    xn=(xhat*gains_ref[0:1,:]+shifts_ref[0:1,:]).astype(BF)
    for c in range(3):
        for m in range(parts):
            at=slice(m*cq,(m+1)*cq)
            y=mm(xn,W_ref[m,:,c*cq:(c+1)*cq]).astype(BF)
            qkv_ref[0,c,:,at]=y
            if c==0: qT_s[at,:]=y.T
            if c==2: vT_s[at,:]=y.T
    labc=labc_ref[0]; labr=labr_ref[0]
    lane=lax.broadcasted_iota(jnp.int32,(WIN,GROUP),1)
    oh=jnp.where((labc==lane)|((labc+3)==lane),1.0,0.0).astype(BF)
    hi=564.0
    lo=MASK-hi
    sub=lax.broadcasted_iota(jnp.int32,(GROUP,WIN),0)
    nm=jnp.where(sub<3,jnp.where(sub!=labr,-hi,0.0),jnp.where(sub<6,jnp.where(sub-3!=labr,-lo,0.0),0.0)).astype(BF)
    hl=lane//HD

    def group(gi,_):
        slot=gi%2
        step=w*groups+gi
        @pl.when(step>=2)
        def _():
            pltpu.make_async_copy(P_s.at[slot],P_hbm.at[0,pl.ds(0,PER)],sem.at[slot]).wait()
        o=pl.multiple_of(gi*GROUP,GROUP)
        qTg=jnp.concatenate([qT_s[pl.ds(o,GROUP),:],nm],axis=0)
        kg=qkv_ref[0,1,:,pl.ds(o,GROUP)]
        for hh in range(PER):
            kh=jnp.concatenate([jnp.where(hl==hh,kg,jnp.zeros_like(kg)),oh],axis=1)
            t=mm(kh,qTg)+bias_ref[gi*PER+hh]
            m=jnp.max(t,axis=0,keepdims=True)
            e=jnp.exp2((t-m)*CEXP)
            l=jnp.sum(e,axis=0,keepdims=True)
            p=(e*(1.0/l)).astype(BF)
            P_s[slot,hh]=p
            OT_s[pl.ds(o+hh*HD,HD),:]=mm(vT_s[pl.ds(o+hh*HD,HD),:],p)
        pltpu.make_async_copy(P_s.at[slot],P_hbm.at[w,pl.ds(gi*PER,PER)],sem.at[slot]).start()
        return 0
    lax.fori_loop(0,groups,group,0)

    attn=OT_s[...].astype(BF).T
    branch=shifts_ref[2:3,:]
    for m in range(parts):
        branch=branch+mm_nt(attn[:,m*cq:(m+1)*cq],W_ref[m,:,3*cq:4*cq])
    branch=branch.astype(BF).astype(F32)
    middle=x+branch
    xhat2,rstd2=norm_stats(middle)
    xn2=(xhat2*gains_ref[1:2,:]+shifts_ref[1:2,:]).astype(BF)
    og=og_ref[0]
    tg=og.astype(BF)
    xn2_s[...]=xn2; xn2T_s[...]=xn2.T; tg_s[...]=tg; tgT_s[...]=tg.T
    up_s[...]=jnp.zeros_like(up_s); gn2_s[...]=jnp.zeros_like(gn2_s)
    CH=min(512,cf); each=cf//CH
    @pl.when(w==0)
    def _():
        acc[...]=jnp.zeros_like(acc)
        small_ref[...]=jnp.zeros_like(small_ref)
    def chunk(c,_):
        m=c//each
        o=pl.multiple_of((c%each)*CH,CH)
        f1=W_ref[m,:,pl.ds(4*cq+o,CH)]; f2=W_ref[m,:,pl.ds(4*cq+cf+o,CH)]
        hid=mm(xn2_s[...],f1)
        act,dact=gelu_both(hid)
        a=act.astype(BF)
        up_s[...]+=mm_nt(a,f2)
        gh=(mm(tg_s[...],f2)*dact).astype(BF)
        gn2_s[...]+=mm_nt(gh,f1)
        acc[m,:,pl.ds(cq+o,CH)]+=mm(xn2T_s[...],gh)
        acc[m,:,pl.ds(cq+cf+o,CH)]+=mm(tgT_s[...],a)
        return 0
    lax.fori_loop(0,parts*each,chunk,0)
    delta_ref[0]=(branch+up_s[...]+shifts_ref[3:4,:]).astype(BF)
    gn2=gn2_s[...]
    gln2=norm_back(gn2,xhat2,rstd2,gains_ref[1:2,:])
    gln2_ref[0]=gln2
    gb=(og+gln2).astype(BF)
    gbT=gb.T
    for m in range(parts):
        at=slice(m*cq,(m+1)*cq)
        acc[m,:,0:cq]+=mm(gbT,attn[:,at])
        g=mm(gb,W_ref[m,:,3*cq:4*cq]).astype(BF)
        g_ref[0,:,at]=g
        gT=g.T
        gT_ref[0,at,:]=gT
        prod=gT.astype(F32)*OT_s[at,:]
        nh=nheads//parts
        D_ref[0,m*nh:(m+1)*nh,:]=jnp.sum(prod.reshape(nh,HD,WIN),axis=1)
    small_ref[1:2,:]+=jnp.sum(gn2*xhat2,axis=0,keepdims=True)
    small_ref[3:4,:]+=jnp.sum(gn2,axis=0,keepdims=True)
    small_ref[4:5,:]+=jnp.sum(gb.astype(F32),axis=0,keepdims=True)
    small_ref[5:6,:]+=jnp.sum(tg.astype(F32),axis=0,keepdims=True)
    @pl.when(w==nw-1)
    def _():
        dcat_ref[...]=acc[...].astype(BF)
        for s in range(2):
            pltpu.make_async_copy(P_s.at[s],P_hbm.at[0,pl.ds(0,PER)],sem.at[s]).wait()

def full(shape,**kw):
    return pl.BlockSpec(shape,lambda w:(0,)*len(shape),**kw)
def per(shape):
    return pl.BlockSpec((1,)+shape,lambda w:(w,)+(0,)*len(shape))
ONE=pl.Buffered(1)
ANY=pl.BlockSpec(memory_space=pl.ANY)

def call_a(x,og,labc,labr,bias,W,gains,shifts):
    nW,WIN,D=x.shape; NH=bias.shape[0]
    parts,_,Ct=W.shape; Cg=Ct-3*(D//parts)
    sd=jax.ShapeDtypeStruct
    outs=[sd((nW,WIN,D),BF),sd((nW,WIN,D),F32),sd((nW,3,WIN,D),BF),sd((nW,WIN,D),BF),sd((nW,D,WIN),BF),sd((nW,NH,WIN),F32),
          sd((nW,NH,WIN,WIN),BF),sd((parts,D,Cg),BF),sd((8,D),F32)]
    return pl.pallas_call(functools.partial(kernel_a,NH),grid=(nW,),
      in_specs=[per((WIN,D)),per((WIN,D)),per((WIN,1)),per((1,WIN)),full((NH,WIN,WIN),pipeline_mode=ONE),
        full((parts,D,Ct),pipeline_mode=ONE),full(gains.shape),full(shifts.shape)],
      out_specs=[per((WIN,D)),per((WIN,D)),per((3,WIN,D)),per((WIN,D)),per((D,WIN)),per((NH,WIN)),ANY,full((parts,D,Cg)),full((8,D))],
      out_shape=outs,
      scratch_shapes=[pltpu.VMEM((D,WIN),BF),pltpu.VMEM((D,WIN),BF),pltpu.VMEM((D,WIN),F32),pltpu.VMEM((2,PER,WIN,WIN),BF),
        pltpu.VMEM((parts,D,Cg),F32),pltpu.SemaphoreType.DMA((2,)),
        pltpu.VMEM((WIN,D),BF),pltpu.VMEM((D,WIN),BF),pltpu.VMEM((WIN,D),BF),pltpu.VMEM((D,WIN),BF),pltpu.VMEM((WIN,D),F32),pltpu.VMEM((WIN,D),F32)],
      compiler_params=pltpu.CompilerParams(vmem_limit_bytes=62*1024*1024,dimension_semantics=("arbitrary",)),
      name="kernel_a")(x,og,labc,labr,bias,W,gains,shifts)

def kernel_b(nheads,linked,x_ref,gln2_ref,qkv_ref,g_ref,gT_ref,D_ref,P_ref,W_ref,gains_ref,shifts_ref,delta_hbm,dcat_hbm,
             dd_hbm,dqkv_ref,G_hbm,small_ref,od_hbm,odd_hbm,mid_hbm,
             G_s,aq,kT_s,gq_s,gqT_s,sem,dd_s,dl,ds,dr,*red_scratch):
    w=pl.program_id(0); nw=pl.num_programs(0)
    D=x_ref.shape[-1]; WIN=x_ref.shape[-2]
    parts=W_ref.shape[0]; cq=D//parts
    groups=nheads//PER
    if linked:
        z,xx,cc,yy=place_of()
        mate=dev(z,xx,cc,1-yy)
        red=Reduce(dcat_hbm,None,*red_scratch)
        give=send(delta_hbm,od_hbm,ds.at[nw_of(delta_hbm)],dr.at[nw_of(delta_hbm)],mate)
        @pl.when(w==0)
        def _():
            greet(peers_of(z,xx,cc,yy))
            red.start()
            give.start()
    @pl.when(w==0)
    def _():
        aq[...]=jnp.zeros_like(aq); G_s[...]=jnp.zeros_like(G_s); small_ref[...]=jnp.zeros_like(small_ref)
    kT_s[...]=qkv_ref[0,1].T
    lane=lax.broadcasted_iota(jnp.int32,(WIN,GROUP),1)
    hl=lane//HD
    def group(gi,_):
        o=pl.multiple_of(gi*GROUP,GROUP)
        gTg=gT_ref[0,pl.ds(o,GROUP),:]
        vg=qkv_ref[0,2,:,pl.ds(o,GROUP)]
        qg=qkv_ref[0,0,:,pl.ds(o,GROUP)]
        gg=g_ref[0,:,pl.ds(o,GROUP)]
        dv=jnp.zeros((WIN,GROUP),F32); dk=jnp.zeros((WIN,GROUP),F32)
        zero=jnp.zeros_like(vg)
        for hh in range(PER):
            h=gi*PER+hh
            p=P_ref[0,h]
            dp=mm(jnp.where(hl==hh,vg,zero),gTg)
            ds_=p.astype(F32)*(dp-D_ref[0,pl.ds(h,1),:])
            for c in range(G_s.shape[0]):
                wd=min(128,WIN-c*128)
                G_s[c,pl.ds(pl.multiple_of(h*WIN,8),WIN),:wd]+=ds_[:,c*128:c*128+wd]
            dsl=ds_.astype(BF)
            dv+=mm(p,jnp.where(hl==hh,gg,zero))
            dk+=mm(dsl,jnp.where(hl==hh,qg,zero))
            gqT_s[pl.ds(o+hh*HD,HD),:]=mm(kT_s[pl.ds(o+hh*HD,HD),:],dsl)
        gq_s[1,:,pl.ds(o,GROUP)]=(dk*(1.0/SQ)).astype(BF)
        gq_s[2,:,pl.ds(o,GROUP)]=dv.astype(BF)
        return 0
    lax.fori_loop(0,groups,group,0)
    gq_s[0]=(gqT_s[...]*(1.0/SQ)).astype(BF).T
    x=x_ref[0]
    xhat,rstd=norm_stats(x)
    xn=(xhat*gains_ref[0:1,:]+shifts_ref[0:1,:]).astype(BF)
    xnT=xn.T
    gr=jnp.zeros((WIN,D),F32)
    for m in range(parts):
        for c in range(3):
            gc=gq_s[c,:,m*cq:(m+1)*cq]
            gr=gr+mm_nt(gc,W_ref[m,:,c*cq:(c+1)*cq])
            aq[m,:,c*cq:(c+1)*cq]+=mm(xnT,gc)
    dd_s[w]=(gln2_ref[0]+norm_back(gr,xhat,rstd,gains_ref[0:1,:])).astype(BF)
    keep=pltpu.make_async_copy(dd_s.at[w],dd_hbm.at[w],dl.at[w]); keep.start()
    if linked:
        send(dd_s.at[w],odd_hbm.at[w],ds.at[w],dr.at[w],mate).start()
        pl.when(w==0)(red.one)
    small_ref[0:1,:]+=jnp.sum(gr*xhat,axis=0,keepdims=True)
    small_ref[2:3,:]+=jnp.sum(gr,axis=0,keepdims=True)
    @pl.when(w==nw-1)
    def _():
        dqkv_ref[...]=aq[...].astype(BF)
        cp=pltpu.make_async_copy(G_s,G_hbm,sem.at[0]); cp.start()
        if linked:
            red.half(mid_hbm,sem.at[1])
        for k in range(nw_of(dd_s)):
            pltpu.make_async_copy(dd_s.at[k],dd_hbm.at[k],dl.at[k]).wait()
            if linked:
                send(dd_s.at[k],odd_hbm.at[k],ds.at[k],dr.at[k],mate).wait()
        if linked:
            give.wait()
        cp.wait()

def nw_of(ref):
    return ref.shape[0]

def call_b(linked,x,gln2,qkv,g,gT,Dd,Pp,W,gains,shifts,delta,dcat):
    nW,WIN,D=x.shape; NH=Dd.shape[1]
    parts=W.shape[0]; cq=D//parts; tiles=-(-WIN//128)
    sd=jax.ShapeDtypeStruct; dma=pltpu.SemaphoreType.DMA
    rows,cols=dcat.shape[-2:]
    row=sd((nW,WIN,D),BF) if linked else sd((8,128),BF)
    mid=sd((4,2,rows,cols),BF) if linked else sd((8,128),BF)
    return pl.pallas_call(functools.partial(kernel_b,NH,linked),grid=(nW,),
      in_specs=[per((WIN,D)),per((WIN,D)),per((3,WIN,D)),per((WIN,D)),per((D,WIN)),per((NH,WIN)),per((NH,WIN,WIN)),
        full((parts,D,3*cq),pipeline_mode=ONE),full(gains.shape),full(shifts.shape),ANY,ANY],
      out_specs=[ANY,full((parts,D,3*cq)),ANY,full((8,D)),ANY,ANY,ANY],
      out_shape=[sd((nW,WIN,D),BF),sd((parts,D,3*cq),BF),sd((tiles,NH*WIN,128),F32),sd((8,D),F32),row,row,mid],
      scratch_shapes=[pltpu.VMEM((tiles,NH*WIN,128),F32),pltpu.VMEM((parts,D,3*cq),F32),pltpu.VMEM((D,WIN),BF),pltpu.VMEM((3,WIN,D),BF),pltpu.VMEM((D,WIN),F32),
        dma((2,)),pltpu.VMEM((nW,WIN,D),BF),dma((nW,)),dma((nW+1,)),dma((nW+1,))]+(reduce_scratch(rows,cols,False) if linked else []),
      compiler_params=pltpu.CompilerParams(vmem_limit_bytes=62*1024*1024,dimension_semantics=("arbitrary",),**(dict(collective_id=2,has_side_effects=True) if linked else {})),
      name="kernel_b")(x,gln2,qkv,g,gT,Dd,Pp,W,gains,shifts,delta,dcat)

FIX=8191.0

def pack_table(table):
    NH,T=table.shape
    n=-(-T//128)
    q=jnp.round(jnp.clip(table,-4.0,4.0)*FIX).astype(jnp.int32)
    q=jnp.pad(q,((0,0),(0,n*128-T)))
    q=q.reshape(NH//2,2,n,128)
    return (q[:,0]*65536)|(q[:,1]&65535)

def kernel_p(pos_ref,tab_ref,bias_ref):
    npair,n,_=tab_ref.shape
    WIN=bias_ref.shape[-1]
    tiles=-(-WIN//128)
    def row(r,_):
        r8=pl.multiple_of(r*8,8)
        for c in range(tiles):
            width=min(128,WIN-c*128)
            idx=pos_ref[pl.ds(r8,8),c*128:(c+1)*128]
            lo=idx&127; hi=idx>>7
            masks=[hi==k for k in range(n)]
            for p in range(npair):
                acc=jnp.zeros((8,128),jnp.int32)
                for k in range(n):
                    src=jnp.broadcast_to(tab_ref[p,k:k+1,:],(8,128))
                    acc=jnp.where(masks[k],jnp.take_along_axis(src,lo,axis=1),acc)
                a=(acc>>16).astype(F32)*(SQ/FIX)
                b=((acc<<16)>>16).astype(F32)*(SQ/FIX)
                bias_ref[2*p,pl.ds(r8,8),c*128:c*128+width]=a[:,:width]
                bias_ref[2*p+1,pl.ds(r8,8),c*128:c*128+width]=b[:,:width]
        return 0
    lax.fori_loop(0,bias_ref.shape[1]//8,row,0)

def call_p(posT_pad,tab,WIN):
    NH=tab.shape[0]*2
    return pl.pallas_call(kernel_p,out_shape=jax.ShapeDtypeStruct((NH,WIN,WIN),F32),
      compiler_params=pltpu.CompilerParams(vmem_limit_bytes=40*1024*1024),name="kernel_p")(posT_pad,tab)

def kernel_t(NH,G_ref,hi_ref,lo_ref,out_ref):
    WIN=hi_ref.shape[0]; LW=G_ref.shape[0]*128
    nh=out_ref.shape[0]//NH
    out_ref[...]=jnp.zeros_like(out_ref)
    def rows(r,_):
        r8=pl.multiple_of(r*8,8)
        hi8=hi_ref[pl.ds(r8,8),:]; lo8=lo_ref[pl.ds(r8,8),:]
        tot=jnp.zeros(out_ref.shape,F32)
        iota=lax.broadcasted_iota(jnp.int32,(256,LW),0).astype(F32).astype(BF)
        for k in range(8):
            g=jnp.concatenate([G_ref[c,pl.ds(r8+k,NH,stride=WIN),:] for c in range(LW//128)],axis=1)
            hr=hi8[k:k+1,:]; lr=lo8[k:k+1,:].astype(F32).astype(BF)
            A=jnp.concatenate([jnp.where(hr==m,g,0.0) for m in range(nh)],axis=0).astype(BF)
            oh=jnp.where(iota==lr,jnp.ones((),BF),jnp.zeros((),BF))
            tot=tot+lax.dot_general(A,oh,(((1,),(1,)),((),())),preferred_element_type=F32)
        out_ref[...]+=tot
        return 0
    lax.fori_loop(0,WIN//8,rows,0)

def call_t(G,posT,T,NH):
    WIN=posT.shape[0]; nt=G.shape[0]
    nh=-(-T//256)
    pp=jnp.pad(posT,((0,0),(0,nt*128-WIN)),constant_values=nh*256)
    hi=pp>>8; lo=pp&255
    o=pl.pallas_call(functools.partial(kernel_t,NH),out_shape=jax.ShapeDtypeStruct((nh*NH,256),F32),
      compiler_params=pltpu.CompilerParams(vmem_limit_bytes=40*1024*1024),name="kernel_t")(G,hi,lo)
    return o.reshape(nh,NH,256).transpose(1,0,2).reshape(NH,nh*256)[:,:T]


MESHID=pl.DeviceIdType.MESH

def place_of():
    s=lax.axis_index("seq"); y=lax.axis_index("heads")
    return s//4,(s//2)%2,s%2,y

def dev(z,x,c,y):
    return ((z*2+x)*2+c,y)

def peers_of(z,x,c,y):
    return [dev(z,x,1-c,y),dev(z,1-x,c,y),dev(z,x,c,1-y)]+[dev((z+i)%4,x,c,y) for i in (1,2,3)]

def greet(devices):
    bar=pltpu.get_barrier_semaphore()
    for d in devices:
        pl.semaphore_signal(bar,inc=1,device_id=d,device_id_type=MESHID)
    pl.semaphore_wait(bar,len(devices))

def send(src,dst,ss,rs,to):
    return pltpu.make_async_remote_copy(src_ref=src,dst_ref=dst,send_sem=ss,recv_sem=rs,device_id=to,device_id_type=MESHID)

def kernel_w(w_ref,pos_ref,tab_ref,W_hbm,bias_hbm,bias_s,ss,rs,bs,br,bl,own):
    z,x,c,y=place_of()
    greet(peers_of(z,x,c,y))
    npair,n=tab_ref.shape[1],tab_ref.shape[2]
    half=2*npair
    WIN=bias_s.shape[-1]; tiles=-(-WIN//128)
    xa=x+(1-2*x)*(1-c); ya=y+(1-2*y)*c
    xb=x+(1-2*x)*c; yb=y+(1-2*y)*(1-c)
    sib=dev(z,x,1-c,y); pa=dev(z,xa,c,ya); pb=dev(z,xb,c,yb)
    started=[]
    def go(src,zz,xx,yy,k,to):
        cp=send(src,W_hbm.at[yy,zz,xx,c],ss.at[k],rs.at[k],to); cp.start(); started.append(cp)
    def came(zz,xx,cc,yy,k):
        send(w_ref,W_hbm.at[yy,zz,xx,cc],ss.at[k],rs.at[k],sib).wait_recv()
    mine=pltpu.make_async_copy(w_ref,W_hbm.at[y,z,x,c],own); mine.start()
    for i in (1,2,3):
        go(w_ref,z,x,y,i-1,dev((z+i)%4,x,c,y))
    go(w_ref,z,x,y,3,pa); go(w_ref,z,x,y,7,pb); go(w_ref,z,x,y,15,sib)
    def zof(i): return (z+4-i)%4
    def turn_z(i):
        zz=zof(i); came(zz,x,c,y,i-1)
        blk=W_hbm.at[y,zz,x,c]
        go(blk,zz,x,y,3+i,pa); go(blk,zz,x,y,7+i,pb); go(blk,zz,x,y,15+i,sib)
    def turn_a(i):
        zz=zof(i); came(zz,xa,c,ya,3+i)
        blk=W_hbm.at[ya,zz,xa,c]
        go(blk,zz,xa,ya,11+i,pb); go(blk,zz,xa,ya,19+i,sib)
    def turn_b(i):
        zz=zof(i); came(zz,xb,c,yb,7+i)
        go(W_hbm.at[yb,zz,xb,c],zz,xb,yb,23+i,sib)
    def turn_ab(i):
        zz=zof(i); came(zz,1-x,c,1-y,11+i)
        go(W_hbm.at[1-y,zz,1-x,c],zz,1-x,1-y,27+i,sib)
    nrow=WIN//8
    steps=7
    cuts=[nrow*k//steps for k in range(steps+1)]
    sends=[]
    def rows(k):
        def row(r,_):
            r8=pl.multiple_of(r*8,8)
            for t in range(tiles):
                width=min(128,WIN-t*128)
                idx=pos_ref[pl.ds(r8,8),t*128:(t+1)*128]
                lo=idx&127; hi=idx>>7
                masks=[hi==q for q in range(n)]
                for p in range(npair):
                    acc=jnp.zeros((8,128),jnp.int32)
                    for q in range(n):
                        src=jnp.broadcast_to(tab_ref[c,p,q:q+1,:],(8,128))
                        acc=jnp.where(masks[q],jnp.take_along_axis(src,lo,axis=1),acc)
                    a=(acc>>16).astype(F32)*(SQ/FIX)
                    b=((acc<<16)>>16).astype(F32)*(SQ/FIX)
                    bias_s[2*p,pl.ds(r8,8),t*128:t*128+width]=a[:,:width]
                    bias_s[2*p+1,pl.ds(r8,8),t*128:t*128+width]=b[:,:width]
            return 0
        lax.fori_loop(cuts[k],cuts[k+1],row,0)
        rr=pl.ds(cuts[k]*8,(cuts[k+1]-cuts[k])*8)
        cp=pltpu.make_async_copy(bias_s.at[:,rr],bias_hbm.at[pl.ds(c*half,half),rr],bl.at[k]); cp.start()
        rc=send(bias_s.at[:,rr],bias_hbm.at[pl.ds(c*half,half),rr],bs.at[k],br.at[k],sib); rc.start()
        sends.append((cp,rc))
    rows(0)
    turn_z(1); turn_z(3)
    rows(1)
    turn_z(2); turn_a(0); turn_b(0)
    rows(2)
    for i in (1,3): turn_a(i); turn_b(i)
    rows(3)
    for i in (2,): turn_a(i); turn_b(i)
    turn_ab(0)
    rows(4)
    for i in (1,3): turn_ab(i)
    rows(5)
    turn_ab(2)
    rows(6)
    for i in range(4):
        zz=zof(i)
        came(zz,x,1-c,y,15+i); came(zz,xb,1-c,yb,19+i); came(zz,xa,1-c,ya,23+i); came(zz,1-x,1-c,1-y,27+i)
    for k in range(steps):
        rr=pl.ds(cuts[k]*8,(cuts[k+1]-cuts[k])*8)
        sends[k][0].wait(); sends[k][1].wait_send()
        send(bias_s.at[:,rr],bias_hbm.at[pl.ds((1-c)*half,half),rr],bs.at[k],br.at[k],sib).wait_recv()
    for cp in started: cp.wait_send()
    mine.wait()

def call_w(wcat,posT_pad,tab,WIN):
    rows,cols=wcat.shape; npair=tab.shape[1]
    return pl.pallas_call(kernel_w,
      out_shape=[jax.ShapeDtypeStruct((2,4,2,2,rows,cols),BF),jax.ShapeDtypeStruct((4*npair,WIN,WIN),F32)],
      in_specs=[pl.BlockSpec(memory_space=pl.ANY),pl.BlockSpec(memory_space=pltpu.VMEM),pl.BlockSpec(memory_space=pltpu.VMEM)],
      out_specs=[pl.BlockSpec(memory_space=pl.ANY)]*2,
      scratch_shapes=[pltpu.VMEM((2*npair,WIN,WIN),F32),pltpu.SemaphoreType.DMA((31,)),pltpu.SemaphoreType.DMA((31,)),
        pltpu.SemaphoreType.DMA((7,)),pltpu.SemaphoreType.DMA((7,)),pltpu.SemaphoreType.DMA((7,)),pltpu.SemaphoreType.DMA],
      compiler_params=pltpu.CompilerParams(vmem_limit_bytes=40*1024*1024,collective_id=1,has_side_effects=True),name="kernel_w")(wcat,posT_pad,tab)

class Reduce:
    def __init__(self,src,out,own,r1,r2,ss,rs,ls,r3=None,fin=None,r4=None,mid=None):
        self.src,self.out,self.own,self.r1,self.r2,self.r3,self.fin,self.r4=src,out,own,r1,r2,r3,fin,r4
        self.ss,self.rs,self.ls=ss,rs,ls
        self.at=place_of()
        self.mid=own.at[self.at[1]] if mid is None else mid
        self.whole=mid is None
    def pairs(self):
        z,x,c,y=self.at
        k=0
        for xx in range(2):
            for yy in range(2):
                yield (pltpu.make_async_copy(self.src.at[yy,:,xx,c],self.own.at[xx,:,yy],self.ls.at[k]),
                       send(self.src.at[yy,:,xx,1-c],self.r1.at[xx,:,yy],self.ss.at[k],self.rs.at[k],dev(z,x,1-c,y)))
                k+=1
    def xsend(self):
        z,x,c,y=self.at
        return send(self.own.at[1-x],self.r2,self.ss.at[4],self.rs.at[4],dev(z,1-x,c,y))
    def zsend(self,i):
        z,x,c,y=self.at
        zz=(z+i)%4
        return send(self.mid.at[zz],self.r3.at[i-1],self.ss.at[4+i],self.rs.at[4+i],dev(zz,x,c,y))
    def ysend(self):
        z,x,c,y=self.at
        return send(self.fin.at[1-y],self.r4,self.ss.at[8],self.rs.at[8],dev(z,x,c,1-y))
    def start(self):
        for a,b in self.pairs():
            a.start(); b.start()
    def add(self,dst,*srcs):
        total=srcs[0][...].astype(F32)
        for s in srcs[1:]: total=total+s[...].astype(F32)
        dst[...]=total.astype(BF)
    def one(self):
        z,x,c,y=self.at
        for a,b in self.pairs():
            a.wait(); b.wait_recv()
        def step(xx):
            def add(k,_):
                at=(xx,k//2,k%2)
                self.add(self.own.at[at],self.own.at[at],self.r1.at[at])
                return 0
            lax.fori_loop(0,8,add,0)
        step(1-x)
        self.xsend().start()
        step(x)
    def summed(self):
        z,x,c,y=self.at
        def add(k,_):
            at=(k//2,k%2)
            self.add(self.own.at[(x,)+at],self.own.at[(x,)+at],self.r2.at[at])
            return 0
        lax.fori_loop(0,8,add,0)
    def half(self,hbm,sem):
        self.xsend().wait_recv()
        self.summed()
        cp=pltpu.make_async_copy(self.mid,hbm,sem); cp.start(); cp.wait()
        self.left()
    def left(self):
        for a,b in self.pairs(): b.wait_send()
        self.xsend().wait_send()
    def zstart(self):
        for i in (2,1,3): self.zsend(i).start()
    def two(self):
        self.xsend().wait_recv()
        self.summed()
        self.zstart()
    def three(self):
        z,x,c,y=self.at
        for i in (1,2,3):
            self.zsend(i).wait_recv()
        def step(yy):
            self.add(self.fin.at[yy],self.mid.at[z,yy],*[self.r3.at[i,yy] for i in range(3)])
        step(1-y)
        self.ysend().start()
        step(y)
    def four(self):
        z,x,c,y=self.at
        self.ysend().wait_recv()
        self.out[...]=self.fin[y].astype(F32)+self.r4[...].astype(F32)
        if self.whole: self.left()
        for i in (1,2,3): self.zsend(i).wait_send()
        self.ysend().wait_send()

def reduce_scratch(rows,cols,last=True,first=True):
    v=lambda *d: pltpu.VMEM(d+(rows,cols),BF)
    return ((([v(2,4,2),v(2,4,2),v(4,2)]) if first else [])+[pltpu.SemaphoreType.DMA((9,)),pltpu.SemaphoreType.DMA((9,)),pltpu.SemaphoreType.DMA((4,))]
            +([v(3,2),v(2),v()] if last else []))

def kernel_c(NH,G_ref,hi_ref,lo_ref,small_ref,dq_hbm,mid_ref,redq_ref,redm_ref,tab_ref,sum_ref,acc,tk,tr,sr,ts,tq,own,r1,r2,ss,rs,ls,r3,fin,r4,ss2,rs2,ls2,s3,sfin,s4):
    WIN=hi_ref.shape[0]; LW=G_ref.shape[0]*128
    nh=acc.shape[0]
    z,x,c,y=place_of()
    greet(peers_of(z,x,c,y))
    red=Reduce(dq_hbm,redq_ref,own,r1,r2,ss,rs,ls,r3,fin,r4)
    big=Reduce(None,redm_ref,None,None,None,ss2,rs2,ls2,s3,sfin,s4,mid=mid_ref)
    red.start(); big.zstart()
    acc[...]=jnp.zeros_like(acc)
    def rows(r,_):
        r8=pl.multiple_of(r*8,8)
        hi8=hi_ref[pl.ds(r8,8),:]; lo8=lo_ref[pl.ds(r8,8),:]
        tot=jnp.zeros((nh*NH,256),F32)
        iota=lax.broadcasted_iota(jnp.int32,(256,LW),0).astype(F32).astype(BF)
        for k in range(8):
            g=jnp.concatenate([G_ref[q,pl.ds(r8+k,NH,stride=WIN),:] for q in range(LW//128)],axis=1)
            hr=hi8[k:k+1,:]; lr=lo8[k:k+1,:].astype(F32).astype(BF)
            A=jnp.concatenate([jnp.where(hr==m,g,0.0) for m in range(nh)],axis=0).astype(BF)
            oh=jnp.where(iota==lr,jnp.ones((),BF),jnp.zeros((),BF))
            tot=tot+mm_nt(A,oh)
        acc[...]+=tot.reshape(acc.shape)
        return 0
    n=WIN//8
    cuts=[0,n*6//49,n*20//49,n*36//49,n*44//49,n]
    for k,f in enumerate((red.one,red.two,big.three,red.three,big.four)):
        lax.fori_loop(cuts[k],cuts[k+1],rows,0)
        f()
    red.four()
    half=NH//2
    cps=(send(acc.at[:,pl.ds((1-y)*half,half)],tr.at[0],ts.at[0],tq.at[0],dev(z,x,c,1-y)),send(small_ref,sr.at[0],ts.at[1],tq.at[1],dev(z,x,c,1-y)))
    for p in cps: p.start()
    for p in cps: p.wait()
    tk[0]=acc[:,pl.ds(pl.multiple_of(y*half,8),half)]+tr[0]
    small=small_ref[...]+sr[0]
    for k,to in ((1,dev(z,x,1-c,y)),(2,dev(z,1-x,c,y))):
        sr[6+k]=small
        cps=(send(tk.at[k-1],tr.at[k],ts.at[2*k],tq.at[2*k],to),send(sr.at[6+k],sr.at[k],ts.at[2*k+1],tq.at[2*k+1],to))
        for p in cps: p.start()
        for p in cps: p.wait()
        tk[k]=tk[k-1]+tr[k]
        small=small+sr[k]
    sr[9]=small
    cps=[]
    for i in (1,2,3):
        to=dev((z+i)%4,x,c,y); k=2+i
        cps+=[send(tk.at[2],tr.at[k],ts.at[2*k],tq.at[2*k],to),send(sr.at[9],sr.at[k],ts.at[2*k+1],tq.at[2*k+1],to)]
    for p in cps: p.start()
    for p in cps: p.wait()
    tab_ref[...]=tk[2]+tr[3]+tr[4]+tr[5]
    sum_ref[...]=small+sr[3]+sr[4]+sr[5]

def call_c(G,posT,T,NH,small,dq,mid):
    WIN=posT.shape[0]; nt=G.shape[0]
    nh=-(-T//256)
    rows,cols=dq.shape[-2:]; more=mid.shape[-1]
    pp=jnp.pad(posT,((0,0),(0,nt*128-WIN)),constant_values=nh*256)
    hi=pp>>8; lo=pp&255
    vm=pl.BlockSpec(memory_space=pltpu.VMEM)
    redq,redm,tab,sm=pl.pallas_call(functools.partial(kernel_c,NH),
      out_shape=[jax.ShapeDtypeStruct((rows,cols),F32),jax.ShapeDtypeStruct((rows,more),F32),jax.ShapeDtypeStruct((nh,NH//2,256),F32),jax.ShapeDtypeStruct(small.shape,F32)],
      in_specs=[vm,vm,vm,vm,ANY,vm],out_specs=[vm]*4,
      scratch_shapes=[pltpu.VMEM((nh,NH,256),F32)]+[pltpu.VMEM((3,nh,NH//2,256),F32),pltpu.VMEM((6,nh,NH//2,256),F32),
        pltpu.VMEM((10,)+small.shape,F32),pltpu.SemaphoreType.DMA((12,)),pltpu.SemaphoreType.DMA((12,))]+reduce_scratch(rows,cols)+reduce_scratch(rows,more,True,False),
      compiler_params=pltpu.CompilerParams(vmem_limit_bytes=60*1024*1024,collective_id=3,has_side_effects=True),name="kernel_c")(G,hi,lo,small,dq,mid)
    return redq,redm,tab.transpose(1,0,2).reshape(NH//2,nh*256)[:,:T],sm

def gathered(piece,names,nseq,nheads):
    full=lax.all_gather(piece,names,axis=0,tiled=False)
    return full.reshape((nseq,nheads)+piece.shape)

def natural(block):
    s,h,r,c=block.shape
    return block.transpose(0,2,1,3).reshape(s*r,h*c)

def owners(grad,nseq,nheads):
    r,c=grad.shape
    return grad.reshape(nseq,r//nseq,nheads,c//nheads).transpose(0,2,1,3).reshape(nseq*nheads,r//nseq,c//nheads)

def from_next(rows):
    n=lax.axis_size("seq")
    return lax.ppermute(rows,"seq",[(i,(i-1)%n) for i in range(n)])

def to_next(rows):
    n=lax.axis_size("seq")
    return lax.ppermute(rows,"seq",[(i,(i+1)%n) for i in range(n)])

def spread(rows):
    n=lax.axis_size("heads")
    flat=rows.reshape(-1,rows.shape[-1])
    if n==2:
        other=lax.ppermute(flat,"heads",[(0,1),(1,0)])
        me=lax.axis_index("heads")
        return jnp.where(me==0,jnp.concatenate([flat,other]),jnp.concatenate([other,flat]))
    return lax.all_gather(flat,"heads",axis=0,tiled=True)

def place(rows,other,base,shift):
    if other is None:
        every=spread(rows)
    else:
        a,b=[v.reshape(-1,v.shape[-1]) for v in (rows,other)]
        me=lax.axis_index("heads")
        every=jnp.where(me==0,jnp.concatenate([a,b]),jnp.concatenate([b,a]))
    keep=every.shape[0]-shift
    moved=jnp.concatenate([to_next(every[keep:]),every[:keep]])
    return base+moved.astype(F32)

def body(inputs,w_qkv,w_proj,w_fc1,w_fc2,gains,shifts,rel_table,region,pos_index,out_grad):
    nseq=lax.axis_size("seq"); nheads=lax.axis_size("heads"); me=lax.axis_index("heads")
    linked=nseq==16 and nheads==2
    names=("seq","heads")
    tok,D=inputs.shape; WIN=pos_index.shape[0]; shift=WIN//2; T=rel_table.shape[1]
    nW=tok//WIN//nheads
    rows=w_qkv.shape[1]; cq=w_qkv.shape[2]; cf=w_fc1.shape[1]
    wcat=jnp.concatenate([w_qkv[0],w_qkv[1],w_qkv[2],w_proj.T,w_fc1,w_fc2.T],axis=1).astype(BF)
    table=lax.all_gather(rel_table,"heads",axis=0,tiled=True)
    NH=table.shape[0]
    posT=pos_index.T
    wide=-(-WIN//128)*128
    posP=jnp.pad(posT,((0,0),(0,wide-WIN)))
    tab=pack_table(table)
    if linked:
        W,bias=call_w(wcat,posP,tab.reshape((2,tab.shape[0]//2)+tab.shape[1:]),WIN)
        W=W.reshape(nheads,D,-1)
    else:
        every=gathered(wcat,names,nseq,nheads)
        ends=[i*cq for i in range(5)]+[4*cq+cf,4*cq+2*cf]
        W=jnp.concatenate([natural(every[...,a:b]) for a,b in zip(ends[:-1],ends[1:])],axis=1)[None]
        bias=call_p(posP,tab,WIN)
    start=me*nW*WIN
    def mine(v):
        ext=jnp.concatenate([v,from_next(v[:shift])])
        return lax.dynamic_slice_in_dim(ext,start+shift,nW*WIN,0).reshape(nW,WIN,-1)
    x=mine(inputs); og=mine(out_grad)
    lab=lax.dynamic_slice_in_dim(region,start,nW*WIN,0).reshape(nW,WIN)
    delta,gln2,qkv,g,gT,Dd,Pp,dcat,sm_a=call_a(x,og,lab[:,:,None],lab[:,None,:],bias,W,gains,shifts)
    if linked:
        dcat=dcat.reshape(2,4,2,2,rows,-1)
    dd,dqkv,G,sm_b,od,odd,mid=call_b(linked,x,gln2,qkv,g,gT,Dd,Pp,W,gains,shifts,delta,dcat)
    if linked:
        redq,redm,d_table,small=call_c(G,posT,T,NH,sm_a+sm_b,dqkv.reshape(2,4,2,2,rows,-1),mid)
    else:
        od=odd=None
        wide=D+2*cf*nheads
        grads=[dqkv[0,:,c*D:(c+1)*D] for c in range(3)]+[dcat[0,:,:D],dcat[0,:,D:D+cf*nheads],dcat[0,:,D+cf*nheads:]]
        red=lax.psum_scatter(jnp.concatenate([owners(v,nseq,nheads) for v in grads],axis=2),names,scatter_dimension=0,tiled=False).astype(F32)
        redq,redm=red[:,:3*cq],red[:,3*cq:]
        d_table,small=lax.psum((call_t(G,posT,T,NH),sm_a+sm_b),names)
        nl=rel_table.shape[0]
        d_table=lax.dynamic_slice_in_dim(d_table,me*nl,nl,0)
    output=place(delta,od,inputs,shift)
    d_inputs=place(dd,odd,out_grad,shift)
    d_qkv=redq.reshape(rows,3,cq).transpose(1,0,2)
    d_proj=redm[:,:cq].T; d_fc1=redm[:,cq:cq+cf]; d_fc2=redm[:,cq+cf:].T
    return (output,d_inputs,d_qkv,d_proj,d_fc1,d_fc2,small[0:2],small[2:6],d_table)

def solution(mesh):
    placed=(P("seq",None),P(None,"seq","heads"),P("heads","seq"),P("seq","heads"),P("heads","seq"),P(),P(),P("heads",None),P("seq"),P(),P("seq",None))
    return jax.shard_map(body,mesh=mesh,in_specs=placed,
        out_specs=(P("seq",None),P("seq",None),P(None,"seq","heads"),P("heads","seq"),P("seq","heads"),P("heads","seq"),P(),P(),P("heads",None)),
        check_vma=False)
```

time: 644 us -> 347 us (0.54)
  waiting for transfers between devices: 192 us -> 8.37 us
  blocking collectives: 109 us -> 5.32 us
  Pallas kernels: 220 us -> 281 us
  local copies, waits for them, and re-layouts: 63.7 us -> 16.3 us
  between operations: 14.2 us -> 1 us
    reduce_scatter x2 -> x0, waiting for transfers between devices: 189 us -> none  [the longest x1 110 us: body(): lax.psum_scatter(pieces, names, scatter_dimension=0, tiled=False)]
    psum x1 -> x0, blocking collectives: 103 us -> none  [body(): tab, small = lax.psum((tab, sm_a + sm_b), names)]
    pallas_call x3, Pallas kernels: 130 us -> 192 us  [the longest x1 84.7 us: call_b(): pl.pallas_call(functools.partial(kernel_b, NH, linked), grid=(nW,), in_sp...]
    unnamed x58 -> x44, local copies, waits for them, and re-layouts: 31.2 us -> 4.41 us
    reshape x9 -> x1, local copies, waits for them, and re-layouts: 11.1 us -> 0.05 us  [body(): d_qkv = redq.reshape(rows, 3, cq).transpose(1, 0, 2)]
    ppermute x2, waiting for transfers between devices: 1.62 us -> 8.36 us  [to_next(): return lax.ppermute(rows, 'seq', [(i, (i + 1) % n) for i in range(n)])]
  transfers between devices with their start and end apart: 10 -> 4, of which waited for: 5 -> 1; matrix products, arithmetic and copies ran while one was open for 8% -> 6% of each run, Pallas kernels for 6% -> 11%
where the time goes in v2:
time: 347 us
  Pallas kernels  281 us (81%)
  other arithmetic  27.5 us (8%)
  local copies, waits for them, and re-layouts  16.3 us (5%)
  waiting for transfers between devices  8.37 us (2%)
  starting transfers between devices  7.18 us (2%)
  blocking collectives  5.32 us (2%)
    pallas_call x1, Pallas kernels, call_a(): pl.pallas_call(functools.partial(kernel_a, NH), grid=(nW,), in_specs=[per...  89.2 us
    pallas_call x1, Pallas kernels, call_b(): pl.pallas_call(functools.partial(kernel_b, NH, linked), grid=(nW,), in_sp...  84.7 us
    pallas_call x1, Pallas kernels, call_c(): pl.pallas_call(functools.partial(kernel_c, NH), out_shape=[jax.ShapeDtype...  69 us
    pallas_call x1, Pallas kernels, call_w(): pl.pallas_call(kernel_w, out_shape=[jax.ShapeDtypeStruct((2, 4, 2, 2, row...  38.4 us
    add x2, other arithmetic, place(): return base + moved.astype(F32)  11.5 us
    concatenate x2, other arithmetic, mine(): ext = jnp.concatenate([v, from_next(v[:shift])])  10.2 us
    ppermute x2, waiting for transfers between devices, to_next(): return lax.ppermute(rows, 'seq', [(i, (i + 1) % n) for i in range(n)])  8.36 us
  transfers between devices with their start and end apart: 4, of which 1 were waited for; matrix products, arithmetic and copies ran while one was open for 6% of the time, Pallas kernels for 11%

profile of v2, /device:TPU:0, one launch (start us, length us, event | category | flops | bytes accessed | tf_op | source)
XLA Modules:
  0.0 346.8 jit_solution(7995237887003577199)
XLA Ops:
  0.6 0.0 copy-start.6
  0.7 0.0 copy-start.12
  0.7 0.0 copy-start.8
  0.7 0.0 copy-start.9
  0.7 1.9 slice.55
  2.6 5.4 %collective-permute-start.1 = (f32[196,512]{1,0:T(8,128)}, f32[196,512]{1,0:T(8,128)}, u32[]{:S(2)}, u32[]{:S(2)}) collective-permute-start(f32[196,512]{1,0:T(8,128)} %slice.55), channel_id=1, source_target_pairs={{0,30},{2,0},{4,2},{6,4},{8,6},{10,8},{12,10},{14,12},{16,14},{18,... | collective-permute-start | bytes 1204232 | tf_op jit(solution)/shard_map/ppermute | solution.py:623
  8.0 1.8 slice.54
  9.7 0.7 collective-permute-start
  10.4 0.9 convert.22
  11.3 5.3 %all_gather.3 = f32[16,2535]{1,0:T(8,128)S(1)} all-gather(f32[8,2535]{1,0:T(8,128)} %param.18), channel_id=1, replica_groups=mesh['seq'=16,'heads'=2] {'heads'}, dimensions={0}, use_global_device_ids=true | all-gather | bytes 243360 | tf_op jit(solution)/shard_map/all_gather | solution.py:657
  16.7 0.0 copy-start.14
  16.8 0.0 copy-done.6
  16.8 0.3 copy.24
  17.1 0.0 copy-done.12
  17.1 0.0 copy-done.8
  17.1 0.0 copy-done.9
  17.2 1.5 pad_and_fusion
  18.7 0.0 copy-done.14
  18.7 0.1 dynamic_slice.11
  18.7 0.7 broadcast_in_dim_reshape.7.labr_ref
  19.4 1.6 broadcast_in_dim_reshape.8.labc_ref
  21.0 38.4 %kernel_w.1 = (bf16[2,4,2,2,32,3072]{5,4,3,2,1,0:T(8,128)(2,1)S(1)}, f32[16,392,392]{2,1,0:T(8,128)}) custom-call(bf16[32,3072]{1,0:T(8,128)(2,1)S(1)} %bitcast_dynamic-update-slice_fusion.w_ref, s32[392,512]{1,0:T(8,128)S(1)} %get-tuple-element.64.pos_ref, s32[2,4,20,128]{3,2,1,0:T(8,128)S(1)} %bitcast.38), custom_call_target="tpu_custom_call" | custom-call | tf_op jit(solution)/shard_map/kernel_w/pallas_call | solution.py:447
  59.4 0.0 copy-start
  59.4 0.0 slice-start.1
  59.4 0.0 collective-permute-done
  59.4 7.2 %fusion.1 = f32[1568,512]{1,0:T(8,128)} fusion(s32[]{:T(128)S(6)} %select_n.20, f32[3136,512]{1,0:T(8,128)} %param.11, f32[196,512]{1,0:T(8,128)} %collective-permute-done), kind=kLoop, calls=%fused_computation.7 | loop fusion | flops 802816 | bytes 10035204 | tf_op jit(solution)/shard_map/concatenate | solution.py:673
  66.6 0.0 copy-done
  66.6 0.0 collective-permute-done.1
  66.6 0.0 slice-done
  66.6 0.0 slice-done.1
  66.7 2.9 fusion
  69.6 89.2 %kernel_a.1 = (bf16[4,392,512]{2,1,0:T(8,128)(2,1)}, f32[4,392,512]{2,1,0:T(8,128)}, bf16[4,3,392,512]{3,2,1,0:T(8,128)(2,1)}, bf16[4,392,512]{2,1,0:T(8,128)(2,...) custom-call(f32[4,392,512]{2,1,0:T(8,128)} %bitcast.39, ...), custom_call_target="tpu_custom_call" | custom-call | tf_op jit(solution)/shard_map/kernel_a/pallas_call | solution.py:163
  158.8 0.0 copy-start.13
  158.8 84.7 %kernel_b.1 = (bf16[4,392,512]{2,1,0:T(8,128)(2,1)}, bf16[2,512,768]{2,1,0:T(8,128)(2,1)}, f32[4,6272,128]{2,1,0:T(8,128)}, f32[8,512]{1,0:T(8,128)}, bf16[4,392...) custom-call(f32[4,392,512]{2,1,0:T(8,128)} %bitcast.40, ...), custom_call_target="tpu_custom_call" | custom-call | tf_op jit(solution)/shard_map/kernel_b/pallas_call | solution.py:263
  243.5 0.0 copy-done.13
  243.5 1.3 add.33.small_ref
  244.8 69.0 %kernel_c.1 = (f32[32,768]{1,0:T(8,128)}, f32[32,2304]{1,0:T(8,128)}, f32[10,8,256]{2,1,0:T(8,128)}, f32[8,512]{1,0:T(8,128)}) custom-call(f32[4,6272,128]{2,1,0:T(8,128)} %get-tuple-element.44.G_ref, s32[392,512]{1,0:T(8,128)} %get-tuple-element.63.hi_ref, s32[392,512]{1,0:T(8,128)} %get-tuple-element.62.lo_ref, f32[8,512]{1,0:T(8,128)} %add.33.small_ref, ...), custom_call_target="tpu_custom_call" | custom-call | tf_op jit(solution)/shard_map/kernel_c/pallas_call | solution.py:601
  313.8 1.3 slice.68
  315.1 1.3 slice.69
  316.4 0.0 copy-done.4
  316.4 0.0 copy-done.5
  316.4 1.0 maximum_select_fusion.1
  317.4 0.1 slice.78
  317.5 1.8 slice.79
  319.3 0.0 copy-done.2
  319.3 1.1 copy-done.3
  320.4 1.0 maximum_select_fusion
  321.4 0.0 copy-start.1
  321.4 0.0 copy-start.10
  321.4 0.1 slice.76
  321.5 0.0 slice-start.2
  321.5 1.6 copy-done.1
  323.1 0.0 copy-done.10
  323.1 0.1 reshape.72
  323.2 0.7 copy.26
  323.8 0.7 slice_bitcast_fusion
  324.5 0.0 collective-permute-start.2
  324.5 1.1 collective-permute-start.3
  325.6 0.6 slice_bitcast_fusion.1
  326.3 8.4 %collective-permute-done.3 = bf16[196,512]{1,0:T(8,128)(2,1)S(1)} collective-permute-done((bf16[196,512]{1,0:T(8,128)(2,1)S(1)}, bf16[196,512]{1,0:T(8,128)(2,1)S(1)}, u32[]{:S(2)}, u32[]{:S(2)}) %collective-permute-start.3) | collective-permute-done | bytes 200736 | tf_op jit(solution)/shard_map/ppermute | solution.py:627
  334.6 7.6 %convert_add_fusion = f32[3136,512]{1,0:T(8,128)} fusion(f32[3136,512]{1,0:T(8,128)} %param.21, bf16[2940,512]{1,0:T(8,128)(2,1)} %slice.79, bf16[196,512]{1,0:T(8,128)(2,1)S(1)} %collective-permute-done.3), kind=kLoop, calls=%fused_computation.4 | loop fusion | flops 8028160 | bytes 16056320 | tf_op jit(solution)/shard_map/add | solution.py:647
  342.2 0.0 collective-permute-done.2
  342.2 4.0 %convert_add_fusion.1 = f32[3136,512]{1,0:T(8,128)} fusion(f32[3136,512]{1,0:T(8,128)S(1)} %bitcast.44, bf16[2940,512]{1,0:T(8,128)(2,1)S(1)} %slice-done.4, bf16[196,512]{1,0:T(8,128)(2,1)S(1)} %collective-permute-done.2), kind=kLoop, calls=%fused_computation.5 | loop fusion | flops 8028160 | bytes 16056320 | tf_op jit(solution)/shard_map/add | solution.py:647
  346.2 0.6 copy.33
  (26 shorter events, 0.1 us)
Async XLA Ops:
  0.6 16.2 %copy-start.6 = (s32[392,392]{1,0:T(8,128)S(1)}, s32[392,392]{1,0:T(8,128)}, u32[]{:S(2)}) copy-start(s32[392,392]{1,0:T(8,128)} %param.20) | copy-start | bytes 1843972
  0.7 16.4 %copy-start.12 = (f32[256,32]{0,1:T(8,128)S(1)}, f32[256,32]{0,1:T(8,128)}, u32[]{:S(2)}) copy-start(f32[256,32]{0,1:T(8,128)} %param.13) | copy-start | bytes 98308
  0.7 16.4 %copy-start.8 = (f32[32,1024]{1,0:T(8,128)S(1)}, f32[32,1024]{1,0:T(8,128)}, u32[]{:S(2)}) copy-start(f32[32,1024]{1,0:T(8,128)} %param.14) | copy-start | bytes 393220
  0.7 16.5 %copy-start.9 = (f32[1024,32]{0,1:T(8,128)S(1)}, f32[1024,32]{0,1:T(8,128)}, u32[]{:S(2)}) copy-start(f32[1024,32]{0,1:T(8,128)} %param.15) | copy-start | bytes 393220
  2.6 64.1 %collective-permute-start.1 = (f32[196,512]{1,0:T(8,128)}, f32[196,512]{1,0:T(8,128)}, u32[]{:S(2)}, u32[]{:S(2)}) collective-permute-start(f32[196,512]{1,0:T(8,128)} %slice.55), channel_id=1, source_target_pairs={{0,30},{2,0},{4,2},{6,4},{8,6},{10,8},{12,10},{14,12},{16,14},{18,... | collective-permute-start | bytes 1204232 | tf_op jit(solution)/shard_map/ppermute | solution.py:623
  9.7 49.6 %collective-permute-start = (f32[196,512]{1,0:T(8,128)}, f32[196,512]{1,0:T(8,128)}, u32[]{:S(2)}, u32[]{:S(2)}) collective-permute-start(f32[196,512]{1,0:T(8,128)} %slice.54), channel_id=1, source_target_pairs={{0,30},{2,0},{4,2},{6,4},{8,6},{10,8},{12,10},{14,12},{16,14},{18,... | collective-permute-start | bytes 1204232 | tf_op jit(solution)/shard_map/ppermute | solution.py:623
  16.7 2.0 copy-start.14
  19.4 47.2 %slice-start = ((s8[6422528]{0:T(1024)(128)(4,1)}), s8[2228224]{0:T(1024)(128)(4,1)S(1)}, s32[]{:S(2)}) async-start(s8[6422528]{0:T(1024)(128)(4,1)} %bitcast.41), calls=%async_computation | async-start | bytes 4456448
  59.4 7.3 %copy-start = (bf16[2,4,2,2,32,3072]{5,4,3,2,1,0:T(8,128)(2,1)}, bf16[2,4,2,2,32,3072]{5,4,3,2,1,0:T(8,128)(2,1)S(1)}, u32[]{:S(2)}) copy-start(bf16[2,4,2,2,32,3072]{5,4,3,2,1,0:T(8,128)(2,1)S(1)} %get-tuple-element.32) | copy-start | bytes 18874372
  59.4 7.3 %slice-start.1 = ((s8[6422528]{0:T(1024)(128)(4,1)}), s8[4194304]{0:T(1024)(128)(4,1)S(1)}, s32[]{:S(2)}) async-start(s8[6422528]{0:T(1024)(128)(4,1)} %bitcast.41), calls=%async_computation.1 | async-start | bytes 8388608
  158.8 84.7 %copy-start.13 = (f32[8,512]{1,0:T(8,128)S(1)}, f32[8,512]{1,0:T(8,128)}, u32[]{:S(2)}) copy-start(f32[8,512]{1,0:T(8,128)} %get-tuple-element.45) | copy-start | bytes 49156
  244.8 71.6 %copy-start.4 = (bf16[4,392,512]{2,1,0:T(8,128)(2,1)S(1)}, bf16[4,392,512]{2,1,0:T(8,128)(2,1)}, u32[]{:S(2)}) copy-start(bf16[4,392,512]{2,1,0:T(8,128)(2,1)} %get-tuple-element.42) | copy-start | bytes 4816900
  244.8 71.6 %copy-start.5 = (bf16[4,392,512]{2,1,0:T(8,128)(2,1)S(1)}, bf16[4,392,512]{2,1,0:T(8,128)(2,1)}, u32[]{:S(2)}) copy-start(bf16[4,392,512]{2,1,0:T(8,128)(2,1)} %get-tuple-element.43) | copy-start | bytes 4816900
  317.4 1.9 copy-start.2
  317.4 3.0 copy-start.3
  321.4 1.7 copy-start.1
  321.4 1.7 copy-start.10
  321.5 2.3 copy-start.7
  321.5 20.7 %slice-start.2 = ((s8[6422528]{0:T(1024)(128)(4,1)}), s8[2228224]{0:T(1024)(128)(4,1)S(1)}, s32[]{:S(2)}) async-start(s8[6422528]{0:T(1024)(128)(4,1)} %bitcast.43), calls=%async_computation.2 | async-start | bytes 4456448
  324.5 17.6 %collective-permute-start.2 = (bf16[196,512]{1,0:T(8,128)(2,1)S(1)}, bf16[196,512]{1,0:T(8,128)(2,1)S(1)}, u32[]{:S(2)}, u32[]{:S(2)}) collective-permute-start(bf16[196,512]{1,0:T(8,128)(2,1)S(1)} %slice.76), channel_id=1, source_target_pairs={{0,2},{2,4},{4,6},{6,8},{8,10},{10,12},{12,14},{14,16},{16,18},{18... | collective-permute-start | bytes 602120 | tf_op jit(solution)/shard_map/ppermute | solution.py:627
  324.5 10.1 %collective-permute-start.3 = (bf16[196,512]{1,0:T(8,128)(2,1)S(1)}, bf16[196,512]{1,0:T(8,128)(2,1)S(1)}, u32[]{:S(2)}, u32[]{:S(2)}) collective-permute-start(bf16[196,512]{1,0:T(8,128)(2,1)S(1)} %slice.78), channel_id=1, source_target_pairs={{0,2},{2,4},{4,6},{6,8},{8,10},{10,12},{12,14},{14,16},{16,18},{18... | collective-permute-start | bytes 602120 | tf_op jit(solution)/shard_map/ppermute | solution.py:627
  326.2 15.9 %slice-start.3 = ((s8[6422528]{0:T(1024)(128)(4,1)}), s8[4194304]{0:T(1024)(128)(4,1)S(1)}, s32[]{:S(2)}) async-start(s8[6422528]{0:T(1024)(128)(4,1)} %bitcast.43), calls=%async_computation.3 | async-start | bytes 8388608
  326.3 15.9 %slice-start.4 = ((bf16[3136,512]{1,0:T(8,128)(2,1)}), bf16[2940,512]{1,0:T(8,128)(2,1)S(1)}, s32[]{:S(2)}) async-start(bf16[3136,512]{1,0:T(8,128)(2,1)} %copy-done.1), calls=%async_computation.4 | async-start | bytes 6029312 | tf_op jit(solution)/shard_map/slice | solution.py:646
  342.2 4.0 %copy-start.11 = (f32[10,8,256]{2,1,0:T(8,128)S(1)}, f32[10,8,256]{2,1,0:T(8,128)}, u32[]{:S(2)}) copy-start(f32[10,8,256]{2,1,0:T(8,128)} %get-tuple-element.52) | copy-start | bytes 245764

commit v3 on v2

--- a/solution.py
+++ b/solution.py
@@ -171,23 +171,12 @@
       compiler_params=pltpu.CompilerParams(vmem_limit_bytes=62*1024*1024,dimension_semantics=("arbitrary",)),
       name="kernel_a")(x,og,labc,labr,bias,W,gains,shifts)
 
-def kernel_b(nheads,linked,x_ref,gln2_ref,qkv_ref,g_ref,gT_ref,D_ref,P_ref,W_ref,gains_ref,shifts_ref,delta_hbm,dcat_hbm,
-             dd_hbm,dqkv_ref,G_hbm,small_ref,od_hbm,odd_hbm,mid_hbm,
-             G_s,aq,kT_s,gq_s,gqT_s,sem,dd_s,dl,ds,dr,*red_scratch):
+def kernel_b(nheads,x_ref,gln2_ref,qkv_ref,g_ref,gT_ref,D_ref,P_ref,W_ref,gains_ref,shifts_ref,
+             dd_ref,dqkv_ref,G_hbm,small_ref,G_s,aq,kT_s,gq_s,gqT_s,sem):
     w=pl.program_id(0); nw=pl.num_programs(0)
     D=x_ref.shape[-1]; WIN=x_ref.shape[-2]
     parts=W_ref.shape[0]; cq=D//parts
     groups=nheads//PER
-    if linked:
-        z,xx,cc,yy=place_of()
-        mate=dev(z,xx,cc,1-yy)
-        red=Reduce(dcat_hbm,None,*red_scratch)
-        give=send(delta_hbm,od_hbm,ds.at[nw_of(delta_hbm)],dr.at[nw_of(delta_hbm)],mate)
-        @pl.when(w==0)
-        def _():
-            greet(peers_of(z,xx,cc,yy))
-            red.start()
-            give.start()
     @pl.when(w==0)
     def _():
         aq[...]=jnp.zeros_like(aq); G_s[...]=jnp.zeros_like(G_s); small_ref[...]=jnp.zeros_like(small_ref)
@@ -229,46 +218,27 @@
             gc=gq_s[c,:,m*cq:(m+1)*cq]
             gr=gr+mm_nt(gc,W_ref[m,:,c*cq:(c+1)*cq])
             aq[m,:,c*cq:(c+1)*cq]+=mm(xnT,gc)
-    dd_s[w]=(gln2_ref[0]+norm_back(gr,xhat,rstd,gains_ref[0:1,:])).astype(BF)
-    keep=pltpu.make_async_copy(dd_s.at[w],dd_hbm.at[w],dl.at[w]); keep.start()
-    if linked:
-        send(dd_s.at[w],odd_hbm.at[w],ds.at[w],dr.at[w],mate).start()
-        pl.when(w==0)(red.one)
+    dd_ref[0]=(gln2_ref[0]+norm_back(gr,xhat,rstd,gains_ref[0:1,:])).astype(BF)
     small_ref[0:1,:]+=jnp.sum(gr*xhat,axis=0,keepdims=True)
     small_ref[2:3,:]+=jnp.sum(gr,axis=0,keepdims=True)
     @pl.when(w==nw-1)
     def _():
         dqkv_ref[...]=aq[...].astype(BF)
-        cp=pltpu.make_async_copy(G_s,G_hbm,sem.at[0]); cp.start()
-        if linked:
-            red.half(mid_hbm,sem.at[1])
-        for k in range(nw_of(dd_s)):
-            pltpu.make_async_copy(dd_s.at[k],dd_hbm.at[k],dl.at[k]).wait()
-            if linked:
-                send(dd_s.at[k],odd_hbm.at[k],ds.at[k],dr.at[k],mate).wait()
-        if linked:
-            give.wait()
-        cp.wait()
-
-def nw_of(ref):
-    return ref.shape[0]
-
-def call_b(linked,x,gln2,qkv,g,gT,Dd,Pp,W,gains,shifts,delta,dcat):
+        cp=pltpu.make_async_copy(G_s,G_hbm,sem); cp.start(); cp.wait()
+
+def call_b(x,gln2,qkv,g,gT,Dd,Pp,W,gains,shifts):
     nW,WIN,D=x.shape; NH=Dd.shape[1]
     parts=W.shape[0]; cq=D//parts; tiles=-(-WIN//128)
-    sd=jax.ShapeDtypeStruct; dma=pltpu.SemaphoreType.DMA
-    rows,cols=dcat.shape[-2:]
-    row=sd((nW,WIN,D),BF) if linked else sd((8,128),BF)
-    mid=sd((4,2,rows,cols),BF) if linked else sd((8,128),BF)
-    return pl.pallas_call(functools.partial(kernel_b,NH,linked),grid=(nW,),
+    sd=jax.ShapeDtypeStruct
+    return pl.pallas_call(functools.partial(kernel_b,NH),grid=(nW,),
       in_specs=[per((WIN,D)),per((WIN,D)),per((3,WIN,D)),per((WIN,D)),per((D,WIN)),per((NH,WIN)),per((NH,WIN,WIN)),
-        full((parts,D,3*cq),pipeline_mode=ONE),full(gains.shape),full(shifts.shape),ANY,ANY],
-      out_specs=[ANY,full((parts,D,3*cq)),ANY,full((8,D)),ANY,ANY,ANY],
-      out_shape=[sd((nW,WIN,D),BF),sd((parts,D,3*cq),BF),sd((tiles,NH*WIN,128),F32),sd((8,D),F32),row,row,mid],
+        full((parts,D,3*cq),pipeline_mode=ONE),full(gains.shape),full(shifts.shape)],
+      out_specs=[per((WIN,D)),full((parts,D,3*cq)),ANY,full((8,D))],
+      out_shape=[sd((nW,WIN,D),BF),sd((parts,D,3*cq),BF),sd((tiles,NH*WIN,128),F32),sd((8,D),F32)],
       scratch_shapes=[pltpu.VMEM((tiles,NH*WIN,128),F32),pltpu.VMEM((parts,D,3*cq),F32),pltpu.VMEM((D,WIN),BF),pltpu.VMEM((3,WIN,D),BF),pltpu.VMEM((D,WIN),F32),
-        dma((2,)),pltpu.VMEM((nW,WIN,D),BF),dma((nW,)),dma((nW+1,)),dma((nW+1,))]+(reduce_scratch(rows,cols,False) if linked else []),
-      compiler_params=pltpu.CompilerParams(vmem_limit_bytes=62*1024*1024,dimension_semantics=("arbitrary",),**(dict(collective_id=2,has_side_effects=True) if linked else {})),
-      name="kernel_b")(x,gln2,qkv,g,gT,Dd,Pp,W,gains,shifts,delta,dcat)
+        pltpu.SemaphoreType.DMA],
+      compiler_params=pltpu.CompilerParams(vmem_limit_bytes=62*1024*1024,dimension_semantics=("arbitrary",)),
+      name="kernel_b")(x,gln2,qkv,g,gT,Dd,Pp,W,gains,shifts)
 
 FIX=8191.0
 
@@ -358,43 +328,86 @@
 def send(src,dst,ss,rs,to):
     return pltpu.make_async_remote_copy(src_ref=src,dst_ref=dst,send_sem=ss,recv_sem=rs,device_id=to,device_id_type=MESHID)
 
-def kernel_w(w_ref,pos_ref,tab_ref,W_hbm,bias_hbm,bias_s,ss,rs,bs,br,bl,own):
+
+class Gather:
+    def __init__(self,src,dst,ss,rs,own):
+        self.src,self.dst,self.ss,self.rs,self.own=src,dst,ss,rs,own
+        z,x,c,y=self.at=place_of()
+        self.xa=x+(1-2*x)*(1-c); self.ya=y+(1-2*y)*c
+        self.xb=x+(1-2*x)*c; self.yb=y+(1-2*y)*(1-c)
+        self.sib=dev(z,x,1-c,y); self.pa=dev(z,self.xa,c,self.ya); self.pb=dev(z,self.xb,c,self.yb)
+    def slot(self,zz,xx,cc,yy):
+        n=self.src.shape[0]
+        return self.dst.at[yy,pl.ds(pl.multiple_of(((zz*2+xx)*2+cc)*n,n),n)]
+    def copy(self,src,where,k,to):
+        return send(src,self.slot(*where),self.ss.at[k],self.rs.at[k],to)
+    def go(self,where,k,to,src=None):
+        self.copy(self.slot(*where) if src is None else src,where,k,to).start()
+    def came(self,where,k):
+        self.copy(self.src,where,k,self.sib).wait_recv()
+    def keep(self):
+        z,x,c,y=self.at
+        return pltpu.make_async_copy(self.src,self.slot(z,x,c,y),self.own)
+    def start(self):
+        z,x,c,y=self.at
+        me=(z,x,c,y)
+        self.keep().start()
+        for i in (1,2,3):
+            self.go(me,i-1,dev((z+i)%4,x,c,y),self.src)
+        self.go(me,3,self.pa,self.src); self.go(me,7,self.pb,self.src); self.go(me,15,self.sib,self.src)
+    def z(self,i):
+        return (self.at[0]+4-i)%4
+    def turn_z(self,i):
+        z,x,c,y=self.at
+        at=(self.z(i),x,c,y); self.came(at,i-1)
+        self.go(at,3+i,self.pa); self.go(at,7+i,self.pb); self.go(at,15+i,self.sib)
+    def turn_a(self,i):
+        at=(self.z(i),self.xa,self.at[2],self.ya); self.came(at,3+i)
+        self.go(at,11+i,self.pb); self.go(at,19+i,self.sib)
+    def turn_b(self,i):
+        at=(self.z(i),self.xb,self.at[2],self.yb); self.came(at,7+i)
+        self.go(at,23+i,self.sib)
+    def turn_ab(self,i):
+        z,x,c,y=self.at
+        at=(self.z(i),1-x,c,1-y); self.came(at,11+i)
+        self.go(at,27+i,self.sib)
+    def last(self):
+        z,x,c,y=self.at
+        for i in range(4):
+            zz=self.z(i)
+            self.came((zz,x,1-c,y),15+i); self.came((zz,self.xb,1-c,self.yb),19+i)
+            self.came((zz,self.xa,1-c,self.ya),23+i); self.came((zz,1-x,1-c,1-y),27+i)
+    def drain(self):
+        z,x,c,y=self.at
+        for k in range(31):
+            self.copy(self.src,(z,x,c,y),k,self.sib).wait_send()
+        self.keep().wait()
+
+def gather_sems():
+    return [pltpu.SemaphoreType.DMA((31,)),pltpu.SemaphoreType.DMA((31,)),pltpu.SemaphoreType.DMA]
+
+STEPS=7
+def kernel_w(w_hbm,pos_ref,tab_ref,W_hbm,bias_hbm,bias_s,tb,tq,ss,rs,own,bs,br,bl,tsem):
     z,x,c,y=place_of()
     greet(peers_of(z,x,c,y))
-    npair,n=tab_ref.shape[1],tab_ref.shape[2]
-    half=2*npair
+    gather=Gather(w_hbm,W_hbm,ss,rs,own)
+    swap=send(tab_ref,tb.at[y],tsem.at[0],tsem.at[1],dev(z,x,c,1-y))
+    swap.start()
+    gather.start()
+    tb[y]=tab_ref[...]
+    swap.wait()
+    half,n=tab_ref.shape[0],tab_ref.shape[1]
+    npair=half//2
+    for p in range(npair):
+        a,b=[jnp.floor(jnp.clip(tb[c,2*p+k],-4.0,4.0)*FIX+0.5).astype(jnp.int32) for k in range(2)]
+        tq[p]=(a*65536)|(b&65535)
     WIN=bias_s.shape[-1]; tiles=-(-WIN//128)
-    xa=x+(1-2*x)*(1-c); ya=y+(1-2*y)*c
-    xb=x+(1-2*x)*c; yb=y+(1-2*y)*(1-c)
-    sib=dev(z,x,1-c,y); pa=dev(z,xa,c,ya); pb=dev(z,xb,c,yb)
-    started=[]
-    def go(src,zz,xx,yy,k,to):
-        cp=send(src,W_hbm.at[yy,zz,xx,c],ss.at[k],rs.at[k],to); cp.start(); started.append(cp)
-    def came(zz,xx,cc,yy,k):
-        send(w_ref,W_hbm.at[yy,zz,xx,cc],ss.at[k],rs.at[k],sib).wait_recv()
-    mine=pltpu.make_async_copy(w_ref,W_hbm.at[y,z,x,c],own); mine.start()
-    for i in (1,2,3):
-        go(w_ref,z,x,y,i-1,dev((z+i)%4,x,c,y))
-    go(w_ref,z,x,y,3,pa); go(w_ref,z,x,y,7,pb); go(w_ref,z,x,y,15,sib)
-    def zof(i): return (z+4-i)%4
-    def turn_z(i):
-        zz=zof(i); came(zz,x,c,y,i-1)
-        blk=W_hbm.at[y,zz,x,c]
-        go(blk,zz,x,y,3+i,pa); go(blk,zz,x,y,7+i,pb); go(blk,zz,x,y,15+i,sib)
-    def turn_a(i):
-        zz=zof(i); came(zz,xa,c,ya,3+i)
-        blk=W_hbm.at[ya,zz,xa,c]
-        go(blk,zz,xa,ya,11+i,pb); go(blk,zz,xa,ya,19+i,sib)
-    def turn_b(i):
-        zz=zof(i); came(zz,xb,c,yb,7+i)
-        go(W_hbm.at[yb,zz,xb,c],zz,xb,yb,23+i,sib)
-    def turn_ab(i):
-        zz=zof(i); came(zz,1-x,c,1-y,11+i)
-        go(W_hbm.at[1-y,zz,1-x,c],zz,1-x,1-y,27+i,sib)
     nrow=WIN//8
-    steps=7
-    cuts=[nrow*k//steps for k in range(steps+1)]
-    sends=[]
+    cuts=[nrow*k//STEPS for k in range(STEPS+1)]
+    sib=dev(z,x,1-c,y)
+    def rows_of(k): return pl.ds(cuts[k]*8,(cuts[k+1]-cuts[k])*8)
+    def kept(k): return pltpu.make_async_copy(bias_s.at[:,rows_of(k)],bias_hbm.at[pl.ds(c*half,half),rows_of(k)],bl.at[k])
+    def sent(k,cc): return send(bias_s.at[:,rows_of(k)],bias_hbm.at[pl.ds(cc*half,half),rows_of(k)],bs.at[k],br.at[k],sib)
     def rows(k):
         def row(r,_):
             r8=pl.multiple_of(r*8,8)
@@ -406,7 +419,7 @@
                 for p in range(npair):
                     acc=jnp.zeros((8,128),jnp.int32)
                     for q in range(n):
-                        src=jnp.broadcast_to(tab_ref[c,p,q:q+1,:],(8,128))
+                        src=jnp.broadcast_to(tq[p,q:q+1,:],(8,128))
                         acc=jnp.where(masks[q],jnp.take_along_axis(src,lo,axis=1),acc)
                     a=(acc>>16).astype(F32)*(SQ/FIX)
                     b=((acc<<16)>>16).astype(F32)*(SQ/FIX)
@@ -414,59 +427,251 @@
                     bias_s[2*p+1,pl.ds(r8,8),t*128:t*128+width]=b[:,:width]
             return 0
         lax.fori_loop(cuts[k],cuts[k+1],row,0)
-        rr=pl.ds(cuts[k]*8,(cuts[k+1]-cuts[k])*8)
-        cp=pltpu.make_async_copy(bias_s.at[:,rr],bias_hbm.at[pl.ds(c*half,half),rr],bl.at[k]); cp.start()
-        rc=send(bias_s.at[:,rr],bias_hbm.at[pl.ds(c*half,half),rr],bs.at[k],br.at[k],sib); rc.start()
-        sends.append((cp,rc))
+        kept(k).start(); sent(k,c).start()
     rows(0)
-    turn_z(1); turn_z(3)
+    for i in (1,3,2): gather.turn_z(i)
     rows(1)
-    turn_z(2); turn_a(0); turn_b(0)
+    for i in (0,): gather.turn_a(i); gather.turn_b(i)
     rows(2)
-    for i in (1,3): turn_a(i); turn_b(i)
+    for i in (1,3): gather.turn_a(i); gather.turn_b(i)
     rows(3)
-    for i in (2,): turn_a(i); turn_b(i)
-    turn_ab(0)
+    for i in (2,): gather.turn_a(i); gather.turn_b(i)
+    gather.turn_ab(0)
     rows(4)
-    for i in (1,3): turn_ab(i)
+    for i in (1,3): gather.turn_ab(i)
     rows(5)
-    turn_ab(2)
+    gather.turn_ab(2)
     rows(6)
-    for i in range(4):
-        zz=zof(i)
-        came(zz,x,1-c,y,15+i); came(zz,xb,1-c,yb,19+i); came(zz,xa,1-c,ya,23+i); came(zz,1-x,1-c,1-y,27+i)
-    for k in range(steps):
-        rr=pl.ds(cuts[k]*8,(cuts[k+1]-cuts[k])*8)
-        sends[k][0].wait(); sends[k][1].wait_send()
-        send(bias_s.at[:,rr],bias_hbm.at[pl.ds((1-c)*half,half),rr],bs.at[k],br.at[k],sib).wait_recv()
-    for cp in started: cp.wait_send()
-    mine.wait()
-
-def call_w(wcat,posT_pad,tab,WIN):
-    rows,cols=wcat.shape; npair=tab.shape[1]
+    gather.last()
+    for k in range(STEPS):
+        kept(k).wait(); sent(k,c).wait_send(); sent(k,1-c).wait_recv()
+    gather.drain()
+
+def call_w(wq,posT_pad,tab,WIN):
+    rows,cols=wq.shape; half=tab.shape[0]; dma=pltpu.SemaphoreType.DMA
+    vm=pl.BlockSpec(memory_space=pltpu.VMEM)
     return pl.pallas_call(kernel_w,
-      out_shape=[jax.ShapeDtypeStruct((2,4,2,2,rows,cols),BF),jax.ShapeDtypeStruct((4*npair,WIN,WIN),F32)],
-      in_specs=[pl.BlockSpec(memory_space=pl.ANY),pl.BlockSpec(memory_space=pltpu.VMEM),pl.BlockSpec(memory_space=pltpu.VMEM)],
-      out_specs=[pl.BlockSpec(memory_space=pl.ANY)]*2,
-      scratch_shapes=[pltpu.VMEM((2*npair,WIN,WIN),F32),pltpu.SemaphoreType.DMA((31,)),pltpu.SemaphoreType.DMA((31,)),
-        pltpu.SemaphoreType.DMA((7,)),pltpu.SemaphoreType.DMA((7,)),pltpu.SemaphoreType.DMA((7,)),pltpu.SemaphoreType.DMA],
-      compiler_params=pltpu.CompilerParams(vmem_limit_bytes=40*1024*1024,collective_id=1,has_side_effects=True),name="kernel_w")(wcat,posT_pad,tab)
+      out_shape=[jax.ShapeDtypeStruct((2,16*rows,cols),BF),jax.ShapeDtypeStruct((2*half,WIN,WIN),F32)],
+      in_specs=[ANY,vm,vm],out_specs=[ANY]*2,
+      scratch_shapes=[pltpu.VMEM((half,WIN,WIN),F32),pltpu.VMEM((2,)+tab.shape,F32),pltpu.VMEM((half//2,)+tab.shape[1:],jnp.int32)]
+        +gather_sems()+[dma((STEPS,)),dma((STEPS,)),dma((STEPS,)),dma((2,))],
+      compiler_params=pltpu.CompilerParams(vmem_limit_bytes=40*1024*1024,collective_id=1,has_side_effects=True),name="kernel_w")(wq,posT_pad,tab)
+
+def neighbours(z,x,c,y):
+    s=(z*2+x)*2+c
+    return [((s+k)%16,yy) for k in (1,15) for yy in (y,1-y)]
+
+def kernel_a2(nheads,in_hbm,og_hbm,wf_hbm,labc_ref,labr_ref,bias_ref,W1,gains_ref,shifts_ref,
+              qkv_ref,x_ref,P_hbm,gln2_ref,g_ref,gT_ref,D_ref,ev_hbm,hd_hbm,dcat_hbm,small_ref,
+              x_s,og_s,W2,OT_s,qT_s,vT_s,P_s,acc,pst,xn2_s,xn2T_s,tg_s,tgT_s,up_s,gn2_s,dl_s,
+              psem,xsem,hsem,ss,rs,own,dl,ds,dr,es,er,fin):
+    i=pl.program_id(0); nw=x_s.shape[0]
+    w=i%nw
+    z,xc,c,y=place_of()
+    s=(z*2+xc)*2+c
+    D=x_s.shape[-1]; WIN=qkv_ref.shape[-2]; SLAB=x_s.shape[1]; HALF=SLAB//2
+    OFF=(SLAB-WIN)//2
+    cq=D//2; cf=W2.shape[2]//2
+    groups=nheads//PER
+    gather=Gather(wf_hbm,W2,ss,rs,own)
+    mate=dev(z,xc,c,1-y)
+    def local(k,half,t):
+        hbm,buf=((in_hbm,x_s),(og_hbm,og_s))[t]
+        r=pl.multiple_of(y*(nw*WIN)+k*WIN+(WIN//2-OFF)+half*HALF,8)
+        return pltpu.make_async_copy(hbm.at[pl.ds(r,HALF)],buf.at[k,pl.ds(half*HALF,HALF)],xsem.at[t,2*k+half])
+    def edge(t):
+        hbm,buf=((in_hbm,x_s),(og_hbm,og_s))[t]
+        return send(hbm.at[pl.ds(0,HALF)],buf.at[nw-1,pl.ds(HALF,HALF)],hsem.at[t,0],hsem.at[t,1],((s+15)%16,1))
+    def ready(t):
+        local(w,0,t).wait()
+        far=jnp.logical_and(w==nw-1,y==1)
+        @pl.when(far)
+        def _(): edge(t).wait_recv()
+        @pl.when(jnp.logical_not(far))
+        def _(): local(w,1,t).wait()
+    def slab(k,to=None):
+        at=ev_hbm.at[y*nw+k]
+        if to is None: return pltpu.make_async_copy(dl_s.at[k],at,dl.at[k])
+        return send(dl_s.at[k],at,ds.at[k],dr.at[k],to)
+    def tail(k):
+        lead=SLAB-hd_hbm.shape[0]
+        return send(dl_s.at[nw-1,pl.ds(lead,hd_hbm.shape[0])],hd_hbm,es.at[k],er,((s+1)%16,k))
+    @pl.when(i==0)
+    def _():
+        greet(peers_of(z,xc,c,y)+neighbours(z,xc,c,y))
+        for k in range(nw):
+            for t in range(2):
+                local(k,0,t).start()
+                if k<nw-1: local(k,1,t).start()
+        for t in range(2):
+            @pl.when(y==1)
+            def _(): edge(t).start()
+            @pl.when(y==0)
+            def _(): local(nw-1,1,t).start()
+        gather.start()
+        acc[...]=jnp.zeros_like(acc)
+        small_ref[...]=jnp.zeros_like(small_ref)
+        dl_s[:,SLAB-16:,:]=jnp.zeros((nw,16,D),BF)
+
+    @pl.when(i<nw)
+    def _():
+        ready(0)
+        x=x_s[w,OFF:OFF+WIN,:]
+        x_ref[0]=x
+        xhat,_=norm_stats(x)
+        xn=(xhat*gains_ref[0:1,:]+shifts_ref[0:1,:]).astype(BF)
+        for k in range(3):
+            for m in range(2):
+                at=slice(m*cq,(m+1)*cq)
+                v=mm(xn,W1[m,:,k*cq:(k+1)*cq]).astype(BF)
+                qkv_ref[0,k,:,at]=v
+                if k==0: qT_s[at,:]=v.T
+                if k==2: vT_s[at,:]=v.T
+        labc=labc_ref[0]; labr=labr_ref[0]
+        lane=lax.broadcasted_iota(jnp.int32,(WIN,GROUP),1)
+        oh=jnp.where((labc==lane)|((labc+3)==lane),1.0,0.0).astype(BF)
+        hi=564.0
+        lo=MASK-hi
+        sub=lax.broadcasted_iota(jnp.int32,(GROUP,WIN),0)
+        nm=jnp.where(sub<3,jnp.where(sub!=labr,-hi,0.0),jnp.where(sub<6,jnp.where(sub-3!=labr,-lo,0.0),0.0)).astype(BF)
+        hl=lane//HD
+        def group(gi,_):
+            slot=gi%2
+            @pl.when(w*groups+gi>=2)
+            def _():
+                pltpu.make_async_copy(P_s.at[slot],P_hbm.at[0,pl.ds(0,PER)],psem.at[slot]).wait()
+            o=pl.multiple_of(gi*GROUP,GROUP)
+            qTg=jnp.concatenate([qT_s[pl.ds(o,GROUP),:],nm],axis=0)
+            kg=qkv_ref[0,1,:,pl.ds(o,GROUP)]
+            for hh in range(PER):
+                kh=jnp.concatenate([jnp.where(hl==hh,kg,jnp.zeros_like(kg)),oh],axis=1)
+                t=mm(kh,qTg)+bias_ref[gi*PER+hh]
+                m=jnp.max(t,axis=0,keepdims=True)
+                e=jnp.exp2((t-m)*CEXP)
+                l=jnp.sum(e,axis=0,keepdims=True)
+                p=(e*(1.0/l)).astype(BF)
+                P_s[slot,hh]=p
+                OT_s[w,pl.ds(o+hh*HD,HD),:]=mm(vT_s[pl.ds(o+hh*HD,HD),:],p)
+            pltpu.make_async_copy(P_s.at[slot],P_hbm.at[w,pl.ds(gi*PER,PER)],psem.at[slot]).start()
+            return 0
+        lax.fori_loop(0,groups,group,0)
+
+    @pl.when(i==0)
+    def _():
+        for k in (1,3,2): gather.turn_z(k)
+    @pl.when(i==1)
+    def _():
+        for k in (0,1,3,2): gather.turn_a(k); gather.turn_b(k)
+    @pl.when(i==2)
+    def _():
+        for k in (0,1,3,2): gather.turn_ab(k)
+    @pl.when(i==nw-1)
+    def _():
+        gather.last(); gather.drain()
+
+    @pl.when(i>=nw)
+    def _():
+        ready(1)
+        x=x_s[w,OFF:OFF+WIN,:]
+        og=og_s[w,OFF:OFF+WIN,:]
+        attn=OT_s[w].astype(BF).T
+        branch=shifts_ref[2:3,:]
+        for m in range(2):
+            branch=branch+mm_nt(attn[:,m*cq:(m+1)*cq],W1[m,:,3*cq:4*cq])
+        branch=branch.astype(BF).astype(F32)
+        middle=x+branch
+        xhat2,rstd2=norm_stats(middle)
+        xn2=(xhat2*gains_ref[1:2,:]+shifts_ref[1:2,:]).astype(BF)
+        tg=og.astype(BF)
+        xn2_s[...]=xn2; xn2T_s[...]=xn2.T; tg_s[...]=tg; tgT_s[...]=tg.T
+        up_s[...]=jnp.zeros_like(up_s); gn2_s[...]=jnp.zeros_like(gn2_s)
+        CH=512; each=cf//CH
+        def chunk(k,_):
+            m=k//each
+            o=pl.multiple_of((k%each)*CH,CH)
+            f1=W2[m,:,pl.ds(o,CH)]; f2=W2[m,:,pl.ds(cf+o,CH)]
+            hid=mm(xn2_s[...],f1)
+            act,dact=gelu_both(hid)
+            a=act.astype(BF)
+            up_s[...]+=mm_nt(a,f2)
+            gh=(mm(tg_s[...],f2)*dact).astype(BF)
+            gn2_s[...]+=mm_nt(gh,f1)
+            acc[m,:,pl.ds(cq+o,CH)]+=mm(xn2T_s[...],gh)
+            acc[m,:,pl.ds(cq+cf+o,CH)]+=mm(tgT_s[...],a)
+            return 0
+        lax.fori_loop(0,2*each,chunk,0)
+        dl_s[w,0:WIN,:]=(branch+up_s[...]+shifts_ref[3:4,:]).astype(BF)
+        slab(w).start(); slab(w,mate).start()
+        @pl.when(jnp.logical_and(w==nw-1,y==1))
+        def _():
+            tail(0).start(); tail(1).start()
+        gn2=gn2_s[...]
+        gln2=norm_back(gn2,xhat2,rstd2,gains_ref[1:2,:])
+        gln2_ref[0]=gln2
+        gb=(og+gln2).astype(BF)
+        gbT=gb.T
+        for m in range(2):
+            at=slice(m*cq,(m+1)*cq)
+            acc[m,:,0:cq]+=mm(gbT,attn[:,at])
+            g=mm(gb,W1[m,:,3*cq:4*cq]).astype(BF)
+            g_ref[0,:,at]=g
+            gT=g.T
+            gT_ref[0,at,:]=gT
+            prod=gT.astype(F32)*OT_s[w,at,:]
+            nh=nheads//2
+            D_ref[0,m*nh:(m+1)*nh,:]=jnp.sum(prod.reshape(nh,HD,WIN),axis=1)
+        small_ref[1:2,:]+=jnp.sum(gn2*xhat2,axis=0,keepdims=True)
+        small_ref[3:4,:]+=jnp.sum(gn2,axis=0,keepdims=True)
+        small_ref[4:5,:]+=jnp.sum(gb.astype(F32),axis=0,keepdims=True)
+        small_ref[5:6,:]+=jnp.sum(tg.astype(F32),axis=0,keepdims=True)
+
+    @pl.when(i==2*nw-1)
+    def _():
+        W2[...]=acc[:,:,cq:].astype(BF)
+        pst[...]=acc[:,:,:cq].astype(BF)
+        a=pltpu.make_async_copy(W2,dcat_hbm.at[:,:,pl.ds(cq,2*cf)],fin.at[0])
+        b=pltpu.make_async_copy(pst,dcat_hbm.at[:,:,pl.ds(0,cq)],fin.at[1])
+        a.start(); b.start()
+        for k in range(2):
+            pltpu.make_async_copy(P_s.at[k],P_hbm.at[0,pl.ds(0,PER)],psem.at[k]).wait()
+        for k in range(nw):
+            slab(k).wait(); slab(k,mate).wait()
+        @pl.when(y==1)
+        def _():
+            for t in range(2): edge(t).wait_send()
+            tail(0).wait_send(); tail(1).wait_send()
+        tail(0).wait_recv()
+        a.wait(); b.wait()
+
+def call_a2(inputs,og,wf,labc,labr,bias,W1,gains,shifts):
+    nW=labc.shape[0]; WIN=labc.shape[1]; D=inputs.shape[1]; NH=bias.shape[0]
+    cf=wf.shape[1]//2; cq=D//2; SLAB=-(-WIN//16)*16; EDGE=-(-(SLAB-WIN//2)//16)*16
+    sd=jax.ShapeDtypeStruct; dma=pltpu.SemaphoreType.DMA; v=pltpu.VMEM
+    early=lambda shape: pl.BlockSpec((1,)+shape,lambda i:(jnp.minimum(i,nW-1),)+(0,)*len(shape))
+    late=lambda shape: pl.BlockSpec((1,)+shape,lambda i:(jnp.maximum(i-nW,0),)+(0,)*len(shape))
+    outs=[sd((nW,3,WIN,D),BF),sd((nW,WIN,D),F32),sd((nW,NH,WIN,WIN),BF),sd((nW,WIN,D),F32),sd((nW,WIN,D),BF),sd((nW,D,WIN),BF),sd((nW,NH,WIN),F32),
+          sd((2*nW,SLAB,D),BF),sd((EDGE,D),BF),sd((2,D,cq+2*cf),BF),sd((8,D),F32)]
+    return pl.pallas_call(functools.partial(kernel_a2,NH),grid=(2*nW,),
+      in_specs=[ANY,ANY,ANY,early((WIN,1)),early((1,WIN)),full((NH,WIN,WIN),pipeline_mode=ONE),full(W1.shape,pipeline_mode=ONE),full(gains.shape),full(shifts.shape)],
+      out_specs=[early((3,WIN,D)),early((WIN,D)),ANY,late((WIN,D)),late((WIN,D)),late((D,WIN)),late((NH,WIN)),ANY,ANY,ANY,full((8,D))],
+      out_shape=outs,
+      scratch_shapes=[v((nW,SLAB,D),F32),v((nW,SLAB,D),F32),v((2,D,2*cf),BF),v((nW,D,WIN),F32),v((D,WIN),BF),v((D,WIN),BF),v((2,PER,WIN,WIN),BF),
+        v((2,D,cq+2*cf),F32),v((2,D,cq),BF),v((WIN,D),BF),v((D,WIN),BF),v((WIN,D),BF),v((D,WIN),BF),v((WIN,D),F32),v((WIN,D),F32),v((nW,SLAB,D),BF),
+        dma((2,)),dma((2,2*nW)),dma((2,2))]+gather_sems()+[dma((nW,)),dma((nW,)),dma((nW,)),dma((2,)),dma,dma((2,))],
+      compiler_params=pltpu.CompilerParams(vmem_limit_bytes=63*1024*1024,dimension_semantics=("arbitrary",),collective_id=2,has_side_effects=True),
+      name="kernel_a2")(inputs,og,wf,labc,labr,bias,W1,gains,shifts)
 
 class Reduce:
-    def __init__(self,src,out,own,r1,r2,ss,rs,ls,r3=None,fin=None,r4=None,mid=None):
+    def __init__(self,src,out,own,r1,r2,ss,rs,ls,r3,fin,r4):
         self.src,self.out,self.own,self.r1,self.r2,self.r3,self.fin,self.r4=src,out,own,r1,r2,r3,fin,r4
         self.ss,self.rs,self.ls=ss,rs,ls
         self.at=place_of()
-        self.mid=own.at[self.at[1]] if mid is None else mid
-        self.whole=mid is None
-    def pairs(self):
-        z,x,c,y=self.at
-        k=0
-        for xx in range(2):
-            for yy in range(2):
-                yield (pltpu.make_async_copy(self.src.at[yy,:,xx,c],self.own.at[xx,:,yy],self.ls.at[k]),
-                       send(self.src.at[yy,:,xx,1-c],self.r1.at[xx,:,yy],self.ss.at[k],self.rs.at[k],dev(z,x,1-c,y)))
-                k+=1
+        self.mid=own.at[self.at[1]]
+    def mine(self,k):
+        return pltpu.make_async_copy(self.src.at[k%2,:,k//2,self.at[2]],self.own.at[k//2,:,k%2],self.ls.at[k])
+    def theirs(self,k):
+        z,x,c,y=self.at
+        return send(self.src.at[k%2,:,k//2,1-c],self.r1.at[k//2,:,k%2],self.ss.at[k],self.rs.at[k],dev(z,x,1-c,y))
     def xsend(self):
         z,x,c,y=self.at
         return send(self.own.at[1-x],self.r2,self.ss.at[4],self.rs.at[4],dev(z,1-x,c,y))
@@ -478,16 +683,16 @@
         z,x,c,y=self.at
         return send(self.fin.at[1-y],self.r4,self.ss.at[8],self.rs.at[8],dev(z,x,c,1-y))
     def start(self):
-        for a,b in self.pairs():
-            a.start(); b.start()
+        for k in range(4):
+            self.theirs(k).start(); self.mine(k).start()
     def add(self,dst,*srcs):
         total=srcs[0][...].astype(F32)
         for s in srcs[1:]: total=total+s[...].astype(F32)
         dst[...]=total.astype(BF)
     def one(self):
         z,x,c,y=self.at
-        for a,b in self.pairs():
-            a.wait(); b.wait_recv()
+        for k in range(4):
+            self.mine(k).wait(); self.theirs(k).wait_recv()
         def step(xx):
             def add(k,_):
                 at=(xx,k//2,k%2)
@@ -504,13 +709,8 @@
             self.add(self.own.at[(x,)+at],self.own.at[(x,)+at],self.r2.at[at])
             return 0
         lax.fori_loop(0,8,add,0)
-    def half(self,hbm,sem):
-        self.xsend().wait_recv()
-        self.summed()
-        cp=pltpu.make_async_copy(self.mid,hbm,sem); cp.start(); cp.wait()
-        self.left()
     def left(self):
-        for a,b in self.pairs(): b.wait_send()
+        for k in range(4): self.theirs(k).wait_send()
         self.xsend().wait_send()
     def zstart(self):
         for i in (2,1,3): self.zsend(i).start()
@@ -531,80 +731,185 @@
         z,x,c,y=self.at
         self.ysend().wait_recv()
         self.out[...]=self.fin[y].astype(F32)+self.r4[...].astype(F32)
-        if self.whole: self.left()
+        self.left()
         for i in (1,2,3): self.zsend(i).wait_send()
         self.ysend().wait_send()
 
-def reduce_scratch(rows,cols,last=True,first=True):
-    v=lambda *d: pltpu.VMEM(d+(rows,cols),BF)
-    return ((([v(2,4,2),v(2,4,2),v(4,2)]) if first else [])+[pltpu.SemaphoreType.DMA((9,)),pltpu.SemaphoreType.DMA((9,)),pltpu.SemaphoreType.DMA((4,))]
-            +([v(3,2),v(2),v()] if last else []))
-
-def kernel_c(NH,G_ref,hi_ref,lo_ref,small_ref,dq_hbm,mid_ref,redq_ref,redm_ref,tab_ref,sum_ref,acc,tk,tr,sr,ts,tq,own,r1,r2,ss,rs,ls,r3,fin,r4,ss2,rs2,ls2,s3,sfin,s4):
-    WIN=hi_ref.shape[0]; LW=G_ref.shape[0]*128
-    nh=acc.shape[0]
-    z,x,c,y=place_of()
-    greet(peers_of(z,x,c,y))
-    red=Reduce(dq_hbm,redq_ref,own,r1,r2,ss,rs,ls,r3,fin,r4)
-    big=Reduce(None,redm_ref,None,None,None,ss2,rs2,ls2,s3,sfin,s4,mid=mid_ref)
-    red.start(); big.zstart()
-    acc[...]=jnp.zeros_like(acc)
-    def rows(r,_):
-        r8=pl.multiple_of(r*8,8)
-        hi8=hi_ref[pl.ds(r8,8),:]; lo8=lo_ref[pl.ds(r8,8),:]
-        tot=jnp.zeros((nh*NH,256),F32)
-        iota=lax.broadcasted_iota(jnp.int32,(256,LW),0).astype(F32).astype(BF)
-        for k in range(8):
-            g=jnp.concatenate([G_ref[q,pl.ds(r8+k,NH,stride=WIN),:] for q in range(LW//128)],axis=1)
-            hr=hi8[k:k+1,:]; lr=lo8[k:k+1,:].astype(F32).astype(BF)
-            A=jnp.concatenate([jnp.where(hr==m,g,0.0) for m in range(nh)],axis=0).astype(BF)
-            oh=jnp.where(iota==lr,jnp.ones((),BF),jnp.zeros((),BF))
-            tot=tot+mm_nt(A,oh)
-        acc[...]+=tot.reshape(acc.shape)
+def reduce_scratch(rows,cols):
+    v=lambda *d: pltpu.VMEM(d+(rows,cols),BF); dma=pltpu.SemaphoreType.DMA
+    return [v(2,4,2),v(2,4,2),v(4,2),dma((9,)),dma((9,)),dma((4,)),v(3,2),v(2),v()]
+
+
+def kernel_bc(nheads,x_ref,gln2_ref,qkv_ref,g_ref,gT_ref,D_ref,P_ref,W1,gains_ref,shifts_ref,sm_ref,pos_ref,dcat_hbm,
+              ev_hbm,hd_hbm,redq_ref,redm_ref,tab_ref,sum_ref,
+              G_s,Gx,aq,dq_s,kT_s,gq_s,gqT_s,dd_s,small_ref,acc,tk,tr,tu,sr,
+              gs,gr_,dl,ds,dr,es,er,ts,tq_,
+              own,r1,r2,ss,rs,ls,r3,fin,r4,own2,p1,p2,ss2,rs2,ls2,p3,fin2,p4):
+    w=pl.program_id(0); nw=dd_s.shape[0]
+    z,xc,c,y=place_of()
+    s=(z*2+xc)*2+c
+    mate=dev(z,xc,c,1-y); sib=dev(z,xc,1-c,y)
+    D=x_ref.shape[-1]; WIN=x_ref.shape[-2]; SLAB=dd_s.shape[1]
+    cq=D//2
+    groups=nheads//PER
+    tiles=G_s.shape[0]; part=Gx.shape[1]//nheads
+    big=Reduce(dcat_hbm,redm_ref,own2,p1,p2,ss2,rs2,ls2,p3,fin2,p4)
+    red=Reduce(dq_s,redq_ref,own,r1,r2,ss,rs,ls,r3,fin,r4)
+    def slab(k,to=None):
+        at=ev_hbm.at[y*nw+k]
+        if to is None: return pltpu.make_async_copy(dd_s.at[k],at,dl.at[k])
+        return send(dd_s.at[k],at,ds.at[k],dr.at[k],to)
+    def tail(k):
+        lead=SLAB-hd_hbm.shape[0]
+        return send(dd_s.at[nw-1,pl.ds(lead,hd_hbm.shape[0])],hd_hbm,es.at[k],er,((s+1)%16,k))
+    def trade(h):
+        r=pl.multiple_of(h*WIN+(1-c)*(WIN-part),8)
+        return send(G_s.at[:,pl.ds(r,part)],Gx.at[:,pl.ds(pl.multiple_of(h*part,8),part)],gs.at[h],gr_.at[h],sib)
+    @pl.when(w==0)
+    def _():
+        greet(peers_of(z,xc,c,y)+neighbours(z,xc,c,y))
+        big.start()
+        aq[...]=jnp.zeros_like(aq); G_s[...]=jnp.zeros_like(G_s); small_ref[...]=sm_ref[...]
+        dd_s[:,SLAB-16:,:]=jnp.zeros((nw,16,D),BF)
+    kT_s[...]=qkv_ref[0,1].T
+    lane=lax.broadcasted_iota(jnp.int32,(WIN,GROUP),1)
+    hl=lane//HD
+    def group(gi,_):
+        o=pl.multiple_of(gi*GROUP,GROUP)
+        gTg=gT_ref[0,pl.ds(o,GROUP),:]
+        vg=qkv_ref[0,2,:,pl.ds(o,GROUP)]
+        qg=qkv_ref[0,0,:,pl.ds(o,GROUP)]
+        gg=g_ref[0,:,pl.ds(o,GROUP)]
+        dv=jnp.zeros((WIN,GROUP),F32); dk=jnp.zeros((WIN,GROUP),F32)
+        zero=jnp.zeros_like(vg)
+        for hh in range(PER):
+            h=gi*PER+hh
+            p=P_ref[0,h]
+            dp=mm(jnp.where(hl==hh,vg,zero),gTg)
+            dsc=p.astype(F32)*(dp-D_ref[0,pl.ds(h,1),:])
+            for k in range(tiles):
+                wd=min(128,WIN-k*128)
+                G_s[k,pl.ds(pl.multiple_of(h*WIN,8),WIN),:wd]+=dsc[:,k*128:k*128+wd]
+            dsl=dsc.astype(BF)
+            dv+=mm(p,jnp.where(hl==hh,gg,zero))
+            dk+=mm(dsl,jnp.where(hl==hh,qg,zero))
+            gqT_s[pl.ds(o+hh*HD,HD),:]=mm(kT_s[pl.ds(o+hh*HD,HD),:],dsl)
+        gq_s[1,:,pl.ds(o,GROUP)]=(dk*(1.0/SQ)).astype(BF)
+        gq_s[2,:,pl.ds(o,GROUP)]=dv.astype(BF)
+        @pl.when(w==nw-1)
+        def _():
+            for hh in range(PER): trade(gi*PER+hh).start()
         return 0
-    n=WIN//8
-    cuts=[0,n*6//49,n*20//49,n*36//49,n*44//49,n]
-    for k,f in enumerate((red.one,red.two,big.three,red.three,big.four)):
-        lax.fori_loop(cuts[k],cuts[k+1],rows,0)
-        f()
-    red.four()
-    half=NH//2
-    cps=(send(acc.at[:,pl.ds((1-y)*half,half)],tr.at[0],ts.at[0],tq.at[0],dev(z,x,c,1-y)),send(small_ref,sr.at[0],ts.at[1],tq.at[1],dev(z,x,c,1-y)))
-    for p in cps: p.start()
-    for p in cps: p.wait()
-    tk[0]=acc[:,pl.ds(pl.multiple_of(y*half,8),half)]+tr[0]
-    small=small_ref[...]+sr[0]
-    for k,to in ((1,dev(z,x,1-c,y)),(2,dev(z,1-x,c,y))):
-        sr[6+k]=small
-        cps=(send(tk.at[k-1],tr.at[k],ts.at[2*k],tq.at[2*k],to),send(sr.at[6+k],sr.at[k],ts.at[2*k+1],tq.at[2*k+1],to))
-        for p in cps: p.start()
-        for p in cps: p.wait()
-        tk[k]=tk[k-1]+tr[k]
-        small=small+sr[k]
-    sr[9]=small
-    cps=[]
-    for i in (1,2,3):
-        to=dev((z+i)%4,x,c,y); k=2+i
-        cps+=[send(tk.at[2],tr.at[k],ts.at[2*k],tq.at[2*k],to),send(sr.at[9],sr.at[k],ts.at[2*k+1],tq.at[2*k+1],to)]
-    for p in cps: p.start()
-    for p in cps: p.wait()
-    tab_ref[...]=tk[2]+tr[3]+tr[4]+tr[5]
-    sum_ref[...]=small+sr[3]+sr[4]+sr[5]
-
-def call_c(G,posT,T,NH,small,dq,mid):
-    WIN=posT.shape[0]; nt=G.shape[0]
-    nh=-(-T//256)
-    rows,cols=dq.shape[-2:]; more=mid.shape[-1]
-    pp=jnp.pad(posT,((0,0),(0,nt*128-WIN)),constant_values=nh*256)
-    hi=pp>>8; lo=pp&255
-    vm=pl.BlockSpec(memory_space=pltpu.VMEM)
-    redq,redm,tab,sm=pl.pallas_call(functools.partial(kernel_c,NH),
-      out_shape=[jax.ShapeDtypeStruct((rows,cols),F32),jax.ShapeDtypeStruct((rows,more),F32),jax.ShapeDtypeStruct((nh,NH//2,256),F32),jax.ShapeDtypeStruct(small.shape,F32)],
-      in_specs=[vm,vm,vm,vm,ANY,vm],out_specs=[vm]*4,
-      scratch_shapes=[pltpu.VMEM((nh,NH,256),F32)]+[pltpu.VMEM((3,nh,NH//2,256),F32),pltpu.VMEM((6,nh,NH//2,256),F32),
-        pltpu.VMEM((10,)+small.shape,F32),pltpu.SemaphoreType.DMA((12,)),pltpu.SemaphoreType.DMA((12,))]+reduce_scratch(rows,cols)+reduce_scratch(rows,more,True,False),
-      compiler_params=pltpu.CompilerParams(vmem_limit_bytes=60*1024*1024,collective_id=3,has_side_effects=True),name="kernel_c")(G,hi,lo,small,dq,mid)
-    return redq,redm,tab.transpose(1,0,2).reshape(NH//2,nh*256)[:,:T],sm
+    lax.fori_loop(0,groups,group,0)
+    gq_s[0]=(gqT_s[...]*(1.0/SQ)).astype(BF).T
+    x=x_ref[0]
+    xhat,rstd=norm_stats(x)
+    xn=(xhat*gains_ref[0:1,:]+shifts_ref[0:1,:]).astype(BF)
+    xnT=xn.T
+    gr=jnp.zeros((WIN,D),F32)
+    for m in range(2):
+        for k in range(3):
+            gc=gq_s[k,:,m*cq:(m+1)*cq]
+            gr=gr+mm_nt(gc,W1[m,:,k*cq:(k+1)*cq])
+            aq[m,:,k*cq:(k+1)*cq]+=mm(xnT,gc)
+    @pl.when(w==nw-1)
+    def _():
+        dq_s[...]=aq[...].astype(BF).reshape(dq_s.shape)
+        red.start()
+    dd_s[w,0:WIN,:]=(gln2_ref[0]+norm_back(gr,xhat,rstd,gains_ref[0:1,:])).astype(BF)
+    slab(w).start(); slab(w,mate).start()
+    @pl.when(jnp.logical_and(w==nw-1,y==1))
+    def _():
+        tail(0).start(); tail(1).start()
+    small_ref[0:1,:]+=jnp.sum(gr*xhat,axis=0,keepdims=True)
+    small_ref[2:3,:]+=jnp.sum(gr,axis=0,keepdims=True)
+    pl.when(w==0)(big.one)
+    pl.when(w==nw-2)(big.two)
+    @pl.when(w==nw-1)
+    def _():
+        for h in range(nheads): trade(h).wait()
+        acc[...]=jnp.zeros_like(acc)
+        nh=acc.shape[0]; LW=tiles*128
+        base=c*(WIN-part)
+        def rows(r,_):
+            r8=pl.multiple_of(r*8,8)
+            f8=pl.multiple_of(base+r*8,8)
+            pos=pos_ref[pl.ds(f8,8),:]
+            hi8=pos>>8; lo8=pos&255
+            tot=jnp.zeros((nh*nheads,256),F32)
+            iota=lax.broadcasted_iota(jnp.int32,(256,LW),0).astype(F32).astype(BF)
+            for k in range(8):
+                g=jnp.concatenate([G_s[q,pl.ds(f8+k,nheads,stride=WIN),:]+Gx[q,pl.ds(r8+k,nheads,stride=part),:] for q in range(tiles)],axis=1)
+                hr=hi8[k:k+1,:]; lr=lo8[k:k+1,:].astype(F32).astype(BF)
+                A=jnp.concatenate([jnp.where(hr==m,g,0.0) for m in range(nh)],axis=0).astype(BF)
+                oh=jnp.where(iota==lr,jnp.ones((),BF),jnp.zeros((),BF))
+                tot=tot+mm_nt(A,oh)
+            acc[...]+=tot.reshape(acc.shape)
+            return 0
+        n=part//8
+        lax.fori_loop(c,n*3//25,rows,0)
+        red.one()
+        lax.fori_loop(n*3//25,n*13//25,rows,0)
+        red.two()
+        lax.fori_loop(n*13//25,n*19//25,rows,0)
+        big.three()
+        lax.fori_loop(n*19//25,n,rows,0)
+        big.four()
+        half=nheads//2; nb=nh//2
+        def pair(k,src,dst,to):
+            return [send(src,dst,ts.at[2*k],tq_.at[2*k],to),send(sr.at[6+min(k,3)],sr.at[k],ts.at[2*k+1],tq_.at[2*k+1],to)]
+        def run(cps):
+            for p in cps: p.start()
+            for p in cps: p.wait()
+        sr[6]=small_ref[...]
+        run(pair(0,acc.at[:,pl.ds(pl.multiple_of((1-y)*half,8),half)],tu.at[0],mate))
+        tu[1]=acc[:,pl.ds(pl.multiple_of(y*half,8),half)]+tu[0]
+        sr[7]=sr[6]+sr[0]
+        run(pair(1,tu.at[1,pl.ds((1-c)*nb,nb)],tr.at[0],sib))
+        tk[0]=tu[1,pl.ds(c*nb,nb)]+tr[0]
+        sr[8]=sr[7]+sr[1]
+        run(pair(2,tk.at[0],tr.at[1],dev(z,1-xc,c,y)))
+        tk[1]=tk[0]+tr[1]
+        sr[9]=sr[8]+sr[2]
+        cps=[]
+        for k in (1,2,3):
+            cps+=pair(2+k,tk.at[1],tr.at[1+k],dev((z+k)%4,xc,c,y))
+        run(cps)
+        red.three()
+        tu[2,pl.ds(c*nb,nb)]=tk[1]+tr[2]+tr[3]+tr[4]
+        sum_ref[...]=sr[9]+sr[3]+sr[4]+sr[5]
+        cp=send(tu.at[2,pl.ds(c*nb,nb)],tu.at[2,pl.ds(c*nb,nb)],ts.at[12],tq_.at[12],sib)
+        cp.start()
+        red.four()
+        cp.wait_send()
+        send(tu.at[2,pl.ds((1-c)*nb,nb)],tu.at[2,pl.ds((1-c)*nb,nb)],ts.at[12],tq_.at[12],sib).wait_recv()
+        for m in range(nh):
+            tab_ref[:,m*256:(m+1)*256]=tu[2,m]
+        for k in range(nw):
+            slab(k).wait(); slab(k,mate).wait()
+        @pl.when(y==1)
+        def _():
+            tail(0).wait_send(); tail(1).wait_send()
+        tail(0).wait_recv()
+
+def call_bc(x,gln2,qkv,g,gT,Dd,Pp,W1,gains,shifts,sm,posT,dcat,T):
+    nW,WIN,D=x.shape; NH=Dd.shape[1]
+    cq=D//2; tiles=-(-WIN//128); SLAB=-(-WIN//16)*16; EDGE=-(-(SLAB-WIN//2)//16)*16
+    part=-(-WIN//16)*8
+    nh=-(-T//256); nh+=nh%2
+    rows,more=dcat.shape[-2:]; cols=3*cq
+    pp=jnp.pad(posT,((0,0),(0,tiles*128-WIN)),constant_values=nh*256)
+    sd=jax.ShapeDtypeStruct; dma=pltpu.SemaphoreType.DMA; v=pltpu.VMEM
+    return pl.pallas_call(functools.partial(kernel_bc,NH),grid=(nW,),
+      in_specs=[per((WIN,D)),per((WIN,D)),per((3,WIN,D)),per((WIN,D)),per((D,WIN)),per((NH,WIN)),per((NH,WIN,WIN)),
+        full((2,D,cols),pipeline_mode=ONE),full(gains.shape),full(shifts.shape),full(sm.shape),full(pp.shape,pipeline_mode=ONE),ANY],
+      out_specs=[ANY,ANY,full((rows,cols)),full((rows,more)),full((NH//2,nh*256)),full(sm.shape)],
+      out_shape=[sd((2*nW,SLAB,D),BF),sd((EDGE,D),BF),sd((rows,cols),F32),sd((rows,more),F32),sd((NH//2,nh*256),F32),sd(sm.shape,F32)],
+      scratch_shapes=[v((tiles,NH*WIN,128),F32),v((tiles,NH*part,128),F32),v((2,D,cols),F32),v((2,4,2,2,rows,cols),BF),v((D,WIN),BF),v((3,WIN,D),BF),v((D,WIN),F32),
+        v((nW,SLAB,D),BF),v(sm.shape,F32),v((nh,NH,256),F32),v((2,nh//2,NH//2,256),F32),v((5,nh//2,NH//2,256),F32),v((3,nh,NH//2,256),F32),v((10,)+sm.shape,F32),
+        dma((NH,)),dma((NH,)),dma((nW,)),dma((nW,)),dma((nW,)),dma((2,)),dma,dma((13,)),dma((13,))]+reduce_scratch(rows,cols)+reduce_scratch(rows,more),
+      compiler_params=pltpu.CompilerParams(vmem_limit_bytes=63*1024*1024,dimension_semantics=("arbitrary",),collective_id=3,has_side_effects=True),
+      name="kernel_bc")(x,gln2,qkv,g,gT,Dd,Pp,W1,gains,shifts,sm,pp,dcat)
 
 def gathered(piece,names,nseq,nheads):
     full=lax.all_gather(piece,names,axis=0,tiled=False)
@@ -635,16 +940,16 @@
         return jnp.where(me==0,jnp.concatenate([flat,other]),jnp.concatenate([other,flat]))
     return lax.all_gather(flat,"heads",axis=0,tiled=True)
 
-def place(rows,other,base,shift):
-    if other is None:
-        every=spread(rows)
-    else:
-        a,b=[v.reshape(-1,v.shape[-1]) for v in (rows,other)]
-        me=lax.axis_index("heads")
-        every=jnp.where(me==0,jnp.concatenate([a,b]),jnp.concatenate([b,a]))
+def place(rows,base,shift):
+    every=spread(rows)
     keep=every.shape[0]-shift
-    moved=jnp.concatenate([to_next(every[keep:]),every[:keep]])
-    return base+moved.astype(F32)
+    return base+jnp.concatenate([to_next(every[keep:]),every[:keep]]).astype(F32)
+
+def settle(slabs,edge,base,shift):
+    n,size,D=slabs.shape; WIN=2*shift
+    keep=base.shape[0]-shift
+    off=edge.shape[0]-(size-shift)
+    return base+jnp.concatenate([edge[off:off+shift],slabs[:,:WIN].reshape(n*WIN,D)[:keep]]).astype(F32)
 
 def body(inputs,w_qkv,w_proj,w_fc1,w_fc2,gains,shifts,rel_table,region,pos_index,out_grad):
     nseq=lax.axis_size("seq"); nheads=lax.axis_size("heads"); me=lax.axis_index("heads")
@@ -653,44 +958,44 @@
     tok,D=inputs.shape; WIN=pos_index.shape[0]; shift=WIN//2; T=rel_table.shape[1]
     nW=tok//WIN//nheads
     rows=w_qkv.shape[1]; cq=w_qkv.shape[2]; cf=w_fc1.shape[1]
-    wcat=jnp.concatenate([w_qkv[0],w_qkv[1],w_qkv[2],w_proj.T,w_fc1,w_fc2.T],axis=1).astype(BF)
-    table=lax.all_gather(rel_table,"heads",axis=0,tiled=True)
-    NH=table.shape[0]
     posT=pos_index.T
     wide=-(-WIN//128)*128
     posP=jnp.pad(posT,((0,0),(0,wide-WIN)))
-    tab=pack_table(table)
+    start=me*nW*WIN
+    lab=lax.dynamic_slice_in_dim(region,start,nW*WIN,0).reshape(nW,WIN)
+    labc=lab[:,:,None]; labr=lab[:,None,:]
+    wq=jnp.concatenate([w_qkv[0],w_qkv[1],w_qkv[2],w_proj.T],axis=1).astype(BF)
+    wf=jnp.concatenate([w_fc1,w_fc2.T],axis=1).astype(BF)
     if linked:
-        W,bias=call_w(wcat,posP,tab.reshape((2,tab.shape[0]//2)+tab.shape[1:]),WIN)
-        W=W.reshape(nheads,D,-1)
+        n=-(-T//128)
+        tab=jnp.pad(rel_table,((0,0),(0,n*128-T))).reshape(-1,n,128)
+        W1,bias=call_w(wq,posP,tab,WIN)
+        qkv,x,Pp,gln2,g,gT,Dd,ev,hd,dcat,sm=call_a2(inputs,out_grad,wf,labc,labr,bias,W1,gains,shifts)
+        output=settle(ev,hd,inputs,shift)
+        ev2,hd2,redq,redm,d_table,small=call_bc(x,gln2,qkv,g,gT,Dd,Pp,W1,gains,shifts,sm,posT,dcat.reshape(2,4,2,2,rows,-1),T)
+        d_table=d_table[:,:T]
+        d_inputs=settle(ev2,hd2,out_grad,shift)
     else:
-        every=gathered(wcat,names,nseq,nheads)
+        table=lax.all_gather(rel_table,"heads",axis=0,tiled=True)
+        NH=table.shape[0]
+        every=gathered(jnp.concatenate([wq,wf],axis=1),names,nseq,nheads)
         ends=[i*cq for i in range(5)]+[4*cq+cf,4*cq+2*cf]
         W=jnp.concatenate([natural(every[...,a:b]) for a,b in zip(ends[:-1],ends[1:])],axis=1)[None]
-        bias=call_p(posP,tab,WIN)
-    start=me*nW*WIN
-    def mine(v):
-        ext=jnp.concatenate([v,from_next(v[:shift])])
-        return lax.dynamic_slice_in_dim(ext,start+shift,nW*WIN,0).reshape(nW,WIN,-1)
-    x=mine(inputs); og=mine(out_grad)
-    lab=lax.dynamic_slice_in_dim(region,start,nW*WIN,0).reshape(nW,WIN)
-    delta,gln2,qkv,g,gT,Dd,Pp,dcat,sm_a=call_a(x,og,lab[:,:,None],lab[:,None,:],bias,W,gains,shifts)
-    if linked:
-        dcat=dcat.reshape(2,4,2,2,rows,-1)
-    dd,dqkv,G,sm_b,od,odd,mid=call_b(linked,x,gln2,qkv,g,gT,Dd,Pp,W,gains,shifts,delta,dcat)
-    if linked:
-        redq,redm,d_table,small=call_c(G,posT,T,NH,sm_a+sm_b,dqkv.reshape(2,4,2,2,rows,-1),mid)
-    else:
-        od=odd=None
-        wide=D+2*cf*nheads
+        bias=call_p(posP,pack_table(table),WIN)
+        def mine(v):
+            ext=jnp.concatenate([v,from_next(v[:shift])])
+            return lax.dynamic_slice_in_dim(ext,start+shift,nW*WIN,0).reshape(nW,WIN,-1)
+        x=mine(inputs); og=mine(out_grad)
+        delta,gln2,qkv,g,gT,Dd,Pp,dcat,sm_a=call_a(x,og,labc,labr,bias,W,gains,shifts)
+        dd,dqkv,G,sm_b=call_b(x,gln2,qkv,g,gT,Dd,Pp,W,gains,shifts)
         grads=[dqkv[0,:,c*D:(c+1)*D] for c in range(3)]+[dcat[0,:,:D],dcat[0,:,D:D+cf*nheads],dcat[0,:,D+cf*nheads:]]
         red=lax.psum_scatter(jnp.concatenate([owners(v,nseq,nheads) for v in grads],axis=2),names,scatter_dimension=0,tiled=False).astype(F32)
         redq,redm=red[:,:3*cq],red[:,3*cq:]
         d_table,small=lax.psum((call_t(G,posT,T,NH),sm_a+sm_b),names)
         nl=rel_table.shape[0]
         d_table=lax.dynamic_slice_in_dim(d_table,me*nl,nl,0)
-    output=place(delta,od,inputs,shift)
-    d_inputs=place(dd,odd,out_grad,shift)
+        output=place(delta,inputs,shift)
+        d_inputs=place(dd,out_grad,shift)
     d_qkv=redq.reshape(rows,3,cq).transpose(1,0,2)
     d_proj=redm[:,:cq].T; d_fc1=redm[:,cq:cq+cf]; d_fc2=redm[:,cq+cf:].T
     return (output,d_inputs,d_qkv,d_proj,d_fc1,d_fc2,small[0:2],small[2:6],d_table)

time: 347 us -> 282 us (0.81)
  Pallas kernels: 281 us -> 246 us
  other arithmetic: 27.5 us -> 9.97 us
  local copies, waits for them, and re-layouts: 16.3 us -> 24.8 us
  waiting for transfers between devices: 8.37 us -> 0 us
  starting transfers between devices: 7.18 us -> 0 us
  blocking collectives: 5.32 us -> 0 us
    pallas_call x4 -> x3, Pallas kernels: 281 us -> 246 us  [the longest x1 109 us: call_a2(): pl.pallas_call(functools.partial(kernel_a2, NH), grid=(2 * nW,), in_specs...]
    concatenate x3 -> x2, other arithmetic: 10.2 us -> 0.67 us  [the longest x1 0.66 us: body(): wf = jnp.concatenate([w_fc1, w_fc2.T], axis=1).astype(BF)]
    ppermute x4 -> x0, waiting for transfers between devices: 8.37 us -> none  [the longest x2 8.36 us: to_next(): return lax.ppermute(rows, 'seq', [(i, (i + 1) % n) for i in range(n)])]
    ppermute x4 -> x0, starting transfers between devices: 7.18 us -> none  [the longest x2 6.09 us: from_next(): return lax.ppermute(rows, 'seq', [(i, (i - 1) % n) for i in range(n)])]
    add x3 -> x1, other arithmetic: 12.9 us -> 5.81 us  [settle(): base + jnp.concatenate([edge[off:off + shift], slabs[:, :WIN].reshape(n *...]
    all_gather x1 -> x0, blocking collectives: 5.32 us -> none  [body(): table = lax.all_gather(rel_table, 'heads', axis=0, tiled=True)]
    unnamed x44 -> x17, local copies, waits for them, and re-layouts: 4.41 us -> 8.25 us
  transfers between devices with their start and end apart: 4 -> 0, of which waited for: 1 -> 0; matrix products, arithmetic and copies ran while one was open for 6% -> 0% of each run, Pallas kernels for 11% -> 0%
where the time goes in v3:
time: 282 us; the launch traced here: 281 us
  Pallas kernels  246 us (87%)
  local copies, waits for them, and re-layouts  24.8 us (9%)
  other arithmetic  9.97 us (4%)
    pallas_call x1, Pallas kernels, call_a2(): pl.pallas_call(functools.partial(kernel_a2, NH), grid=(2 * nW,), in_specs...  109 us
    pallas_call x1, Pallas kernels, call_bc(): pl.pallas_call(functools.partial(kernel_bc, NH), grid=(nW,), in_specs=[pe...  103 us
    pallas_call x1, Pallas kernels, call_w(): pl.pallas_call(kernel_w, out_shape=[jax.ShapeDtypeStruct((2, 16 * rows, c...  33.5 us
    unnamed x17, local copies, waits for them, and re-layouts  8.25 us
    add x1, other arithmetic, settle(): base + jnp.concatenate([edge[off:off + shift], slabs[:, :WIN].reshape(n *...  5.81 us

profile of v3, /device:TPU:0, one launch (start us, length us, event | category | flops | bytes accessed | tf_op | source)
XLA Modules:
  0.0 281.2 jit_solution(15227973490216291858)
XLA Ops:
  0.6 0.8 dynamic_slice.3
  1.4 0.7 broadcast_in_dim_reshape.7.labr_ref
  2.1 0.8 convert_bitcast_fusion.1
  2.9 0.9 convert.24
  3.8 0.9 convert.22
  4.7 0.9 convert_bitcast_fusion
  5.6 0.7 pad_maximum_fusion.wf_hbm
  6.3 0.9 pad_bitcast_fusion
  7.2 1.6 broadcast_in_dim_reshape.8.labc_ref
  8.8 1.4 copy.22
  10.2 1.1 fusion
  11.3 33.5 %kernel_w.1 = (bf16[2,512,1024]{2,1,0:T(8,128)(2,1)S(1)}, f32[16,392,392]{2,1,0:T(8,128)}) custom-call(bf16[32,1024]{1,0:T(8,128)(2,1)S(1)} %pad_maximum_fusion.1.w_hbm, s32[392,512]{1,0:T(8,128)S(1)} %get-tuple-element.57.pos_ref, f32[8,20,128]{2,1,0:T(8,128)S(1)} %copy.23.tab_ref), custom_call_target="tpu_custom_call" | custom-call | tf_op jit(solution)/shard_map/kernel_w/pallas_call | solution.py:453
  44.8 0.0 copy-start
  44.8 1.3 copy-done
  46.1 109.2 %kernel_a2.1 = (bf16[4,3,392,512]{3,2,1,0:T(8,128)(2,1)}, f32[4,392,512]{2,1,0:T(8,128)}, bf16[4,16,392,392]{3,2,1,0:T(8,128)(2,1)}, f32[4,392,512]{2,1,0:T(8,12...) custom-call(f32[3136,512]{1,0:T(8,128)} %in_hbm.1, ...), custom_call_target="tpu_custom_call" | custom-call | tf_op jit(solution)/shard_map/kernel_a2/pallas_call | solution.py:654
  155.3 1.0 slice.51
  156.3 102.9 %kernel_bc.1 = (bf16[8,400,512]{2,1,0:T(8,128)(2,1)}, bf16[208,512]{1,0:T(8,128)(2,1)}, f32[32,768]{1,0:T(8,128)}, f32[32,2304]{1,0:T(8,128)}, f32[8,2560]{1,0:T(8,128)}, /*index=5*/f32[8,512]{1,0:T(8,128)}) custom-call(f32[4,392,512]{2,1,0:T(8,128)} %get-tuple-element.32.x_ref, f32[4,392,512]{2,1,0:T(8,128)} %get-tuple-element.33.gln2_ref, ...), custom_call_target="tpu_custom_call" | custom-call | tf_op jit(solution)/shard_map/kernel_bc/pallas_call | solution.py:903
  259.2 1.0 slice.54
  260.2 1.3 slice.60
  261.5 1.3 slice.61
  262.8 1.4 slice_bitcast_fusion.1
  264.2 1.7 slice_bitcast_fusion
  265.9 0.9 reshape.37
  266.8 0.7 copy.25
  267.5 0.0 copy-start.1
  267.5 2.3 slice.55
  269.8 0.0 slice-start
  269.8 0.0 slice-start.2
  269.8 0.2 slice.67
  270.0 0.4 copy-done.1
  270.4 0.0 slice-start.1
  270.4 0.0 slice-start.3
  270.4 0.3 slice.52
  270.7 0.2 slice.66
  270.9 1.2 slice-done
  272.1 1.2 slice-done.2
  273.3 0.6 slice-done.1
  273.9 0.8 slice-done.3
  274.7 0.0 copy-start.2
  274.7 5.8 %convert_add_fusion = (f32[3136,512]{1,0:T(8,128)}, f32[3136,512]{1,0:T(8,128)}) fusion(f32[3136,512]{1,0:T(8,128)S(1)} %bitcast.23, bf16[2940,512]{1,0:T(8,128)(2,1)S(1)} %slice.67, bf16[196,512]{1,0:T(8,128)(2,1)S(1)} %slice.54, f32[3136,512]{1,0:T(8,128)S(1)} %bitcast.25, bf16[2940,512]{1,0:T(8,128)(2,1)S(1)} %slice.66, bf16[196,512]{1,0:T(8,128)(2,1)S(1)} %slice.51), kind=kLoop, calls=%fused_computation | loop fusion | flops 16056320 | bytes 32112640 | tf_op jit(solution)/shard_map/add | solution.py:952
  280.5 0.0 copy-done.2
  280.5 0.6 copy.27
  (5 shorter events, 0.0 us)
Async XLA Ops:
  44.8 1.3 copy-start
  267.5 2.9 %copy-start.1 = (bf16[8,400,512]{2,1,0:T(8,128)(2,1)S(1)}, bf16[8,400,512]{2,1,0:T(8,128)(2,1)}, u32[]{:S(2)}) copy-start(bf16[8,400,512]{2,1,0:T(8,128)(2,1)} %get-tuple-element.31) | copy-start | bytes 9830404
  269.8 2.3 slice-start
  269.8 3.5 %slice-start.2 = ((s8[6422528]{0:T(1024)(128)(4,1)}), s8[4194304]{0:T(1024)(128)(4,1)S(1)}, s32[]{:S(2)}) async-start(s8[6422528]{0:T(1024)(128)(4,1)} %bitcast.24), calls=%async_computation.2 | async-start | bytes 8388608
  270.4 3.5 %slice-start.1 = ((s8[6422528]{0:T(1024)(128)(4,1)}), s8[2228224]{0:T(1024)(128)(4,1)S(1)}, s32[]{:S(2)}) async-start(s8[6422528]{0:T(1024)(128)(4,1)} %bitcast.22), calls=%async_computation.1 | async-start | bytes 4456448
  270.4 4.3 %slice-start.3 = ((s8[6422528]{0:T(1024)(128)(4,1)}), s8[2228224]{0:T(1024)(128)(4,1)S(1)}, s32[]{:S(2)}) async-start(s8[6422528]{0:T(1024)(128)(4,1)} %bitcast.24), calls=%async_computation.3 | async-start | bytes 4456448
  274.7 5.8 %copy-start.2 = (f32[8,2560]{1,0:T(8,128)S(1)}, f32[8,2560]{1,0:T(8,128)}, u32[]{:S(2)}) copy-start(f32[8,2560]{1,0:T(8,128)} %get-tuple-element.46) | copy-start | bytes 245764

commit v4 on v3

--- a/solution.py
+++ b/solution.py
@@ -387,21 +387,31 @@
     return [pltpu.SemaphoreType.DMA((31,)),pltpu.SemaphoreType.DMA((31,)),pltpu.SemaphoreType.DMA]
 
 STEPS=7
-def kernel_w(w_hbm,pos_ref,tab_ref,W_hbm,bias_hbm,bias_s,tb,tq,ss,rs,own,bs,br,bl,tsem):
+def kernel_w(qkv_ref,proj_ref,fc1_ref,fc2_ref,pos_ref,tab_ref,W_hbm,bias_hbm,wf_ref,posT_ref,
+             bias_s,wq_s,tb,tq,ss,rs,own,bs,br,bl,tsem):
     z,x,c,y=place_of()
+    cq=qkv_ref.shape[2]; cf=fc1_ref.shape[1]
+    for k in range(3): wq_s[:,k*cq:(k+1)*cq]=qkv_ref[k].astype(BF)
+    wq_s[:,3*cq:4*cq]=proj_ref[...].T.astype(BF)
+    half,T=tab_ref.shape
+    tb[2]=jnp.zeros(tb.shape[1:],F32)
+    tb[2,:,0:T]=tab_ref[...]
     greet(peers_of(z,x,c,y))
-    gather=Gather(w_hbm,W_hbm,ss,rs,own)
-    swap=send(tab_ref,tb.at[y],tsem.at[0],tsem.at[1],dev(z,x,c,1-y))
+    gather=Gather(wq_s,W_hbm,ss,rs,own)
+    swap=send(tb.at[2],tb.at[y],tsem.at[0],tsem.at[1],dev(z,x,c,1-y))
     swap.start()
     gather.start()
-    tb[y]=tab_ref[...]
+    tb[y]=tb[2]
+    wf_ref[:,0:cf]=fc1_ref[...].astype(BF)
+    wf_ref[:,cf:2*cf]=fc2_ref[...].T.astype(BF)
+    WIN=bias_s.shape[-1]; tiles=-(-WIN//128); n=tb.shape[2]//128
+    posT_ref[...]=jnp.full(posT_ref.shape,1<<15,jnp.int32)
+    posT_ref[:,0:WIN]=pos_ref[...].astype(F32).T.astype(jnp.int32)
     swap.wait()
-    half,n=tab_ref.shape[0],tab_ref.shape[1]
     npair=half//2
     for p in range(npair):
-        a,b=[jnp.floor(jnp.clip(tb[c,2*p+k],-4.0,4.0)*FIX+0.5).astype(jnp.int32) for k in range(2)]
-        tq[p]=(a*65536)|(b&65535)
-    WIN=bias_s.shape[-1]; tiles=-(-WIN//128)
+        a,b=[jnp.floor(jnp.clip(tb[c,2*p+k:2*p+k+1,:],-4.0,4.0)*FIX+0.5).astype(jnp.int32) for k in range(2)]
+        tq[p:p+1,:]=(a*65536)|(b&65535)
     nrow=WIN//8
     cuts=[nrow*k//STEPS for k in range(STEPS+1)]
     sib=dev(z,x,1-c,y)
@@ -413,13 +423,13 @@
             r8=pl.multiple_of(r*8,8)
             for t in range(tiles):
                 width=min(128,WIN-t*128)
-                idx=pos_ref[pl.ds(r8,8),t*128:(t+1)*128]
+                idx=posT_ref[pl.ds(r8,8),t*128:(t+1)*128]
                 lo=idx&127; hi=idx>>7
                 masks=[hi==q for q in range(n)]
                 for p in range(npair):
                     acc=jnp.zeros((8,128),jnp.int32)
                     for q in range(n):
-                        src=jnp.broadcast_to(tq[p,q:q+1,:],(8,128))
+                        src=jnp.broadcast_to(tq[p:p+1,q*128:(q+1)*128],(8,128))
                         acc=jnp.where(masks[q],jnp.take_along_axis(src,lo,axis=1),acc)
                     a=(acc>>16).astype(F32)*(SQ/FIX)
                     b=((acc<<16)>>16).astype(F32)*(SQ/FIX)
@@ -447,24 +457,26 @@
         kept(k).wait(); sent(k,c).wait_send(); sent(k,1-c).wait_recv()
     gather.drain()
 
-def call_w(wq,posT_pad,tab,WIN):
-    rows,cols=wq.shape; half=tab.shape[0]; dma=pltpu.SemaphoreType.DMA
+def call_w(w_qkv,w_proj,w_fc1,w_fc2,pos_index,rel_table):
+    rows,cq=w_qkv.shape[1:]; cf=w_fc1.shape[1]; WIN=pos_index.shape[0]; half,T=rel_table.shape; dma=pltpu.SemaphoreType.DMA
+    wide=-(-WIN//128)*128; n=-(-T//128); v=pltpu.VMEM
+    sd=jax.ShapeDtypeStruct
     vm=pl.BlockSpec(memory_space=pltpu.VMEM)
     return pl.pallas_call(kernel_w,
-      out_shape=[jax.ShapeDtypeStruct((2,16*rows,cols),BF),jax.ShapeDtypeStruct((2*half,WIN,WIN),F32)],
-      in_specs=[ANY,vm,vm],out_specs=[ANY]*2,
-      scratch_shapes=[pltpu.VMEM((half,WIN,WIN),F32),pltpu.VMEM((2,)+tab.shape,F32),pltpu.VMEM((half//2,)+tab.shape[1:],jnp.int32)]
+      out_shape=[sd((2,16*rows,4*cq),BF),sd((2*half,WIN,WIN),F32),sd((rows,2*cf),BF),sd((WIN,wide),jnp.int32)],
+      in_specs=[vm]*6,out_specs=[ANY,ANY,vm,vm],
+      scratch_shapes=[v((half,WIN,WIN),F32),v((rows,4*cq),BF),v((3,half,n*128),F32),v((half//2,n*128),jnp.int32)]
         +gather_sems()+[dma((STEPS,)),dma((STEPS,)),dma((STEPS,)),dma((2,))],
-      compiler_params=pltpu.CompilerParams(vmem_limit_bytes=40*1024*1024,collective_id=1,has_side_effects=True),name="kernel_w")(wq,posT_pad,tab)
+      compiler_params=pltpu.CompilerParams(vmem_limit_bytes=40*1024*1024,collective_id=1,has_side_effects=True),name="kernel_w")(w_qkv,w_proj,w_fc1,w_fc2,pos_index,rel_table)
 
 def neighbours(z,x,c,y):
     s=(z*2+x)*2+c
     return [((s+k)%16,yy) for k in (1,15) for yy in (y,1-y)]
 
-def kernel_a2(nheads,in_hbm,og_hbm,wf_hbm,labc_ref,labr_ref,bias_ref,W1,gains_ref,shifts_ref,
-              qkv_ref,x_ref,P_hbm,gln2_ref,g_ref,gT_ref,D_ref,ev_hbm,hd_hbm,dcat_hbm,small_ref,
+def kernel_a2(nheads,in_hbm,og_hbm,wf_hbm,lab_ref,bias_ref,W1,gains_ref,shifts_ref,
+              qkv_ref,x_ref,P_hbm,gln2_ref,g_ref,gT_ref,D_ref,ev_hbm,dlast_hbm,dcat_hbm,small_ref,
               x_s,og_s,W2,OT_s,qT_s,vT_s,P_s,acc,pst,xn2_s,xn2T_s,tg_s,tgT_s,up_s,gn2_s,dl_s,
-              psem,xsem,hsem,ss,rs,own,dl,ds,dr,es,er,fin):
+              lab_s,psem,xsem,hsem,ss,rs,own,dl,ds,dr,fin):
     i=pl.program_id(0); nw=x_s.shape[0]
     w=i%nw
     z,xc,c,y=place_of()
@@ -490,12 +502,10 @@
         @pl.when(jnp.logical_not(far))
         def _(): local(w,1,t).wait()
     def slab(k,to=None):
+        if k is None: return pltpu.make_async_copy(dl_s.at[nw-1],dlast_hbm,dl.at[nw-1])
         at=ev_hbm.at[y*nw+k]
         if to is None: return pltpu.make_async_copy(dl_s.at[k],at,dl.at[k])
         return send(dl_s.at[k],at,ds.at[k],dr.at[k],to)
-    def tail(k):
-        lead=SLAB-hd_hbm.shape[0]
-        return send(dl_s.at[nw-1,pl.ds(lead,hd_hbm.shape[0])],hd_hbm,es.at[k],er,((s+1)%16,k))
     @pl.when(i==0)
     def _():
         greet(peers_of(z,xc,c,y)+neighbours(z,xc,c,y))
@@ -509,6 +519,7 @@
             @pl.when(y==0)
             def _(): local(nw-1,1,t).start()
         gather.start()
+        lab_s[...]=lab_ref[...].astype(F32).T
         acc[...]=jnp.zeros_like(acc)
         small_ref[...]=jnp.zeros_like(small_ref)
         dl_s[:,SLAB-16:,:]=jnp.zeros((nw,16,D),BF)
@@ -527,7 +538,9 @@
                 qkv_ref[0,k,:,at]=v
                 if k==0: qT_s[at,:]=v.T
                 if k==2: vT_s[at,:]=v.T
-        labc=labc_ref[0]; labr=labr_ref[0]
+        mine=y*nw+w
+        labr=lab_ref[pl.ds(mine,1),:]
+        labc=jnp.sum(jnp.where(lax.broadcasted_iota(jnp.int32,lab_s.shape,1)==mine,lab_s[...],0.0),axis=1,keepdims=True).astype(jnp.int32)
         lane=lax.broadcasted_iota(jnp.int32,(WIN,GROUP),1)
         oh=jnp.where((labc==lane)|((labc+3)==lane),1.0,0.0).astype(BF)
         hi=564.0
@@ -601,10 +614,11 @@
             return 0
         lax.fori_loop(0,2*each,chunk,0)
         dl_s[w,0:WIN,:]=(branch+up_s[...]+shifts_ref[3:4,:]).astype(BF)
-        slab(w).start(); slab(w,mate).start()
-        @pl.when(jnp.logical_and(w==nw-1,y==1))
+        @pl.when(w<nw-1)
         def _():
-            tail(0).start(); tail(1).start()
+            slab(w).start(); slab(w,mate).start()
+        @pl.when(w==nw-1)
+        def _(): slab(None).start()
         gn2=gn2_s[...]
         gln2=norm_back(gn2,xhat2,rstd2,gains_ref[1:2,:])
         gln2_ref[0]=gln2
@@ -634,32 +648,31 @@
         a.start(); b.start()
         for k in range(2):
             pltpu.make_async_copy(P_s.at[k],P_hbm.at[0,pl.ds(0,PER)],psem.at[k]).wait()
-        for k in range(nw):
+        for k in range(nw-1):
             slab(k).wait(); slab(k,mate).wait()
+        slab(None).wait()
         @pl.when(y==1)
         def _():
             for t in range(2): edge(t).wait_send()
-            tail(0).wait_send(); tail(1).wait_send()
-        tail(0).wait_recv()
         a.wait(); b.wait()
 
-def call_a2(inputs,og,wf,labc,labr,bias,W1,gains,shifts):
-    nW=labc.shape[0]; WIN=labc.shape[1]; D=inputs.shape[1]; NH=bias.shape[0]
-    cf=wf.shape[1]//2; cq=D//2; SLAB=-(-WIN//16)*16; EDGE=-(-(SLAB-WIN//2)//16)*16
+def call_a2(inputs,og,wf,lab,bias,W1,gains,shifts):
+    nW=lab.shape[0]//2; WIN=lab.shape[1]; D=inputs.shape[1]; NH=bias.shape[0]
+    cf=wf.shape[1]//2; cq=D//2; SLAB=-(-WIN//16)*16
     sd=jax.ShapeDtypeStruct; dma=pltpu.SemaphoreType.DMA; v=pltpu.VMEM
     early=lambda shape: pl.BlockSpec((1,)+shape,lambda i:(jnp.minimum(i,nW-1),)+(0,)*len(shape))
     late=lambda shape: pl.BlockSpec((1,)+shape,lambda i:(jnp.maximum(i-nW,0),)+(0,)*len(shape))
     outs=[sd((nW,3,WIN,D),BF),sd((nW,WIN,D),F32),sd((nW,NH,WIN,WIN),BF),sd((nW,WIN,D),F32),sd((nW,WIN,D),BF),sd((nW,D,WIN),BF),sd((nW,NH,WIN),F32),
-          sd((2*nW,SLAB,D),BF),sd((EDGE,D),BF),sd((2,D,cq+2*cf),BF),sd((8,D),F32)]
+          sd((2*nW,SLAB,D),BF),sd((SLAB,D),BF),sd((2,D,cq+2*cf),BF),sd((8,D),F32)]
     return pl.pallas_call(functools.partial(kernel_a2,NH),grid=(2*nW,),
-      in_specs=[ANY,ANY,ANY,early((WIN,1)),early((1,WIN)),full((NH,WIN,WIN),pipeline_mode=ONE),full(W1.shape,pipeline_mode=ONE),full(gains.shape),full(shifts.shape)],
+      in_specs=[ANY,ANY,ANY,full(lab.shape),full((NH,WIN,WIN),pipeline_mode=ONE),full(W1.shape,pipeline_mode=ONE),full(gains.shape),full(shifts.shape)],
       out_specs=[early((3,WIN,D)),early((WIN,D)),ANY,late((WIN,D)),late((WIN,D)),late((D,WIN)),late((NH,WIN)),ANY,ANY,ANY,full((8,D))],
       out_shape=outs,
       scratch_shapes=[v((nW,SLAB,D),F32),v((nW,SLAB,D),F32),v((2,D,2*cf),BF),v((nW,D,WIN),F32),v((D,WIN),BF),v((D,WIN),BF),v((2,PER,WIN,WIN),BF),
         v((2,D,cq+2*cf),F32),v((2,D,cq),BF),v((WIN,D),BF),v((D,WIN),BF),v((WIN,D),BF),v((D,WIN),BF),v((WIN,D),F32),v((WIN,D),F32),v((nW,SLAB,D),BF),
-        dma((2,)),dma((2,2*nW)),dma((2,2))]+gather_sems()+[dma((nW,)),dma((nW,)),dma((nW,)),dma((2,)),dma,dma((2,))],
+        v((WIN,2*nW),F32),dma((2,)),dma((2,2*nW)),dma((2,2))]+gather_sems()+[dma((nW,)),dma((nW,)),dma((nW,)),dma((2,))],
       compiler_params=pltpu.CompilerParams(vmem_limit_bytes=63*1024*1024,dimension_semantics=("arbitrary",),collective_id=2,has_side_effects=True),
-      name="kernel_a2")(inputs,og,wf,labc,labr,bias,W1,gains,shifts)
+      name="kernel_a2")(inputs,og,wf,lab,bias,W1,gains,shifts)
 
 class Reduce:
     def __init__(self,src,out,own,r1,r2,ss,rs,ls,r3,fin,r4):
@@ -740,10 +753,10 @@
     return [v(2,4,2),v(2,4,2),v(4,2),dma((9,)),dma((9,)),dma((4,)),v(3,2),v(2),v()]
 
 
-def kernel_bc(nheads,x_ref,gln2_ref,qkv_ref,g_ref,gT_ref,D_ref,P_ref,W1,gains_ref,shifts_ref,sm_ref,pos_ref,dcat_hbm,
-              ev_hbm,hd_hbm,redq_ref,redm_ref,tab_ref,sum_ref,
+def kernel_bc(nheads,x_ref,gln2_ref,qkv_ref,g_ref,gT_ref,D_ref,P_ref,W1,gains_ref,shifts_ref,sm_ref,pos_ref,dcat_hbm,dlast_hbm,
+              ev_hbm,hd_hbm,evl_hbm,hdl_hbm,redq_ref,redm_ref,tab_ref,sum_ref,
               G_s,Gx,aq,dq_s,kT_s,gq_s,gqT_s,dd_s,small_ref,acc,tk,tr,tu,sr,
-              gs,gr_,dl,ds,dr,es,er,ts,tq_,
+              gs,gr_,dl,ds,dr,es,er,us,ts,tq_,
               own,r1,r2,ss,rs,ls,r3,fin,r4,own2,p1,p2,ss2,rs2,ls2,p3,fin2,p4):
     w=pl.program_id(0); nw=dd_s.shape[0]
     z,xc,c,y=place_of()
@@ -762,6 +775,11 @@
     def tail(k):
         lead=SLAB-hd_hbm.shape[0]
         return send(dd_s.at[nw-1,pl.ds(lead,hd_hbm.shape[0])],hd_hbm,es.at[k],er,((s+1)%16,k))
+    def early(k):
+        lead=SLAB-hdl_hbm.shape[0]
+        if k==0: return pltpu.make_async_copy(dlast_hbm,evl_hbm.at[y],us.at[0])
+        if k==1: return send(dlast_hbm,evl_hbm.at[y],us.at[1],us.at[2],mate)
+        return send(dlast_hbm.at[pl.ds(lead,hdl_hbm.shape[0])],hdl_hbm,us.at[k+1],us.at[5],((s+1)%16,k-2))
     def trade(h):
         r=pl.multiple_of(h*WIN+(1-c)*(WIN-part),8)
         return send(G_s.at[:,pl.ds(r,part)],Gx.at[:,pl.ds(pl.multiple_of(h*part,8),part)],gs.at[h],gr_.at[h],sib)
@@ -769,6 +787,10 @@
     def _():
         greet(peers_of(z,xc,c,y)+neighbours(z,xc,c,y))
         big.start()
+        early(0).start(); early(1).start()
+        @pl.when(y==1)
+        def _():
+            early(2).start(); early(3).start()
         aq[...]=jnp.zeros_like(aq); G_s[...]=jnp.zeros_like(G_s); small_ref[...]=sm_ref[...]
         dd_s[:,SLAB-16:,:]=jnp.zeros((nw,16,D),BF)
     kT_s[...]=qkv_ref[0,1].T
@@ -889,27 +911,63 @@
             slab(k).wait(); slab(k,mate).wait()
         @pl.when(y==1)
         def _():
-            tail(0).wait_send(); tail(1).wait_send()
-        tail(0).wait_recv()
-
-def call_bc(x,gln2,qkv,g,gT,Dd,Pp,W1,gains,shifts,sm,posT,dcat,T):
+            tail(0).wait_send(); tail(1).wait_send(); early(2).wait_send(); early(3).wait_send()
+        tail(0).wait_recv(); early(2).wait_recv()
+        early(0).wait(); early(1).wait()
+
+def call_bc(x,gln2,qkv,g,gT,Dd,Pp,W1,gains,shifts,sm,pp,dcat,dlast,T):
     nW,WIN,D=x.shape; NH=Dd.shape[1]
     cq=D//2; tiles=-(-WIN//128); SLAB=-(-WIN//16)*16; EDGE=-(-(SLAB-WIN//2)//16)*16
     part=-(-WIN//16)*8
     nh=-(-T//256); nh+=nh%2
     rows,more=dcat.shape[-2:]; cols=3*cq
-    pp=jnp.pad(posT,((0,0),(0,tiles*128-WIN)),constant_values=nh*256)
     sd=jax.ShapeDtypeStruct; dma=pltpu.SemaphoreType.DMA; v=pltpu.VMEM
     return pl.pallas_call(functools.partial(kernel_bc,NH),grid=(nW,),
       in_specs=[per((WIN,D)),per((WIN,D)),per((3,WIN,D)),per((WIN,D)),per((D,WIN)),per((NH,WIN)),per((NH,WIN,WIN)),
-        full((2,D,cols),pipeline_mode=ONE),full(gains.shape),full(shifts.shape),full(sm.shape),full(pp.shape,pipeline_mode=ONE),ANY],
-      out_specs=[ANY,ANY,full((rows,cols)),full((rows,more)),full((NH//2,nh*256)),full(sm.shape)],
-      out_shape=[sd((2*nW,SLAB,D),BF),sd((EDGE,D),BF),sd((rows,cols),F32),sd((rows,more),F32),sd((NH//2,nh*256),F32),sd(sm.shape,F32)],
+        full((2,D,cols),pipeline_mode=ONE),full(gains.shape),full(shifts.shape),full(sm.shape),full(pp.shape,pipeline_mode=ONE),ANY,ANY],
+      out_specs=[ANY,ANY,ANY,ANY,full((rows,cols)),full((rows,more)),full((NH//2,nh*256)),full(sm.shape)],
+      out_shape=[sd((2*nW,SLAB,D),BF),sd((EDGE,D),BF),sd((2,SLAB,D),BF),sd((EDGE,D),BF),sd((rows,cols),F32),sd((rows,more),F32),sd((NH//2,nh*256),F32),sd(sm.shape,F32)],
       scratch_shapes=[v((tiles,NH*WIN,128),F32),v((tiles,NH*part,128),F32),v((2,D,cols),F32),v((2,4,2,2,rows,cols),BF),v((D,WIN),BF),v((3,WIN,D),BF),v((D,WIN),F32),
         v((nW,SLAB,D),BF),v(sm.shape,F32),v((nh,NH,256),F32),v((2,nh//2,NH//2,256),F32),v((5,nh//2,NH//2,256),F32),v((3,nh,NH//2,256),F32),v((10,)+sm.shape,F32),
-        dma((NH,)),dma((NH,)),dma((nW,)),dma((nW,)),dma((nW,)),dma((2,)),dma,dma((13,)),dma((13,))]+reduce_scratch(rows,cols)+reduce_scratch(rows,more),
+        dma((NH,)),dma((NH,)),dma((nW,)),dma((nW,)),dma((nW,)),dma((2,)),dma,dma((6,)),dma((13,)),dma((13,))]+reduce_scratch(rows,cols)+reduce_scratch(rows,more),
       compiler_params=pltpu.CompilerParams(vmem_limit_bytes=63*1024*1024,dimension_semantics=("arbitrary",),collective_id=3,has_side_effects=True),
-      name="kernel_bc")(x,gln2,qkv,g,gT,Dd,Pp,W1,gains,shifts,sm,pp,dcat)
+      name="kernel_bc")(x,gln2,qkv,g,gT,Dd,Pp,W1,gains,shifts,sm,pp,dcat,dlast)
+
+
+def kernel_f(in_ref,og_ref,ev_ref,evl_ref,ev2_ref,hd_ref,hd2_ref,redq_ref,redm_ref,tab_ref,sum_ref,
+             out_ref,din_ref,dqkv_ref,dproj_ref,dfc1_ref,dfc2_ref,dgain_ref,dshift_ref,dtab_ref,end_s):
+    j=pl.program_id(0); nw=pl.num_programs(0)//2
+    shift=in_ref.shape[0]//2; WIN=2*shift
+    edge,SLAB=hd_ref.shape[0],ev_ref.shape[1]
+    off=edge-(SLAB-shift)
+    @pl.when(j==0)
+    def _():
+        end_s[0]=hd_ref[...].astype(F32); end_s[1]=hd2_ref[...].astype(F32)
+        cq=dqkv_ref.shape[2]; cf=dfc1_ref.shape[1]
+        for k in range(3): dqkv_ref[k]=redq_ref[:,k*cq:(k+1)*cq]
+        dproj_ref[...]=redm_ref[:,0:cq].T
+        dfc1_ref[...]=redm_ref[:,cq:cq+cf]
+        dfc2_ref[...]=redm_ref[:,cq+cf:].T
+        dgain_ref[...]=sum_ref[0:2,:]; dshift_ref[...]=sum_ref[2:6,:]
+        dtab_ref[...]=tab_ref[:,0:dtab_ref.shape[1]]
+    e=jnp.where(j%nw==nw-1,evl_ref[0],ev_ref[0]).astype(F32)
+    for k,(base,res,v) in enumerate(((in_ref,out_ref,e),(og_ref,din_ref,ev2_ref[0].astype(F32)))):
+        res[0:shift,:]=base[0:shift,:]+end_s[k,off:off+shift,:]
+        res[shift:WIN,:]=base[shift:WIN,:]+v[0:shift,:]
+        end_s[k]=v[SLAB-edge:,:]
+
+def call_f(inputs,og,ev,evl,ev2,hd,hd2,redq,redm,tab,small,cq,cf,T):
+    tok,D=inputs.shape; n,SLAB,_=ev.shape; WIN=tok//n; rows=redq.shape[0]
+    sd=jax.ShapeDtypeStruct
+    blk=pl.BlockSpec((WIN,D),lambda j:(j,0)); slab=pl.BlockSpec((1,SLAB,D),lambda j:(j,0,0))
+    shapes=[(3,rows,cq),(cq,rows),(rows,cf),(cf,rows),(2,D),(4,D),(tab.shape[0],T)]
+    return pl.pallas_call(kernel_f,grid=(n,),
+      in_specs=[blk,blk,slab,pl.BlockSpec((1,SLAB,D),lambda j:(j//(n//2),0,0)),slab]+[full(v.shape) for v in (hd,hd2,redq,redm,tab,small)],
+      out_specs=[blk,blk]+[full(v) for v in shapes],
+      out_shape=[sd((tok,D),F32),sd((tok,D),F32)]+[sd(v,F32) for v in shapes],
+      scratch_shapes=[pltpu.VMEM((2,)+hd.shape,F32)],
+      compiler_params=pltpu.CompilerParams(vmem_limit_bytes=40*1024*1024,dimension_semantics=("arbitrary",)),
+      name="kernel_f")(inputs,og,ev,evl,ev2,hd,hd2,redq,redm,tab,small)
 
 def gathered(piece,names,nseq,nheads):
     full=lax.all_gather(piece,names,axis=0,tiled=False)
@@ -945,12 +1003,6 @@
     keep=every.shape[0]-shift
     return base+jnp.concatenate([to_next(every[keep:]),every[:keep]]).astype(F32)
 
-def settle(slabs,edge,base,shift):
-    n,size,D=slabs.shape; WIN=2*shift
-    keep=base.shape[0]-shift
-    off=edge.shape[0]-(size-shift)
-    return base+jnp.concatenate([edge[off:off+shift],slabs[:,:WIN].reshape(n*WIN,D)[:keep]]).astype(F32)
-
 def body(inputs,w_qkv,w_proj,w_fc1,w_fc2,gains,shifts,rel_table,region,pos_index,out_grad):
     nseq=lax.axis_size("seq"); nheads=lax.axis_size("heads"); me=lax.axis_index("heads")
     linked=nseq==16 and nheads==2
@@ -958,44 +1010,40 @@
     tok,D=inputs.shape; WIN=pos_index.shape[0]; shift=WIN//2; T=rel_table.shape[1]
     nW=tok//WIN//nheads
     rows=w_qkv.shape[1]; cq=w_qkv.shape[2]; cf=w_fc1.shape[1]
+    lab=region.reshape(-1,WIN)
+    if linked:
+        W1,bias,wf,posT=call_w(w_qkv,w_proj,w_fc1,w_fc2,pos_index,rel_table)
+        qkv,x,Pp,gln2,g,gT,Dd,ev,dlast,dcat,sm=call_a2(inputs,out_grad,wf,lab,bias,W1,gains,shifts)
+        ev2,hd2,evl,hd,redq,redm,d_table,small=call_bc(x,gln2,qkv,g,gT,Dd,Pp,W1,gains,shifts,sm,posT,dcat.reshape(2,4,2,2,rows,-1),dlast,T)
+        return tuple(call_f(inputs,out_grad,ev,evl,ev2,hd,hd2,redq,redm,d_table,small,cq,cf,T))
     posT=pos_index.T
     wide=-(-WIN//128)*128
     posP=jnp.pad(posT,((0,0),(0,wide-WIN)))
     start=me*nW*WIN
-    lab=lax.dynamic_slice_in_dim(region,start,nW*WIN,0).reshape(nW,WIN)
+    lab=lax.dynamic_slice_in_dim(lab,me*nW,nW,0)
     labc=lab[:,:,None]; labr=lab[:,None,:]
     wq=jnp.concatenate([w_qkv[0],w_qkv[1],w_qkv[2],w_proj.T],axis=1).astype(BF)
     wf=jnp.concatenate([w_fc1,w_fc2.T],axis=1).astype(BF)
-    if linked:
-        n=-(-T//128)
-        tab=jnp.pad(rel_table,((0,0),(0,n*128-T))).reshape(-1,n,128)
-        W1,bias=call_w(wq,posP,tab,WIN)
-        qkv,x,Pp,gln2,g,gT,Dd,ev,hd,dcat,sm=call_a2(inputs,out_grad,wf,labc,labr,bias,W1,gains,shifts)
-        output=settle(ev,hd,inputs,shift)
-        ev2,hd2,redq,redm,d_table,small=call_bc(x,gln2,qkv,g,gT,Dd,Pp,W1,gains,shifts,sm,posT,dcat.reshape(2,4,2,2,rows,-1),T)
-        d_table=d_table[:,:T]
-        d_inputs=settle(ev2,hd2,out_grad,shift)
-    else:
-        table=lax.all_gather(rel_table,"heads",axis=0,tiled=True)
-        NH=table.shape[0]
-        every=gathered(jnp.concatenate([wq,wf],axis=1),names,nseq,nheads)
-        ends=[i*cq for i in range(5)]+[4*cq+cf,4*cq+2*cf]
-        W=jnp.concatenate([natural(every[...,a:b]) for a,b in zip(ends[:-1],ends[1:])],axis=1)[None]
-        bias=call_p(posP,pack_table(table),WIN)
-        def mine(v):
-            ext=jnp.concatenate([v,from_next(v[:shift])])
-            return lax.dynamic_slice_in_dim(ext,start+shift,nW*WIN,0).reshape(nW,WIN,-1)
-        x=mine(inputs); og=mine(out_grad)
-        delta,gln2,qkv,g,gT,Dd,Pp,dcat,sm_a=call_a(x,og,labc,labr,bias,W,gains,shifts)
-        dd,dqkv,G,sm_b=call_b(x,gln2,qkv,g,gT,Dd,Pp,W,gains,shifts)
-        grads=[dqkv[0,:,c*D:(c+1)*D] for c in range(3)]+[dcat[0,:,:D],dcat[0,:,D:D+cf*nheads],dcat[0,:,D+cf*nheads:]]
-        red=lax.psum_scatter(jnp.concatenate([owners(v,nseq,nheads) for v in grads],axis=2),names,scatter_dimension=0,tiled=False).astype(F32)
-        redq,redm=red[:,:3*cq],red[:,3*cq:]
-        d_table,small=lax.psum((call_t(G,posT,T,NH),sm_a+sm_b),names)
-        nl=rel_table.shape[0]
-        d_table=lax.dynamic_slice_in_dim(d_table,me*nl,nl,0)
-        output=place(delta,inputs,shift)
-        d_inputs=place(dd,out_grad,shift)
+    table=lax.all_gather(rel_table,"heads",axis=0,tiled=True)
+    NH=table.shape[0]
+    every=gathered(jnp.concatenate([wq,wf],axis=1),names,nseq,nheads)
+    ends=[i*cq for i in range(5)]+[4*cq+cf,4*cq+2*cf]
+    W=jnp.concatenate([natural(every[...,a:b]) for a,b in zip(ends[:-1],ends[1:])],axis=1)[None]
+    bias=call_p(posP,pack_table(table),WIN)
+    def mine(v):
+        ext=jnp.concatenate([v,from_next(v[:shift])])
+        return lax.dynamic_slice_in_dim(ext,start+shift,nW*WIN,0).reshape(nW,WIN,-1)
+    x=mine(inputs); og=mine(out_grad)
+    delta,gln2,qkv,g,gT,Dd,Pp,dcat,sm_a=call_a(x,og,labc,labr,bias,W,gains,shifts)
+    dd,dqkv,G,sm_b=call_b(x,gln2,qkv,g,gT,Dd,Pp,W,gains,shifts)
+    grads=[dqkv[0,:,c*D:(c+1)*D] for c in range(3)]+[dcat[0,:,:D],dcat[0,:,D:D+cf*nheads],dcat[0,:,D+cf*nheads:]]
+    red=lax.psum_scatter(jnp.concatenate([owners(v,nseq,nheads) for v in grads],axis=2),names,scatter_dimension=0,tiled=False).astype(F32)
+    redq,redm=red[:,:3*cq],red[:,3*cq:]
+    d_table,small=lax.psum((call_t(G,posT,T,NH),sm_a+sm_b),names)
+    nl=rel_table.shape[0]
+    d_table=lax.dynamic_slice_in_dim(d_table,me*nl,nl,0)
+    output=place(delta,inputs,shift)
+    d_inputs=place(dd,out_grad,shift)
     d_qkv=redq.reshape(rows,3,cq).transpose(1,0,2)
     d_proj=redm[:,:cq].T; d_fc1=redm[:,cq:cq+cf]; d_fc2=redm[:,cq+cf:].T
     return (output,d_inputs,d_qkv,d_proj,d_fc1,d_fc2,small[0:2],small[2:6],d_table)
@@ -1003,5 +1051,5 @@
 def solution(mesh):
     placed=(P("seq",None),P(None,"seq","heads"),P("heads","seq"),P("seq","heads"),P("heads","seq"),P(),P(),P("heads",None),P("seq"),P(),P("seq",None))
     return jax.shard_map(body,mesh=mesh,in_specs=placed,
-        out_specs=(P("seq",None),P("seq",None),P(None,"seq","heads"),P("heads","seq"),P("seq","heads"),P("heads","seq"),P(),P(),P("heads",None)),
-        check_vma=False)
+    out_specs=(P("seq",None),P("seq",None),P(None,"seq","heads"),P("heads","seq"),P("seq","heads"),P("heads","seq"),P(),P(),P("heads",None)),
+    check_vma=False)

time: 282 us -> 276 us (0.979)
  other arithmetic: 9.97 us -> 0 us
  Pallas kernels: 246 us -> 253 us
  local copies, waits for them, and re-layouts: 24.8 us -> 21.9 us
    pallas_call x1 -> x2, Pallas kernels: 33.5 us -> 45.2 us  [the longest x1 33.6 us: call_w(): pl.pallas_call(kernel_w, out_shape=[sd((2, 16 * rows, 4 * cq), BF), sd((2...]
    unnamed x17 -> x34, local copies, waits for them, and re-layouts: 8.25 us -> 18.9 us
    slice x8 -> x0, local copies, waits for them, and re-layouts: 7.53 us -> none  [the longest x4 2.94 us: settle(): slabs[:, :WIN].reshape(n * WIN, D)[:keep]]
    add x1 -> x0, other arithmetic: 5.81 us -> none  [settle(): base + jnp.concatenate([edge[off:off + shift], slabs[:, :WIN].reshape(n *...]
    pallas_call x1, Pallas kernels: 109 us -> 103 us  [call_a2(): pl.pallas_call(functools.partial(kernel_a2, NH), grid=(2 * nW,), in_specs...]
    transpose x2 -> x0, local copies, waits for them, and re-layouts: 3.06 us -> none  [the longest x1 1.68 us: body(): d_fc2 = redm[:, cq + cf:].T]
where the time goes in v4:
time: 276 us; the launch traced here: 275 us
  Pallas kernels  253 us (92%)
  local copies, waits for them, and re-layouts  21.9 us (8%)
    pallas_call x1, Pallas kernels, call_bc(): pl.pallas_call(functools.partial(kernel_bc, NH), grid=(nW,), in_specs=[pe...  104 us
    pallas_call x1, Pallas kernels, call_a2(): pl.pallas_call(functools.partial(kernel_a2, NH), grid=(2 * nW,), in_specs...  103 us
    pallas_call x1, Pallas kernels, call_w(): pl.pallas_call(kernel_w, out_shape=[sd((2, 16 * rows, 4 * cq), BF), sd((2...  33.6 us
    unnamed x34, local copies, waits for them, and re-layouts  18.9 us
    pallas_call x1, Pallas kernels, call_f(): pl.pallas_call(kernel_f, grid=(n,), in_specs=[blk, blk, slab, pl.BlockSpe...  11.6 us

profile of v4, /device:TPU:0, one launch (start us, length us, event | category | flops | bytes accessed | tf_op | source)
XLA Modules:
  0.0 275.3 jit_solution(4093957041492281853)
XLA Ops:
  0.6 1.4 reshape.24.lab_ref
  2.0 0.9 copy.20.proj_ref
  2.9 1.1 copy.21.fc2_ref
  4.0 0.0 copy-start.4
  4.0 1.1 copy-done.4
  5.2 0.0 copy-start.10
  5.2 0.9 copy-done.10
  6.1 0.0 copy-start.12
  6.1 0.9 copy-done.12
  7.0 0.0 copy-start.14
  7.0 0.9 copy-done.14
  7.8 33.6 %kernel_w.1 = (bf16[2,512,1024]{2,1,0:T(8,128)(2,1)S(1)}, f32[16,392,392]{2,1,0:T(8,128)}, bf16[32,2048]{1,0:T(8,128)(2,1)S(1)}, s32[392,512]{1,0:T(8,128)S(1)}) custom-call(f32[3,32,256]{2,1,0:T(8,128)S(1)} %copy-done.12, f32[256,32]{1,0:T(8,128)S(1)} %copy.20.proj_ref, f32[32,1024]{1,0:T(8,128)S(1)} %copy-done.10, f32[1024,32]{1,0:T(8,128)S(1)} %copy.21.fc2_ref, ...), custom_call_target="tpu_custom_call" | custom-call | tf_op jit(solution)/shard_map/kernel_w/pallas_call | solution.py:465
  41.4 0.0 copy-start
  41.4 1.3 copy-done
  42.8 0.0 copy-start.5
  42.8 0.9 copy-done.5
  43.6 0.0 copy-start.9
  43.6 0.7 copy-done.9
  44.3 103.4 %kernel_a2.1 = (bf16[4,3,392,512]{3,2,1,0:T(8,128)(2,1)}, f32[4,392,512]{2,1,0:T(8,128)}, bf16[4,16,392,392]{3,2,1,0:T(8,128)(2,1)}, f32[4,392,512]{2,1,0:T(8,12...) custom-call(f32[3136,512]{1,0:T(8,128)} %in_ref.1, ...), custom_call_target="tpu_custom_call" | custom-call | tf_op jit(solution)/shard_map/kernel_a2/pallas_call | solution.py:667
  147.7 104.1 %kernel_bc.1 = (bf16[8,400,512]{2,1,0:T(8,128)(2,1)}, bf16[208,512]{1,0:T(8,128)(2,1)}, bf16[2,400,512]{2,1,0:T(8,128)(2,1)}, bf16[208,512]{1,0:T(8,128)(2,1)}, ...) custom-call(f32[4,392,512]{2,1,0:T(8,128)} %get-tuple-element.36.x_ref, ...), custom_call_target="tpu_custom_call" | custom-call | tf_op jit(solution)/shard_map/kernel_bc/pallas_call | solution.py:925
  251.9 0.0 copy-start.1
  251.9 1.9 copy-done.1
  253.8 0.0 copy-start.2
  253.8 1.9 copy-done.2
  255.7 0.0 copy-start.3
  255.7 1.1 copy-done.3
  256.9 0.0 copy-start.6
  256.9 1.0 copy-done.6
  257.8 0.0 copy-start.7
  257.8 0.9 copy-done.7
  258.8 0.0 copy-start.8
  258.8 0.9 copy-done.8
  259.7 0.0 copy-start.11
  259.7 0.9 copy-done.11
  260.6 0.0 copy-start.13
  260.6 0.9 copy-done.13
  261.5 0.0 copy-start.15
  261.5 0.7 copy-done.15
  262.2 11.6 %kernel_f.1 = (f32[3136,512]{1,0:T(8,128)}, f32[3136,512]{1,0:T(8,128)}, f32[3,32,256]{2,1,0:T(8,128)}, f32[256,32]{1,0:T(8,128)S(1)}, f32[32,1024]{1,0:T(8,128)...) custom-call(f32[3136,512]{1,0:T(8,128)} %in_ref.1, f32[3136,512]{1,0:T(8,128)} %og_ref.1, ...), custom_call_target="tpu_custom_call" | custom-call | tf_op jit(solution)/shard_map/kernel_f/pallas_call | solution.py:964
  273.8 0.7 copy.22
  274.5 0.8 copy.23
Async XLA Ops:
  4.0 1.1 copy-start.4
  5.2 0.9 copy-start.10
  6.1 0.9 copy-start.12
  7.0 0.9 copy-start.14
  41.4 1.3 copy-start
  42.8 0.9 copy-start.5
  43.6 0.7 copy-start.9
  251.9 1.9 copy-start.1
  253.8 1.9 copy-start.2
  255.7 1.1 copy-start.3
  256.9 1.0 copy-start.6
  257.8 0.9 copy-start.7
  258.8 0.9 copy-start.8
  259.7 0.9 copy-start.11
  260.6 0.9 copy-start.13
  261.5 0.7 copy-start.15

commit v5 on v4

--- a/solution.py
+++ b/solution.py
@@ -149,8 +149,8 @@
 
 def full(shape,**kw):
     return pl.BlockSpec(shape,lambda w:(0,)*len(shape),**kw)
-def per(shape):
-    return pl.BlockSpec((1,)+shape,lambda w:(w,)+(0,)*len(shape))
+def per(shape,**kw):
+    return pl.BlockSpec((1,)+shape,lambda w:(w,)+(0,)*len(shape),**kw)
 ONE=pl.Buffered(1)
 ANY=pl.BlockSpec(memory_space=pl.ANY)
 
@@ -392,7 +392,7 @@
     z,x,c,y=place_of()
     cq=qkv_ref.shape[2]; cf=fc1_ref.shape[1]
     for k in range(3): wq_s[:,k*cq:(k+1)*cq]=qkv_ref[k].astype(BF)
-    wq_s[:,3*cq:4*cq]=proj_ref[...].T.astype(BF)
+    wq_s[:,3*cq:4*cq]=proj_ref[...].astype(BF)
     half,T=tab_ref.shape
     tb[2]=jnp.zeros(tb.shape[1:],F32)
     tb[2,:,0:T]=tab_ref[...]
@@ -403,7 +403,7 @@
     gather.start()
     tb[y]=tb[2]
     wf_ref[:,0:cf]=fc1_ref[...].astype(BF)
-    wf_ref[:,cf:2*cf]=fc2_ref[...].T.astype(BF)
+    wf_ref[:,cf:2*cf]=fc2_ref[...].astype(BF)
     WIN=bias_s.shape[-1]; tiles=-(-WIN//128); n=tb.shape[2]//128
     posT_ref[...]=jnp.full(posT_ref.shape,1<<15,jnp.int32)
     posT_ref[:,0:WIN]=pos_ref[...].astype(F32).T.astype(jnp.int32)
@@ -459,15 +459,14 @@
 
 def call_w(w_qkv,w_proj,w_fc1,w_fc2,pos_index,rel_table):
     rows,cq=w_qkv.shape[1:]; cf=w_fc1.shape[1]; WIN=pos_index.shape[0]; half,T=rel_table.shape; dma=pltpu.SemaphoreType.DMA
-    wide=-(-WIN//128)*128; n=-(-T//128); v=pltpu.VMEM
+    wide=-(-WIN//128)*128; n=-(-T//128); mem=pltpu.VMEM
     sd=jax.ShapeDtypeStruct
-    vm=pl.BlockSpec(memory_space=pltpu.VMEM)
-    return pl.pallas_call(kernel_w,
+    return pl.pallas_call(kernel_w,grid=(1,),
       out_shape=[sd((2,16*rows,4*cq),BF),sd((2*half,WIN,WIN),F32),sd((rows,2*cf),BF),sd((WIN,wide),jnp.int32)],
-      in_specs=[vm]*6,out_specs=[ANY,ANY,vm,vm],
-      scratch_shapes=[v((half,WIN,WIN),F32),v((rows,4*cq),BF),v((3,half,n*128),F32),v((half//2,n*128),jnp.int32)]
+      in_specs=[full(v.shape) for v in (w_qkv,w_proj,w_fc1,w_fc2,pos_index,rel_table)],out_specs=[ANY,ANY,full((rows,2*cf)),full((WIN,wide))],
+      scratch_shapes=[mem((half,WIN,WIN),F32),mem((rows,4*cq),BF),mem((3,half,n*128),F32),mem((half//2,n*128),jnp.int32)]
         +gather_sems()+[dma((STEPS,)),dma((STEPS,)),dma((STEPS,)),dma((2,))],
-      compiler_params=pltpu.CompilerParams(vmem_limit_bytes=40*1024*1024,collective_id=1,has_side_effects=True),name="kernel_w")(w_qkv,w_proj,w_fc1,w_fc2,pos_index,rel_table)
+      compiler_params=pltpu.CompilerParams(vmem_limit_bytes=63*1024*1024,collective_id=1,has_side_effects=True),name="kernel_w")(w_qkv,w_proj,w_fc1,w_fc2,pos_index,rel_table)
 
 def neighbours(z,x,c,y):
     s=(z*2+x)*2+c
@@ -675,89 +674,156 @@
       name="kernel_a2")(inputs,og,wf,lab,bias,W1,gains,shifts)
 
 class Reduce:
-    def __init__(self,src,out,own,r1,r2,ss,rs,ls,r3,fin,r4):
-        self.src,self.out,self.own,self.r1,self.r2,self.r3,self.fin,self.r4=src,out,own,r1,r2,r3,fin,r4
+    def __init__(self,src,out,own,r1,r2,ss,rs,ls,r3,fin,r4,r5):
+        self.src,self.out,self.own,self.r1,self.r2,self.r3,self.fin,self.r4,self.r5=src,out,own,r1,r2,r3,fin,r4,r5
         self.ss,self.rs,self.ls=ss,rs,ls
         self.at=place_of()
-        self.mid=own.at[self.at[1]]
+    def put(self,src,dst,k,to):
+        return send(src,dst,self.ss.at[k],self.rs.at[k],to)
     def mine(self,k):
         return pltpu.make_async_copy(self.src.at[k%2,:,k//2,self.at[2]],self.own.at[k//2,:,k%2],self.ls.at[k])
     def theirs(self,k):
         z,x,c,y=self.at
-        return send(self.src.at[k%2,:,k//2,1-c],self.r1.at[k//2,:,k%2],self.ss.at[k],self.rs.at[k],dev(z,x,1-c,y))
-    def xsend(self):
-        z,x,c,y=self.at
-        return send(self.own.at[1-x],self.r2,self.ss.at[4],self.rs.at[4],dev(z,1-x,c,y))
-    def zsend(self,i):
+        return self.put(self.src.at[k%2,:,k//2,1-c],self.r1.at[k//2,:,k%2],k,dev(z,x,1-c,y))
+    def kept(self,b):
+        z,x,c,y=self.at
+        return x*(1-c)+b*c,b*(1-c)+y*c
+    def first(self,b):
+        z,x,c,y=self.at
+        at=self.own.at[(1-x)*(1-c)+b*c,:,b*(1-c)+(1-y)*c]
+        return self.put(at,self.r2.at[:,b],4+b,dev(z,x+(1-2*x)*(1-c),c,y+(1-2*y)*c))
+    def zboth(self,i):
         z,x,c,y=self.at
         zz=(z+i)%4
-        return send(self.mid.at[zz],self.r3.at[i-1],self.ss.at[4+i],self.rs.at[4+i],dev(zz,x,c,y))
-    def ysend(self):
-        z,x,c,y=self.at
-        return send(self.fin.at[1-y],self.r4,self.ss.at[8],self.rs.at[8],dev(z,x,c,1-y))
+        return self.put(self.own.at[x,zz],self.r3.at[i-1],5+i,dev(zz,x,c,y))
+    def zone(self,i):
+        z,x,c,y=self.at
+        zz=(z+i)%4
+        return self.put(self.own.at[x,zz,y],self.r3.at[i-1,0],5+i,dev(zz,x,c,y))
+    def ylast(self):
+        z,x,c,y=self.at
+        return self.put(self.fin.at[1-y],self.r4,9,dev(z,x,c,1-y))
+    def xsecond(self):
+        z,x,c,y=self.at
+        return self.put(self.own.at[1-x,:,y],self.r5,9,dev(z,1-x,c,y))
     def start(self):
         for k in range(4):
             self.theirs(k).start(); self.mine(k).start()
     def add(self,dst,*srcs):
         total=srcs[0][...].astype(F32)
         for s in srcs[1:]: total=total+s[...].astype(F32)
-        dst[...]=total.astype(BF)
+        dst[...]=total.astype(dst.dtype)
+    def by_core(self,zero,one):
+        c=self.at[2]
+        pl.when(c==0)(zero)
+        pl.when(c==1)(one)
     def one(self):
         z,x,c,y=self.at
         for k in range(4):
             self.mine(k).wait(); self.theirs(k).wait_recv()
-        def step(xx):
-            def add(k,_):
-                at=(xx,k//2,k%2)
-                self.add(self.own.at[at],self.own.at[at],self.r1.at[at])
-                return 0
-            lax.fori_loop(0,8,add,0)
-        step(1-x)
-        self.xsend().start()
-        step(x)
-    def summed(self):
-        z,x,c,y=self.at
-        def add(k,_):
-            at=(k//2,k%2)
-            self.add(self.own.at[(x,)+at],self.own.at[(x,)+at],self.r2.at[at])
+        def step(k,_):
+            self.add(self.own.at[k//8,(k//2)%4,k%2],self.own.at[k//8,(k//2)%4,k%2],self.r1.at[k//8,(k//2)%4,k%2])
             return 0
-        lax.fori_loop(0,8,add,0)
-    def left(self):
+        lax.fori_loop(0,16,step,0)
+        for b in range(2): self.first(b).start()
+    def two(self):
+        z,x,c,y=self.at
+        for b in range(2): self.first(b).wait_recv()
+        def step(k,_):
+            zz,b=k//2,k%2
+            p,q=self.kept(b)
+            self.add(self.own.at[p,zz,q],self.own.at[p,zz,q],self.r2.at[zz,b])
+            return 0
+        lax.fori_loop(0,8,step,0)
+        def zero():
+            for i in (2,1,3): self.zboth(i).start()
+        self.by_core(zero,lambda: self.xsecond().start())
+    def three(self):
+        z,x,c,y=self.at
+        def zero():
+            for i in (1,2,3): self.zboth(i).wait_recv()
+            for yy in (1-y,y):
+                self.add(self.fin.at[yy],self.own.at[x,z,yy],*[self.r3.at[i,yy] for i in range(3)])
+                if yy is not y: self.ylast().start()
+        def one():
+            self.xsecond().wait_recv()
+            for zz in range(4):
+                self.add(self.own.at[x,zz,y],self.own.at[x,zz,y],self.r5.at[zz])
+            for i in (2,1,3): self.zone(i).start()
+        self.by_core(zero,one)
+    def four(self):
+        z,x,c,y=self.at
+        def zero():
+            self.ylast().wait_recv()
+            self.add(self.out,self.fin.at[y],self.r4)
+            for i in (1,2,3): self.zboth(i).wait_send()
+            self.ylast().wait_send()
+        def one():
+            for i in (1,2,3): self.zone(i).wait_recv()
+            self.add(self.out,self.own.at[x,z,y],*[self.r3.at[i,0] for i in range(3)])
+            for i in (1,2,3): self.zone(i).wait_send()
+            self.xsecond().wait_send()
+        self.by_core(zero,one)
         for k in range(4): self.theirs(k).wait_send()
-        self.xsend().wait_send()
-    def zstart(self):
-        for i in (2,1,3): self.zsend(i).start()
-    def two(self):
-        self.xsend().wait_recv()
-        self.summed()
-        self.zstart()
-    def three(self):
-        z,x,c,y=self.at
-        for i in (1,2,3):
-            self.zsend(i).wait_recv()
-        def step(yy):
-            self.add(self.fin.at[yy],self.mid.at[z,yy],*[self.r3.at[i,yy] for i in range(3)])
-        step(1-y)
-        self.ysend().start()
-        step(y)
-    def four(self):
-        z,x,c,y=self.at
-        self.ysend().wait_recv()
-        self.out[...]=self.fin[y].astype(F32)+self.r4[...].astype(F32)
-        self.left()
-        for i in (1,2,3): self.zsend(i).wait_send()
-        self.ysend().wait_send()
+        for b in range(2): self.first(b).wait_send()
 
 def reduce_scratch(rows,cols):
     v=lambda *d: pltpu.VMEM(d+(rows,cols),BF); dma=pltpu.SemaphoreType.DMA
-    return [v(2,4,2),v(2,4,2),v(4,2),dma((9,)),dma((9,)),dma((4,)),v(3,2),v(2),v()]
-
+    return [v(2,4,2),v(2,4,2),v(4,2),dma((10,)),dma((10,)),dma((4,)),v(3,2),v(2),v(),v(4)]
+
+class Sums:
+    def __init__(self,slabs,got,res,ss,rs,ts,us):
+        self.slabs,self.got,self.res,self.ss,self.rs,self.ts,self.us=slabs,got,res,ss,rs,ts,us
+        z,x,c,y=place_of()
+        self.s=(z*2+x)*2+c; self.y=y; self.n=slabs.shape[1]
+    def part(self,k,yy):
+        me=self.y*16+self.s
+        return send(self.slabs.at[yy,k],self.got.at[me],self.ss.at[yy*self.n+k],self.rs.at[me],(k,yy))
+    def other(self,k,yy):
+        return jnp.logical_or(self.s!=k,self.y!=yy)
+    def scatter(self):
+        for k in range(self.n):
+            for yy in range(2):
+                @pl.when(self.other(k,yy))
+                def _(): self.part(k,yy).start()
+    def back(self,to,k):
+        return send(self.res.at[k],self.res.at[k],self.ts.at[to],self.us.at[k],(to,self.y))
+    def collect(self):
+        me=self.y*16+self.s
+        @pl.when(self.s<self.n)
+        def _():
+            self.got[me]=self.slabs[self.y,self.s]
+            def wait(i,_):
+                @pl.when(i!=me)
+                def _():
+                    send(self.slabs.at[0,0],self.got.at[i],self.ss.at[0],self.rs.at[i],(self.s,1-self.y)).wait_recv()
+                return 0
+            lax.fori_loop(0,32,wait,0)
+            total=self.got[0]
+            for i in range(1,32): total=total+self.got[i]
+            self.res[self.s]=total
+            for to in range(16):
+                @pl.when(self.s!=to)
+                def _(): self.back(to,self.s).start()
+    def finish(self):
+        for k in range(self.n):
+            @pl.when(self.s!=k)
+            def _(): self.back(k,k).wait_recv()
+        @pl.when(self.s<self.n)
+        def _():
+            for to in range(16):
+                @pl.when(self.s!=to)
+                def _(): self.back(to,self.s).wait_send()
+        for k in range(self.n):
+            for yy in range(2):
+                @pl.when(self.other(k,yy))
+                def _(): self.part(k,yy).wait_send()
 
 def kernel_bc(nheads,x_ref,gln2_ref,qkv_ref,g_ref,gT_ref,D_ref,P_ref,W1,gains_ref,shifts_ref,sm_ref,pos_ref,dcat_hbm,dlast_hbm,
               ev_hbm,hd_hbm,evl_hbm,hdl_hbm,redq_ref,redm_ref,tab_ref,sum_ref,
-              G_s,Gx,aq,dq_s,kT_s,gq_s,gqT_s,dd_s,small_ref,acc,tk,tr,tu,sr,
-              gs,gr_,dl,ds,dr,es,er,us,ts,tq_,
-              own,r1,r2,ss,rs,ls,r3,fin,r4,own2,p1,p2,ss2,rs2,ls2,p3,fin2,p4):
+              G_s,Gx,aq,dq_s,kT_s,gq_s,gqT_s,dd_s,small_ref,acc,slabs,got,res,
+              gs,gr_,dl,ds,dr,es,er,us,ss0,rs0,ts0,us0,
+              own,r1,r2,ss,rs,ls,r3,fin,r4,r5,own2,p1,p2,ss2,rs2,ls2,p3,fin2,p4,p5):
     w=pl.program_id(0); nw=dd_s.shape[0]
     z,xc,c,y=place_of()
     s=(z*2+xc)*2+c
@@ -766,8 +832,8 @@
     cq=D//2
     groups=nheads//PER
     tiles=G_s.shape[0]; part=Gx.shape[1]//nheads
-    big=Reduce(dcat_hbm,redm_ref,own2,p1,p2,ss2,rs2,ls2,p3,fin2,p4)
-    red=Reduce(dq_s,redq_ref,own,r1,r2,ss,rs,ls,r3,fin,r4)
+    big=Reduce(dcat_hbm,redm_ref,own2,p1,p2,ss2,rs2,ls2,p3,fin2,p4,p5)
+    red=Reduce(dq_s,redq_ref,own,r1,r2,ss,rs,ls,r3,fin,r4,r5)
     def slab(k,to=None):
         at=ev_hbm.at[y*nw+k]
         if to is None: return pltpu.make_async_copy(dd_s.at[k],at,dl.at[k])
@@ -785,7 +851,7 @@
         return send(G_s.at[:,pl.ds(r,part)],Gx.at[:,pl.ds(pl.multiple_of(h*part,8),part)],gs.at[h],gr_.at[h],sib)
     @pl.when(w==0)
     def _():
-        greet(peers_of(z,xc,c,y)+neighbours(z,xc,c,y))
+        greet([((s+t)%16,yy) for t in range(1,16) for yy in (y,1-y)]+[mate])
         big.start()
         early(0).start(); early(1).start()
         @pl.when(y==1)
@@ -846,7 +912,8 @@
     small_ref[0:1,:]+=jnp.sum(gr*xhat,axis=0,keepdims=True)
     small_ref[2:3,:]+=jnp.sum(gr,axis=0,keepdims=True)
     pl.when(w==0)(big.one)
-    pl.when(w==nw-2)(big.two)
+    pl.when(w==nw//2-1)(big.two)
+    pl.when(w==nw-2)(big.three)
     @pl.when(w==nw-1)
     def _():
         for h in range(nheads): trade(h).wait()
@@ -869,44 +936,26 @@
             acc[...]+=tot.reshape(acc.shape)
             return 0
         n=part//8
-        lax.fori_loop(c,n*3//25,rows,0)
+        lax.fori_loop(c,n*4//25,rows,0)
         red.one()
-        lax.fori_loop(n*3//25,n*13//25,rows,0)
+        lax.fori_loop(n*4//25,n*11//25,rows,0)
         red.two()
-        lax.fori_loop(n*13//25,n*19//25,rows,0)
-        big.three()
-        lax.fori_loop(n*19//25,n,rows,0)
+        lax.fori_loop(n*11//25,n*18//25,rows,0)
+        red.three()
+        lax.fori_loop(n*18//25,n,rows,0)
+        half=nheads//2
+        for yy in range(2):
+            for k in range(nh): slabs[yy,k]=acc[k,yy*half:(yy+1)*half]
+            for k in range(2): slabs[yy,nh+k]=small_ref[:,k*256:(k+1)*256]
+        sums=Sums(slabs,got,res,ss0,rs0,ts0,us0)
+        sums.scatter()
+        red.four()
+        sums.collect()
         big.four()
-        half=nheads//2; nb=nh//2
-        def pair(k,src,dst,to):
-            return [send(src,dst,ts.at[2*k],tq_.at[2*k],to),send(sr.at[6+min(k,3)],sr.at[k],ts.at[2*k+1],tq_.at[2*k+1],to)]
-        def run(cps):
-            for p in cps: p.start()
-            for p in cps: p.wait()
-        sr[6]=small_ref[...]
-        run(pair(0,acc.at[:,pl.ds(pl.multiple_of((1-y)*half,8),half)],tu.at[0],mate))
-        tu[1]=acc[:,pl.ds(pl.multiple_of(y*half,8),half)]+tu[0]
-        sr[7]=sr[6]+sr[0]
-        run(pair(1,tu.at[1,pl.ds((1-c)*nb,nb)],tr.at[0],sib))
-        tk[0]=tu[1,pl.ds(c*nb,nb)]+tr[0]
-        sr[8]=sr[7]+sr[1]
-        run(pair(2,tk.at[0],tr.at[1],dev(z,1-xc,c,y)))
-        tk[1]=tk[0]+tr[1]
-        sr[9]=sr[8]+sr[2]
-        cps=[]
-        for k in (1,2,3):
-            cps+=pair(2+k,tk.at[1],tr.at[1+k],dev((z+k)%4,xc,c,y))
-        run(cps)
-        red.three()
-        tu[2,pl.ds(c*nb,nb)]=tk[1]+tr[2]+tr[3]+tr[4]
-        sum_ref[...]=sr[9]+sr[3]+sr[4]+sr[5]
-        cp=send(tu.at[2,pl.ds(c*nb,nb)],tu.at[2,pl.ds(c*nb,nb)],ts.at[12],tq_.at[12],sib)
-        cp.start()
-        red.four()
-        cp.wait_send()
-        send(tu.at[2,pl.ds((1-c)*nb,nb)],tu.at[2,pl.ds((1-c)*nb,nb)],ts.at[12],tq_.at[12],sib).wait_recv()
+        sums.finish()
         for m in range(nh):
-            tab_ref[:,m*256:(m+1)*256]=tu[2,m]
+            tab_ref[:,m*256:(m+1)*256]=res[m]
+        for k in range(2): sum_ref[:,k*256:(k+1)*256]=res[nh+k]
         for k in range(nw):
             slab(k).wait(); slab(k,mate).wait()
         @pl.when(y==1)
@@ -919,17 +968,17 @@
     nW,WIN,D=x.shape; NH=Dd.shape[1]
     cq=D//2; tiles=-(-WIN//128); SLAB=-(-WIN//16)*16; EDGE=-(-(SLAB-WIN//2)//16)*16
     part=-(-WIN//16)*8
-    nh=-(-T//256); nh+=nh%2
+    nh=-(-T//256)
     rows,more=dcat.shape[-2:]; cols=3*cq
     sd=jax.ShapeDtypeStruct; dma=pltpu.SemaphoreType.DMA; v=pltpu.VMEM
     return pl.pallas_call(functools.partial(kernel_bc,NH),grid=(nW,),
-      in_specs=[per((WIN,D)),per((WIN,D)),per((3,WIN,D)),per((WIN,D)),per((D,WIN)),per((NH,WIN)),per((NH,WIN,WIN)),
+      in_specs=[per((WIN,D)),per((WIN,D),pipeline_mode=ONE),per((3,WIN,D)),per((WIN,D)),per((D,WIN)),per((NH,WIN)),per((NH,WIN,WIN)),
         full((2,D,cols),pipeline_mode=ONE),full(gains.shape),full(shifts.shape),full(sm.shape),full(pp.shape,pipeline_mode=ONE),ANY,ANY],
-      out_specs=[ANY,ANY,ANY,ANY,full((rows,cols)),full((rows,more)),full((NH//2,nh*256)),full(sm.shape)],
+      out_specs=[ANY,ANY,ANY,ANY,full((rows,cols),pipeline_mode=ONE),full((rows,more),pipeline_mode=ONE),full((NH//2,nh*256),pipeline_mode=ONE),full(sm.shape)],
       out_shape=[sd((2*nW,SLAB,D),BF),sd((EDGE,D),BF),sd((2,SLAB,D),BF),sd((EDGE,D),BF),sd((rows,cols),F32),sd((rows,more),F32),sd((NH//2,nh*256),F32),sd(sm.shape,F32)],
       scratch_shapes=[v((tiles,NH*WIN,128),F32),v((tiles,NH*part,128),F32),v((2,D,cols),F32),v((2,4,2,2,rows,cols),BF),v((D,WIN),BF),v((3,WIN,D),BF),v((D,WIN),F32),
-        v((nW,SLAB,D),BF),v(sm.shape,F32),v((nh,NH,256),F32),v((2,nh//2,NH//2,256),F32),v((5,nh//2,NH//2,256),F32),v((3,nh,NH//2,256),F32),v((10,)+sm.shape,F32),
-        dma((NH,)),dma((NH,)),dma((nW,)),dma((nW,)),dma((nW,)),dma((2,)),dma,dma((6,)),dma((13,)),dma((13,))]+reduce_scratch(rows,cols)+reduce_scratch(rows,more),
+        v((nW,SLAB,D),BF),v(sm.shape,F32),v((nh,NH,256),F32),v((2,nh+2,8,256),F32),v((32,8,256),F32),v((nh+2,8,256),F32),
+        dma((NH,)),dma((NH,)),dma((nW,)),dma((nW,)),dma((nW,)),dma((2,)),dma,dma((6,)),dma((2*nh+4,)),dma((32,)),dma((16,)),dma((nh+2,))]+reduce_scratch(rows,cols)+reduce_scratch(rows,more),
       compiler_params=pltpu.CompilerParams(vmem_limit_bytes=63*1024*1024,dimension_semantics=("arbitrary",),collective_id=3,has_side_effects=True),
       name="kernel_bc")(x,gln2,qkv,g,gT,Dd,Pp,W1,gains,shifts,sm,pp,dcat,dlast)
 
@@ -945,9 +994,9 @@
         end_s[0]=hd_ref[...].astype(F32); end_s[1]=hd2_ref[...].astype(F32)
         cq=dqkv_ref.shape[2]; cf=dfc1_ref.shape[1]
         for k in range(3): dqkv_ref[k]=redq_ref[:,k*cq:(k+1)*cq]
-        dproj_ref[...]=redm_ref[:,0:cq].T
+        dproj_ref[...]=redm_ref[:,0:cq]
         dfc1_ref[...]=redm_ref[:,cq:cq+cf]
-        dfc2_ref[...]=redm_ref[:,cq+cf:].T
+        dfc2_ref[...]=redm_ref[:,cq+cf:]
         dgain_ref[...]=sum_ref[0:2,:]; dshift_ref[...]=sum_ref[2:6,:]
         dtab_ref[...]=tab_ref[:,0:dtab_ref.shape[1]]
     e=jnp.where(j%nw==nw-1,evl_ref[0],ev_ref[0]).astype(F32)
@@ -960,13 +1009,13 @@
     tok,D=inputs.shape; n,SLAB,_=ev.shape; WIN=tok//n; rows=redq.shape[0]
     sd=jax.ShapeDtypeStruct
     blk=pl.BlockSpec((WIN,D),lambda j:(j,0)); slab=pl.BlockSpec((1,SLAB,D),lambda j:(j,0,0))
-    shapes=[(3,rows,cq),(cq,rows),(rows,cf),(cf,rows),(2,D),(4,D),(tab.shape[0],T)]
+    shapes=[(3,rows,cq),(rows,cq),(rows,cf),(rows,cf),(2,D),(4,D),(tab.shape[0],T)]
     return pl.pallas_call(kernel_f,grid=(n,),
       in_specs=[blk,blk,slab,pl.BlockSpec((1,SLAB,D),lambda j:(j//(n//2),0,0)),slab]+[full(v.shape) for v in (hd,hd2,redq,redm,tab,small)],
       out_specs=[blk,blk]+[full(v) for v in shapes],
       out_shape=[sd((tok,D),F32),sd((tok,D),F32)]+[sd(v,F32) for v in shapes],
       scratch_shapes=[pltpu.VMEM((2,)+hd.shape,F32)],
-      compiler_params=pltpu.CompilerParams(vmem_limit_bytes=40*1024*1024,dimension_semantics=("arbitrary",)),
+      compiler_params=pltpu.CompilerParams(vmem_limit_bytes=63*1024*1024,dimension_semantics=("arbitrary",)),
       name="kernel_f")(inputs,og,ev,evl,ev2,hd,hd2,redq,redm,tab,small)
 
 def gathered(piece,names,nseq,nheads):
@@ -1012,10 +1061,11 @@
     rows=w_qkv.shape[1]; cq=w_qkv.shape[2]; cf=w_fc1.shape[1]
     lab=region.reshape(-1,WIN)
     if linked:
-        W1,bias,wf,posT=call_w(w_qkv,w_proj,w_fc1,w_fc2,pos_index,rel_table)
+        W1,bias,wf,posT=call_w(w_qkv,w_proj.T,w_fc1,w_fc2.T,pos_index,rel_table)
         qkv,x,Pp,gln2,g,gT,Dd,ev,dlast,dcat,sm=call_a2(inputs,out_grad,wf,lab,bias,W1,gains,shifts)
         ev2,hd2,evl,hd,redq,redm,d_table,small=call_bc(x,gln2,qkv,g,gT,Dd,Pp,W1,gains,shifts,sm,posT,dcat.reshape(2,4,2,2,rows,-1),dlast,T)
-        return tuple(call_f(inputs,out_grad,ev,evl,ev2,hd,hd2,redq,redm,d_table,small,cq,cf,T))
+        out,din,dq,dp,d1,d2,dg,dsh,dt=call_f(inputs,out_grad,ev,evl,ev2,hd,hd2,redq,redm,d_table,small,cq,cf,T)
+        return (out,din,dq,dp.T,d1,d2.T,dg,dsh,dt)
     posT=pos_index.T
     wide=-(-WIN//128)*128
     posP=jnp.pad(posT,((0,0),(0,wide-WIN)))

time: 276 us -> 269 us (0.975)
  local copies, waits for them, and re-layouts: 21.9 us -> 1.41 us
  Pallas kernels: 253 us -> 266 us
    unnamed x34 -> x0, local copies, waits for them, and re-layouts: 18.9 us -> none
    pallas_call x1, Pallas kernels: 104 us -> 114 us  [call_bc(): pl.pallas_call(functools.partial(kernel_bc, NH), grid=(nW,), in_specs=[pe...]
where the time goes in v5:
time: 269 us; the launch traced here: 268 us
  Pallas kernels  266 us (99%)
    pallas_call x1, Pallas kernels, call_bc(): pl.pallas_call(functools.partial(kernel_bc, NH), grid=(nW,), in_specs=[pe...  114 us
    pallas_call x1, Pallas kernels, call_a2(): pl.pallas_call(functools.partial(kernel_a2, NH), grid=(2 * nW,), in_specs...  103 us
    pallas_call x1, Pallas kernels, call_w(): pl.pallas_call(kernel_w, grid=(1,), out_shape=[sd((2, 16 * rows, 4 * cq),...  35.8 us
    pallas_call x1, Pallas kernels, call_f(): pl.pallas_call(kernel_f, grid=(n,), in_specs=[blk, blk, slab, pl.BlockSpe...  13.4 us

profile of v5, /device:TPU:0, one launch (start us, length us, event | category | flops | bytes accessed | tf_op | source)
XLA Modules:
  0.0 268.4 jit_solution(3369824759293672883)
XLA Ops:
  0.6 1.4 reshape.24.lab_ref
  2.0 35.8 %kernel_w.1 = (bf16[2,512,1024]{2,1,0:T(8,128)(2,1)}, f32[16,392,392]{2,1,0:T(8,128)}, bf16[32,2048]{1,0:T(8,128)(2,1)}, s32[392,512]{1,0:T(8,128)}) custom-call(f32[3,32,256]{2,1,0:T(8,128)} %qkv_ref.1, f32[32,256]{1,0:T(8,128)} %bitcast.7, f32[32,1024]{1,0:T(8,128)} %fc1_ref.1, f32[32,1024]{1,0:T(8,128)} %bitcast.6, s32[392,392]{1,0:T(8,128)} %pos_ref.1, ...), custom_call_target="tpu_custom_call" | custom-call | tf_op jit(solution)/shard_map/kernel_w/pallas_call | solution.py:464
  37.9 103.3 %kernel_a2.1 = (bf16[4,3,392,512]{3,2,1,0:T(8,128)(2,1)}, f32[4,392,512]{2,1,0:T(8,128)}, bf16[4,16,392,392]{3,2,1,0:T(8,128)(2,1)}, f32[4,392,512]{2,1,0:T(8,12...) custom-call(f32[3136,512]{1,0:T(8,128)} %in_ref.1, ...), custom_call_target="tpu_custom_call" | custom-call | tf_op jit(solution)/shard_map/kernel_a2/pallas_call | solution.py:666
  141.2 113.6 %kernel_bc.1 = (bf16[8,400,512]{2,1,0:T(8,128)(2,1)}, bf16[208,512]{1,0:T(8,128)(2,1)}, bf16[2,400,512]{2,1,0:T(8,128)(2,1)}, bf16[208,512]{1,0:T(8,128)(2,1)}, ...) custom-call(f32[4,392,512]{2,1,0:T(8,128)} %get-tuple-element.45.x_ref, ...), custom_call_target="tpu_custom_call" | custom-call | tf_op jit(solution)/shard_map/kernel_bc/pallas_call | solution.py:974
  254.8 13.4 %kernel_f.1 = (f32[3136,512]{1,0:T(8,128)}, f32[3136,512]{1,0:T(8,128)}, f32[3,32,256]{2,1,0:T(8,128)}, f32[32,256]{1,0:T(8,128)}, f32[32,1024]{1,0:T(8,128)}, /...) custom-call(f32[3136,512]{1,0:T(8,128)} %in_ref.1, f32[3136,512]{1,0:T(8,128)} %og_ref.1, ...), custom_call_target="tpu_custom_call" | custom-call | tf_op jit(solution)/shard_map/kernel_f/pallas_call | solution.py:1013

commit v6 on v5

--- a/solution.py
+++ b/solution.py
@@ -319,11 +319,17 @@
 def peers_of(z,x,c,y):
     return [dev(z,x,1-c,y),dev(z,1-x,c,y),dev(z,x,c,1-y)]+[dev((z+i)%4,x,c,y) for i in (1,2,3)]
 
-def greet(devices):
+def hail(devices):
     bar=pltpu.get_barrier_semaphore()
     for d in devices:
         pl.semaphore_signal(bar,inc=1,device_id=d,device_id_type=MESHID)
-    pl.semaphore_wait(bar,len(devices))
+
+def heard(devices):
+    pl.semaphore_wait(pltpu.get_barrier_semaphore(),len(devices))
+
+def greet(devices):
+    hail(devices)
+    heard(devices)
 
 def send(src,dst,ss,rs,to):
     return pltpu.make_async_remote_copy(src_ref=src,dst_ref=dst,send_sem=ss,recv_sem=rs,device_id=to,device_id_type=MESHID)
@@ -674,38 +680,29 @@
       name="kernel_a2")(inputs,og,wf,lab,bias,W1,gains,shifts)
 
 class Reduce:
-    def __init__(self,src,out,own,r1,r2,ss,rs,ls,r3,fin,r4,r5):
-        self.src,self.out,self.own,self.r1,self.r2,self.r3,self.fin,self.r4,self.r5=src,out,own,r1,r2,r3,fin,r4,r5
+    def __init__(self,src,out,own,r1,bufs,ss,rs,ls):
+        self.src,self.out,self.own,self.r1,self.bufs=src,out,own,r1,bufs
         self.ss,self.rs,self.ls=ss,rs,ls
-        self.at=place_of()
-    def put(self,src,dst,k,to):
-        return send(src,dst,self.ss.at[k],self.rs.at[k],to)
+        z,x,c,y=place_of()
+        self.x,self.c,self.y,self.h,self.l=x,c,y,z//2,z%2
+    def to(self,x=None,h=None,l=None,c=None,y=None):
+        pick=lambda new,old: old if new is None else new
+        return dev(pick(h,self.h)*2+pick(l,self.l),pick(x,self.x),pick(c,self.c),pick(y,self.y))
     def mine(self,k):
-        return pltpu.make_async_copy(self.src.at[k%2,:,k//2,self.at[2]],self.own.at[k//2,:,k%2],self.ls.at[k])
+        return pltpu.make_async_copy(self.src.at[k%2,:,:,k//2,self.c],self.own.at[k//2,:,:,k%2],self.ls.at[k])
     def theirs(self,k):
-        z,x,c,y=self.at
-        return self.put(self.src.at[k%2,:,k//2,1-c],self.r1.at[k//2,:,k%2],k,dev(z,x,1-c,y))
-    def kept(self,b):
-        z,x,c,y=self.at
-        return x*(1-c)+b*c,b*(1-c)+y*c
-    def first(self,b):
-        z,x,c,y=self.at
-        at=self.own.at[(1-x)*(1-c)+b*c,:,b*(1-c)+(1-y)*c]
-        return self.put(at,self.r2.at[:,b],4+b,dev(z,x+(1-2*x)*(1-c),c,y+(1-2*y)*c))
-    def zboth(self,i):
-        z,x,c,y=self.at
-        zz=(z+i)%4
-        return self.put(self.own.at[x,zz],self.r3.at[i-1],5+i,dev(zz,x,c,y))
-    def zone(self,i):
-        z,x,c,y=self.at
-        zz=(z+i)%4
-        return self.put(self.own.at[x,zz,y],self.r3.at[i-1,0],5+i,dev(zz,x,c,y))
-    def ylast(self):
-        z,x,c,y=self.at
-        return self.put(self.fin.at[1-y],self.r4,9,dev(z,x,c,1-y))
-    def xsecond(self):
-        z,x,c,y=self.at
-        return self.put(self.own.at[1-x,:,y],self.r5,9,dev(z,1-x,c,y))
+        return send(self.src.at[k%2,:,:,k//2,1-self.c],self.r1.at[k//2,:,:,k%2],self.ss.at[k],self.rs.at[k],self.to(c=1-self.c))
+    def turns(self,core):
+        x,h,l,y=self.x,self.h,self.l,self.y
+        s=slice(None)
+        if core==0:
+            return [((1-x,),dict(x=1-x),lambda a,b,d:(x,a,b,d)),((x,s,1-l),dict(l=1-l),lambda a,d:(x,a,l,d)),
+                    ((x,1-h,l),dict(h=1-h),lambda d:(x,h,l,d)),((x,h,l,1-y),dict(y=1-y),None)]
+        return [((s,s,1-l),dict(l=1-l),lambda a,b,d:(a,b,l,d)),((s,1-h,l),dict(h=1-h),lambda a,d:(a,h,l,d)),
+                ((1-x,h,l),dict(x=1-x),lambda d:(x,h,l,d)),((x,h,l,1-y),dict(y=1-y),None)]
+    def give(self,k,core):
+        at,where,_=self.turns(core)[k]
+        return send(self.own.at[at],self.bufs[k],self.ss.at[4+k],self.rs.at[4+k],self.to(**where))
     def start(self):
         for k in range(4):
             self.theirs(k).start(); self.mine(k).start()
@@ -713,63 +710,41 @@
         total=srcs[0][...].astype(F32)
         for s in srcs[1:]: total=total+s[...].astype(F32)
         dst[...]=total.astype(dst.dtype)
-    def by_core(self,zero,one):
-        c=self.at[2]
-        pl.when(c==0)(zero)
-        pl.when(c==1)(one)
+    def by_core(self,f):
+        for core in range(2):
+            @pl.when(self.c==core)
+            def _(): f(core)
     def one(self):
-        z,x,c,y=self.at
         for k in range(4):
             self.mine(k).wait(); self.theirs(k).wait_recv()
         def step(k,_):
-            self.add(self.own.at[k//8,(k//2)%4,k%2],self.own.at[k//8,(k//2)%4,k%2],self.r1.at[k//8,(k//2)%4,k%2])
+            at=(k//8,(k//4)%2,(k//2)%2,k%2)
+            self.add(self.own.at[at],self.own.at[at],self.r1.at[at])
             return 0
         lax.fori_loop(0,16,step,0)
-        for b in range(2): self.first(b).start()
-    def two(self):
-        z,x,c,y=self.at
-        for b in range(2): self.first(b).wait_recv()
-        def step(k,_):
-            zz,b=k//2,k%2
-            p,q=self.kept(b)
-            self.add(self.own.at[p,zz,q],self.own.at[p,zz,q],self.r2.at[zz,b])
-            return 0
-        lax.fori_loop(0,8,step,0)
-        def zero():
-            for i in (2,1,3): self.zboth(i).start()
-        self.by_core(zero,lambda: self.xsecond().start())
-    def three(self):
-        z,x,c,y=self.at
-        def zero():
-            for i in (1,2,3): self.zboth(i).wait_recv()
-            for yy in (1-y,y):
-                self.add(self.fin.at[yy],self.own.at[x,z,yy],*[self.r3.at[i,yy] for i in range(3)])
-                if yy is not y: self.ylast().start()
-        def one():
-            self.xsecond().wait_recv()
-            for zz in range(4):
-                self.add(self.own.at[x,zz,y],self.own.at[x,zz,y],self.r5.at[zz])
-            for i in (2,1,3): self.zone(i).start()
-        self.by_core(zero,one)
+        self.by_core(lambda core: self.give(0,core).start())
+    def turn(self,k):
+        def f(core):
+            stay=self.turns(core)[k][2]
+            self.give(k,core).wait_recv()
+            def step(i,_):
+                at=[(i//4,(i//2)%2,i%2),(i//2,i%2),(i,)][k]
+                self.add(self.own.at[stay(*at)],self.own.at[stay(*at)],self.bufs[k].at[at])
+                return 0
+            lax.fori_loop(0,8>>k,step,0)
+            self.give(k+1,core).start()
+        self.by_core(f)
     def four(self):
-        z,x,c,y=self.at
-        def zero():
-            self.ylast().wait_recv()
-            self.add(self.out,self.fin.at[y],self.r4)
-            for i in (1,2,3): self.zboth(i).wait_send()
-            self.ylast().wait_send()
-        def one():
-            for i in (1,2,3): self.zone(i).wait_recv()
-            self.add(self.out,self.own.at[x,z,y],*[self.r3.at[i,0] for i in range(3)])
-            for i in (1,2,3): self.zone(i).wait_send()
-            self.xsecond().wait_send()
-        self.by_core(zero,one)
+        def f(core):
+            self.give(3,core).wait_recv()
+            self.add(self.out,self.own.at[self.x,self.h,self.l,self.y],self.bufs[3])
+            for k in range(4): self.give(k,core).wait_send()
+        self.by_core(f)
         for k in range(4): self.theirs(k).wait_send()
-        for b in range(2): self.first(b).wait_send()
 
 def reduce_scratch(rows,cols):
     v=lambda *d: pltpu.VMEM(d+(rows,cols),BF); dma=pltpu.SemaphoreType.DMA
-    return [v(2,4,2),v(2,4,2),v(4,2),dma((10,)),dma((10,)),dma((4,)),v(3,2),v(2),v(),v(4)]
+    return [v(2,2,2,2),v(2,2,2,2),v(2,2,2),v(2,2),v(2),v(),dma((8,)),dma((8,)),dma((4,))]
 
 class Sums:
     def __init__(self,slabs,got,res,ss,rs,ts,us):
@@ -823,7 +798,7 @@
               ev_hbm,hd_hbm,evl_hbm,hdl_hbm,redq_ref,redm_ref,tab_ref,sum_ref,
               G_s,Gx,aq,dq_s,kT_s,gq_s,gqT_s,dd_s,small_ref,acc,slabs,got,res,
               gs,gr_,dl,ds,dr,es,er,us,ss0,rs0,ts0,us0,
-              own,r1,r2,ss,rs,ls,r3,fin,r4,r5,own2,p1,p2,ss2,rs2,ls2,p3,fin2,p4,p5):
+              *more):
     w=pl.program_id(0); nw=dd_s.shape[0]
     z,xc,c,y=place_of()
     s=(z*2+xc)*2+c
@@ -832,8 +807,8 @@
     cq=D//2
     groups=nheads//PER
     tiles=G_s.shape[0]; part=Gx.shape[1]//nheads
-    big=Reduce(dcat_hbm,redm_ref,own2,p1,p2,ss2,rs2,ls2,p3,fin2,p4,p5)
-    red=Reduce(dq_s,redq_ref,own,r1,r2,ss,rs,ls,r3,fin,r4,r5)
+    big=Reduce(dcat_hbm,redm_ref,more[9],more[10],more[11:15],*more[15:18])
+    red=Reduce(dq_s,redq_ref,more[0],more[1],more[2:6],*more[6:9])
     def slab(k,to=None):
         at=ev_hbm.at[y*nw+k]
         if to is None: return pltpu.make_async_copy(dd_s.at[k],at,dl.at[k])
@@ -849,16 +824,20 @@
     def trade(h):
         r=pl.multiple_of(h*WIN+(1-c)*(WIN-part),8)
         return send(G_s.at[:,pl.ds(r,part)],Gx.at[:,pl.ds(pl.multiple_of(h*part,8),part)],gs.at[h],gr_.at[h],sib)
+    everyone=[((s+t)%16,yy) for t in range(1,16) for yy in (y,1-y)]+[mate]
     @pl.when(w==0)
     def _():
-        greet([((s+t)%16,yy) for t in range(1,16) for yy in (y,1-y)]+[mate])
+        hail(everyone)
+        aq[...]=jnp.zeros_like(aq); G_s[...]=jnp.zeros_like(G_s); small_ref[...]=sm_ref[...]
+        dd_s[:,SLAB-16:,:]=jnp.zeros((nw,16,D),BF)
+    def met():
+        heard(everyone)
         big.start()
         early(0).start(); early(1).start()
         @pl.when(y==1)
         def _():
             early(2).start(); early(3).start()
-        aq[...]=jnp.zeros_like(aq); G_s[...]=jnp.zeros_like(G_s); small_ref[...]=sm_ref[...]
-        dd_s[:,SLAB-16:,:]=jnp.zeros((nw,16,D),BF)
+    plan=((0,met),(2,big.one),(6,lambda: big.turn(0)),(10,lambda: big.turn(1)),(13,lambda: big.turn(2)))
     kT_s[...]=qkv_ref[0,1].T
     lane=lax.broadcasted_iota(jnp.int32,(WIN,GROUP),1)
     hl=lane//HD
@@ -884,6 +863,8 @@
             gqT_s[pl.ds(o+hh*HD,HD),:]=mm(kT_s[pl.ds(o+hh*HD,HD),:],dsl)
         gq_s[1,:,pl.ds(o,GROUP)]=(dk*(1.0/SQ)).astype(BF)
         gq_s[2,:,pl.ds(o,GROUP)]=dv.astype(BF)
+        for when,what in plan:
+            pl.when(w*groups+gi==min(when,nw*groups-1))(what)
         @pl.when(w==nw-1)
         def _():
             for hh in range(PER): trade(gi*PER+hh).start()
@@ -911,9 +892,6 @@
         tail(0).start(); tail(1).start()
     small_ref[0:1,:]+=jnp.sum(gr*xhat,axis=0,keepdims=True)
     small_ref[2:3,:]+=jnp.sum(gr,axis=0,keepdims=True)
-    pl.when(w==0)(big.one)
-    pl.when(w==nw//2-1)(big.two)
-    pl.when(w==nw-2)(big.three)
     @pl.when(w==nw-1)
     def _():
         for h in range(nheads): trade(h).wait()
@@ -936,13 +914,11 @@
             acc[...]+=tot.reshape(acc.shape)
             return 0
         n=part//8
-        lax.fori_loop(c,n*4//25,rows,0)
-        red.one()
-        lax.fori_loop(n*4//25,n*11//25,rows,0)
-        red.two()
-        lax.fori_loop(n*11//25,n*18//25,rows,0)
-        red.three()
-        lax.fori_loop(n*18//25,n,rows,0)
+        cuts=[c]+[n*f//25 for f in (4,9,14,19)]+[n]
+        after=(red.one,lambda: red.turn(0),lambda: red.turn(1),lambda: red.turn(2),None)
+        for f in range(5):
+            lax.fori_loop(cuts[f],cuts[f+1],rows,0)
+            if after[f]: after[f]()
         half=nheads//2
         for yy in range(2):
             for k in range(nh): slabs[yy,k]=acc[k,yy*half:(yy+1)*half]
@@ -976,7 +952,7 @@
         full((2,D,cols),pipeline_mode=ONE),full(gains.shape),full(shifts.shape),full(sm.shape),full(pp.shape,pipeline_mode=ONE),ANY,ANY],
       out_specs=[ANY,ANY,ANY,ANY,full((rows,cols),pipeline_mode=ONE),full((rows,more),pipeline_mode=ONE),full((NH//2,nh*256),pipeline_mode=ONE),full(sm.shape)],
       out_shape=[sd((2*nW,SLAB,D),BF),sd((EDGE,D),BF),sd((2,SLAB,D),BF),sd((EDGE,D),BF),sd((rows,cols),F32),sd((rows,more),F32),sd((NH//2,nh*256),F32),sd(sm.shape,F32)],
-      scratch_shapes=[v((tiles,NH*WIN,128),F32),v((tiles,NH*part,128),F32),v((2,D,cols),F32),v((2,4,2,2,rows,cols),BF),v((D,WIN),BF),v((3,WIN,D),BF),v((D,WIN),F32),
+      scratch_shapes=[v((tiles,NH*WIN,128),F32),v((tiles,NH*part,128),F32),v((2,D,cols),F32),v((2,2,2,2,2,rows,cols),BF),v((D,WIN),BF),v((3,WIN,D),BF),v((D,WIN),F32),
         v((nW,SLAB,D),BF),v(sm.shape,F32),v((nh,NH,256),F32),v((2,nh+2,8,256),F32),v((32,8,256),F32),v((nh+2,8,256),F32),
         dma((NH,)),dma((NH,)),dma((nW,)),dma((nW,)),dma((nW,)),dma((2,)),dma,dma((6,)),dma((2*nh+4,)),dma((32,)),dma((16,)),dma((nh+2,))]+reduce_scratch(rows,cols)+reduce_scratch(rows,more),
       compiler_params=pltpu.CompilerParams(vmem_limit_bytes=63*1024*1024,dimension_semantics=("arbitrary",),collective_id=3,has_side_effects=True),
@@ -1063,7 +1039,7 @@
     if linked:
         W1,bias,wf,posT=call_w(w_qkv,w_proj.T,w_fc1,w_fc2.T,pos_index,rel_table)
         qkv,x,Pp,gln2,g,gT,Dd,ev,dlast,dcat,sm=call_a2(inputs,out_grad,wf,lab,bias,W1,gains,shifts)
-        ev2,hd2,evl,hd,redq,redm,d_table,small=call_bc(x,gln2,qkv,g,gT,Dd,Pp,W1,gains,shifts,sm,posT,dcat.reshape(2,4,2,2,rows,-1),dlast,T)
+        ev2,hd2,evl,hd,redq,redm,d_table,small=call_bc(x,gln2,qkv,g,gT,Dd,Pp,W1,gains,shifts,sm,posT,dcat.reshape(2,2,2,2,2,rows,-1),dlast,T)
         out,din,dq,dp,d1,d2,dg,dsh,dt=call_f(inputs,out_grad,ev,evl,ev2,hd,hd2,redq,redm,d_table,small,cq,cf,T)
         return (out,din,dq,dp.T,d1,d2.T,dg,dsh,dt)
     posT=pos_index.T

time: 269 us -> 258 us (0.959)
  Pallas kernels: 266 us -> 256 us
    pallas_call x1, Pallas kernels: 114 us -> 103 us  [call_bc(): pl.pallas_call(functools.partial(kernel_bc, NH), grid=(nW,), in_specs=[pe...]
where the time goes in v6:
time: 258 us
  Pallas kernels  256 us (99%)
    pallas_call x1, Pallas kernels, call_a2(): pl.pallas_call(functools.partial(kernel_a2, NH), grid=(2 * nW,), in_specs...  103 us
    pallas_call x1, Pallas kernels, call_bc(): pl.pallas_call(functools.partial(kernel_bc, NH), grid=(nW,), in_specs=[pe...  103 us
    pallas_call x1, Pallas kernels, call_w(): pl.pallas_call(kernel_w, grid=(1,), out_shape=[sd((2, 16 * rows, 4 * cq),...  35.8 us
    pallas_call x1, Pallas kernels, call_f(): pl.pallas_call(kernel_f, grid=(n,), in_specs=[blk, blk, slab, pl.BlockSpe...  13.4 us

profile of v6, /device:TPU:0, one launch (start us, length us, event | category | flops | bytes accessed | tf_op | source)
XLA Modules:
  0.0 258.1 jit_solution(12456679904135897788)
XLA Ops:
  0.6 1.4 reshape.24.lab_ref
  2.0 35.8 %kernel_w.1 = (bf16[2,512,1024]{2,1,0:T(8,128)(2,1)}, f32[16,392,392]{2,1,0:T(8,128)}, bf16[32,2048]{1,0:T(8,128)(2,1)}, s32[392,512]{1,0:T(8,128)}) custom-call(f32[3,32,256]{2,1,0:T(8,128)} %qkv_ref.1, f32[32,256]{1,0:T(8,128)} %bitcast.7, f32[32,1024]{1,0:T(8,128)} %fc1_ref.1, f32[32,1024]{1,0:T(8,128)} %bitcast.6, s32[392,392]{1,0:T(8,128)} %pos_ref.1, ...), custom_call_target="tpu_custom_call" | custom-call | tf_op jit(solution)/shard_map/kernel_w/pallas_call | solution.py:470
  37.9 103.3 %kernel_a2.1 = (bf16[4,3,392,512]{3,2,1,0:T(8,128)(2,1)}, f32[4,392,512]{2,1,0:T(8,128)}, bf16[4,16,392,392]{3,2,1,0:T(8,128)(2,1)}, f32[4,392,512]{2,1,0:T(8,12...) custom-call(f32[3136,512]{1,0:T(8,128)} %in_ref.1, ...), custom_call_target="tpu_custom_call" | custom-call | tf_op jit(solution)/shard_map/kernel_a2/pallas_call | solution.py:672
  141.2 103.3 %kernel_bc.1 = (bf16[8,400,512]{2,1,0:T(8,128)(2,1)}, bf16[208,512]{1,0:T(8,128)(2,1)}, bf16[2,400,512]{2,1,0:T(8,128)(2,1)}, bf16[208,512]{1,0:T(8,128)(2,1)}, ...) custom-call(f32[4,392,512]{2,1,0:T(8,128)} %get-tuple-element.45.x_ref, ...), custom_call_target="tpu_custom_call" | custom-call | tf_op jit(solution)/shard_map/kernel_bc/pallas_call | solution.py:950
  244.5 13.4 %kernel_f.1 = (f32[3136,512]{1,0:T(8,128)}, f32[3136,512]{1,0:T(8,128)}, f32[3,32,256]{2,1,0:T(8,128)}, f32[32,256]{1,0:T(8,128)}, f32[32,1024]{1,0:T(8,128)}, /...) custom-call(f32[3136,512]{1,0:T(8,128)} %in_ref.1, f32[3136,512]{1,0:T(8,128)} %og_ref.1, ...), custom_call_target="tpu_custom_call" | custom-call | tf_op jit(solution)/shard_map/kernel_f/pallas_call | solution.py:989

commit v7 on v6

--- a/solution.py
+++ b/solution.py
@@ -393,8 +393,8 @@
     return [pltpu.SemaphoreType.DMA((31,)),pltpu.SemaphoreType.DMA((31,)),pltpu.SemaphoreType.DMA]
 
 STEPS=7
-def kernel_w(qkv_ref,proj_ref,fc1_ref,fc2_ref,pos_ref,tab_ref,W_hbm,bias_hbm,wf_ref,posT_ref,
-             bias_s,wq_s,tb,tq,ss,rs,own,bs,br,bl,tsem):
+def kernel_w(qkv_ref,proj_ref,fc1_ref,fc2_ref,pos_ref,tab_ref,W_hbm,bias_hbm,brem_hbm,wf_ref,posT_ref,
+             bias_s,brem_s,wq_s,tb,tq,ss,rs,own,bs,br,bl,tsem,ed):
     z,x,c,y=place_of()
     cq=qkv_ref.shape[2]; cf=fc1_ref.shape[1]
     for k in range(3): wq_s[:,k*cq:(k+1)*cq]=qkv_ref[k].astype(BF)
@@ -410,7 +410,7 @@
     tb[y]=tb[2]
     wf_ref[:,0:cf]=fc1_ref[...].astype(BF)
     wf_ref[:,cf:2*cf]=fc2_ref[...].astype(BF)
-    WIN=bias_s.shape[-1]; tiles=-(-WIN//128); n=tb.shape[2]//128
+    WIN,Q=bias_s.shape[-2:]; tiles=-(-WIN//128); n=tb.shape[2]//128
     posT_ref[...]=jnp.full(posT_ref.shape,1<<15,jnp.int32)
     posT_ref[:,0:WIN]=pos_ref[...].astype(F32).T.astype(jnp.int32)
     swap.wait()
@@ -439,8 +439,9 @@
                         acc=jnp.where(masks[q],jnp.take_along_axis(src,lo,axis=1),acc)
                     a=(acc>>16).astype(F32)*(SQ/FIX)
                     b=((acc<<16)>>16).astype(F32)*(SQ/FIX)
-                    bias_s[2*p,pl.ds(r8,8),t*128:t*128+width]=a[:,:width]
-                    bias_s[2*p+1,pl.ds(r8,8),t*128:t*128+width]=b[:,:width]
+                    for h,v in ((2*p,a),(2*p+1,b)):
+                        if width==128: bias_s[h,pl.ds(r8,8),t*128:(t+1)*128]=v
+                        else: brem_s[pl.ds(r8,8),h*width:(h+1)*width]=v[:,:width]
             return 0
         lax.fori_loop(cuts[k],cuts[k+1],row,0)
         kept(k).start(); sent(k,c).start()
@@ -458,29 +459,39 @@
     rows(5)
     gather.turn_ab(2)
     rows(6)
+    edges=[pltpu.make_async_copy(brem_s,brem_hbm.at[c],ed.at[0]),send(brem_s,brem_hbm.at[c],ed.at[1],ed.at[2],sib)]
+    for e in edges: e.start()
     gather.last()
+    for e in edges: e.wait()
     for k in range(STEPS):
         kept(k).wait(); sent(k,c).wait_send(); sent(k,1-c).wait_recv()
     gather.drain()
 
 def call_w(w_qkv,w_proj,w_fc1,w_fc2,pos_index,rel_table):
     rows,cq=w_qkv.shape[1:]; cf=w_fc1.shape[1]; WIN=pos_index.shape[0]; half,T=rel_table.shape; dma=pltpu.SemaphoreType.DMA
-    wide=-(-WIN//128)*128; n=-(-T//128); mem=pltpu.VMEM
+    wide=-(-WIN//128)*128; Q=WIN//128*128; n=-(-T//128); mem=pltpu.VMEM
     sd=jax.ShapeDtypeStruct
     return pl.pallas_call(kernel_w,grid=(1,),
-      out_shape=[sd((2,16*rows,4*cq),BF),sd((2*half,WIN,WIN),F32),sd((rows,2*cf),BF),sd((WIN,wide),jnp.int32)],
-      in_specs=[full(v.shape) for v in (w_qkv,w_proj,w_fc1,w_fc2,pos_index,rel_table)],out_specs=[ANY,ANY,full((rows,2*cf)),full((WIN,wide))],
-      scratch_shapes=[mem((half,WIN,WIN),F32),mem((rows,4*cq),BF),mem((3,half,n*128),F32),mem((half//2,n*128),jnp.int32)]
-        +gather_sems()+[dma((STEPS,)),dma((STEPS,)),dma((STEPS,)),dma((2,))],
+      out_shape=[sd((2,16*rows,4*cq),BF),sd((2*half,WIN,Q),F32),sd((2,WIN,half*(WIN-Q)),F32),sd((rows,2*cf),BF),sd((WIN,wide),jnp.int32)],
+      in_specs=[full(v.shape) for v in (w_qkv,w_proj,w_fc1,w_fc2,pos_index,rel_table)],out_specs=[ANY,ANY,ANY,full((rows,2*cf)),full((WIN,wide))],
+      scratch_shapes=[mem((half,WIN,Q),F32),mem((WIN,half*(WIN-Q)),F32),mem((rows,4*cq),BF),mem((3,half,n*128),F32),mem((half//2,n*128),jnp.int32)]
+        +gather_sems()+[dma((STEPS,)),dma((STEPS,)),dma((STEPS,)),dma((2,)),dma((3,))],
       compiler_params=pltpu.CompilerParams(vmem_limit_bytes=63*1024*1024,collective_id=1,has_side_effects=True),name="kernel_w")(w_qkv,w_proj,w_fc1,w_fc2,pos_index,rel_table)
 
 def neighbours(z,x,c,y):
     s=(z*2+x)*2+c
     return [((s+k)%16,yy) for k in (1,15) for yy in (y,1-y)]
 
-def kernel_a2(nheads,in_hbm,og_hbm,wf_hbm,lab_ref,bias_ref,W1,gains_ref,shifts_ref,
-              qkv_ref,x_ref,P_hbm,gln2_ref,g_ref,gT_ref,D_ref,ev_hbm,dlast_hbm,dcat_hbm,small_ref,
-              x_s,og_s,W2,OT_s,qT_s,vT_s,P_s,acc,pst,xn2_s,xn2T_s,tg_s,tgT_s,up_s,gn2_s,dl_s,
+def pick(shape,test):
+    r=lax.broadcasted_iota(jnp.int32,shape,0); c=lax.broadcasted_iota(jnp.int32,shape,1)
+    return jnp.where(test(r,c),1.0,0.0)
+
+def exact(a,b):
+    return lax.dot_general(a,b,(((1,),(0,)),((),())),precision=lax.Precision.HIGHEST,preferred_element_type=F32)
+
+def kernel_a2(nheads,in_hbm,og_hbm,wf_hbm,lab_ref,bias_ref,brem_ref,W1,gains_ref,shifts_ref,
+              qkv_ref,x_ref,P_hbm,pr_ref,gln2_ref,g_ref,gT_ref,D_ref,ev_hbm,dlast_hbm,dcat_hbm,small_ref,
+              x_s,og_s,W2,OT_s,qT_s,vT_s,P_s,kst_s,acc,pst,xn2_s,xn2T_s,tg_s,tgT_s,up_s,gn2_s,dl_s,
               lab_s,psem,xsem,hsem,ss,rs,own,dl,ds,dr,fin):
     i=pl.program_id(0); nw=x_s.shape[0]
     w=i%nw
@@ -489,7 +500,7 @@
     D=x_s.shape[-1]; WIN=qkv_ref.shape[-2]; SLAB=x_s.shape[1]; HALF=SLAB//2
     OFF=(SLAB-WIN)//2
     cq=D//2; cf=W2.shape[2]//2
-    groups=nheads//PER
+    groups=nheads//PER; Q=bias_ref.shape[2]; R=WIN-Q
     gather=Gather(wf_hbm,W2,ss,rs,own)
     mate=dev(z,xc,c,1-y)
     def local(k,half,t):
@@ -526,6 +537,7 @@
         gather.start()
         lab_s[...]=lab_ref[...].astype(F32).T
         acc[...]=jnp.zeros_like(acc)
+        for hh in range(PER): kst_s[(hh+1)*SLAB-16:(hh+1)*SLAB,:]=jnp.zeros((16,2*GROUP),BF)
         small_ref[...]=jnp.zeros_like(small_ref)
         dl_s[:,SLAB-16:,:]=jnp.zeros((nw,16,D),BF)
 
@@ -553,26 +565,38 @@
         sub=lax.broadcasted_iota(jnp.int32,(GROUP,WIN),0)
         nm=jnp.where(sub<3,jnp.where(sub!=labr,-hi,0.0),jnp.where(sub<6,jnp.where(sub-3!=labr,-lo,0.0),0.0)).astype(BF)
         hl=lane//HD
+        for hh in range(PER): kst_s[hh*SLAB:hh*SLAB+WIN,GROUP:]=oh
+        nmq=nm[:,0:Q]
+        def soften(t):
+            m=jnp.max(t,axis=0,keepdims=True)
+            e=jnp.exp2((t-m)*CEXP)
+            l=jnp.sum(e,axis=0,keepdims=True)
+            return (e*(1.0/l)).astype(BF)
         def group(gi,_):
             slot=gi%2
             @pl.when(w*groups+gi>=2)
             def _():
-                pltpu.make_async_copy(P_s.at[slot],P_hbm.at[0,pl.ds(0,PER)],psem.at[slot]).wait()
+                pltpu.make_async_copy(P_s.at[slot],P_hbm.at[0,0],psem.at[slot]).wait()
             o=pl.multiple_of(gi*GROUP,GROUP)
-            qTg=jnp.concatenate([qT_s[pl.ds(o,GROUP),:],nm],axis=0)
+            qTg=jnp.concatenate([qT_s[pl.ds(o,GROUP),0:Q],nmq],axis=0)
             kg=qkv_ref[0,1,:,pl.ds(o,GROUP)]
+            for hh in range(PER): kst_s[hh*SLAB:hh*SLAB+WIN,0:GROUP]=jnp.where(hl==hh,kg,jnp.zeros_like(kg))
+            t4=mm(kst_s[...],qTg)
             for hh in range(PER):
-                kh=jnp.concatenate([jnp.where(hl==hh,kg,jnp.zeros_like(kg)),oh],axis=1)
-                t=mm(kh,qTg)+bias_ref[gi*PER+hh]
-                m=jnp.max(t,axis=0,keepdims=True)
-                e=jnp.exp2((t-m)*CEXP)
-                l=jnp.sum(e,axis=0,keepdims=True)
-                p=(e*(1.0/l)).astype(BF)
-                P_s[slot,hh]=p
-                OT_s[w,pl.ds(o+hh*HD,HD),:]=mm(vT_s[pl.ds(o+hh*HD,HD),:],p)
-            pltpu.make_async_copy(P_s.at[slot],P_hbm.at[w,pl.ds(gi*PER,PER)],psem.at[slot]).start()
+                p=soften(t4[hh*SLAB:hh*SLAB+WIN]+bias_ref[gi*PER+hh])
+                P_s[slot,:,hh*Q:(hh+1)*Q]=p
+                OT_s[w,pl.ds(o+hh*HD,HD),0:Q]=mm(vT_s[pl.ds(o+hh*HD,HD),:],p)
+            pltpu.make_async_copy(P_s.at[slot],P_hbm.at[w,gi],psem.at[slot]).start()
             return 0
         lax.fori_loop(0,groups,group,0)
+        spread=pick((R,GROUP),lambda r,c: c%R==r).astype(BF)
+        own_rows=pick((D,GROUP),lambda r,c: r//HD==c//R)
+        qbd=(mm(qT_s[:,Q:WIN],spread)*own_rows).astype(BF)
+        nmr=mm(nm[:,Q:WIN],spread).astype(BF)
+        brem=jnp.concatenate([brem_ref[0],brem_ref[1]],axis=1)
+        pr=soften(mm(qkv_ref[0,1],qbd)+mm(oh,nmr)+brem)
+        pr_ref[0]=pr
+        OT_s[w,:,Q:WIN]=exact(mm(vT_s[...],pr)*own_rows,pick((GROUP,R),lambda r,c: r%R==c))
 
     @pl.when(i==0)
     def _():
@@ -652,7 +676,7 @@
         b=pltpu.make_async_copy(pst,dcat_hbm.at[:,:,pl.ds(0,cq)],fin.at[1])
         a.start(); b.start()
         for k in range(2):
-            pltpu.make_async_copy(P_s.at[k],P_hbm.at[0,pl.ds(0,PER)],psem.at[k]).wait()
+            pltpu.make_async_copy(P_s.at[k],P_hbm.at[0,0],psem.at[k]).wait()
         for k in range(nw-1):
             slab(k).wait(); slab(k,mate).wait()
         slab(None).wait()
@@ -661,23 +685,24 @@
             for t in range(2): edge(t).wait_send()
         a.wait(); b.wait()
 
-def call_a2(inputs,og,wf,lab,bias,W1,gains,shifts):
+def call_a2(inputs,og,wf,lab,bias,brem,W1,gains,shifts):
     nW=lab.shape[0]//2; WIN=lab.shape[1]; D=inputs.shape[1]; NH=bias.shape[0]
     cf=wf.shape[1]//2; cq=D//2; SLAB=-(-WIN//16)*16
+    Q=bias.shape[2]
     sd=jax.ShapeDtypeStruct; dma=pltpu.SemaphoreType.DMA; v=pltpu.VMEM
     early=lambda shape: pl.BlockSpec((1,)+shape,lambda i:(jnp.minimum(i,nW-1),)+(0,)*len(shape))
     late=lambda shape: pl.BlockSpec((1,)+shape,lambda i:(jnp.maximum(i-nW,0),)+(0,)*len(shape))
-    outs=[sd((nW,3,WIN,D),BF),sd((nW,WIN,D),F32),sd((nW,NH,WIN,WIN),BF),sd((nW,WIN,D),F32),sd((nW,WIN,D),BF),sd((nW,D,WIN),BF),sd((nW,NH,WIN),F32),
+    outs=[sd((nW,3,WIN,D),BF),sd((nW,WIN,D),F32),sd((nW,NH//PER,WIN,PER*Q),BF),sd((nW,WIN,GROUP),BF),sd((nW,WIN,D),F32),sd((nW,WIN,D),BF),sd((nW,D,WIN),BF),sd((nW,NH,WIN),F32),
           sd((2*nW,SLAB,D),BF),sd((SLAB,D),BF),sd((2,D,cq+2*cf),BF),sd((8,D),F32)]
     return pl.pallas_call(functools.partial(kernel_a2,NH),grid=(2*nW,),
-      in_specs=[ANY,ANY,ANY,full(lab.shape),full((NH,WIN,WIN),pipeline_mode=ONE),full(W1.shape,pipeline_mode=ONE),full(gains.shape),full(shifts.shape)],
-      out_specs=[early((3,WIN,D)),early((WIN,D)),ANY,late((WIN,D)),late((WIN,D)),late((D,WIN)),late((NH,WIN)),ANY,ANY,ANY,full((8,D))],
+      in_specs=[ANY,ANY,ANY,full(lab.shape),full(bias.shape,pipeline_mode=ONE),full(brem.shape),full(W1.shape,pipeline_mode=ONE),full(gains.shape),full(shifts.shape)],
+      out_specs=[early((3,WIN,D)),early((WIN,D)),ANY,early((WIN,GROUP)),late((WIN,D)),late((WIN,D)),late((D,WIN)),late((NH,WIN)),ANY,ANY,ANY,full((8,D))],
       out_shape=outs,
-      scratch_shapes=[v((nW,SLAB,D),F32),v((nW,SLAB,D),F32),v((2,D,2*cf),BF),v((nW,D,WIN),F32),v((D,WIN),BF),v((D,WIN),BF),v((2,PER,WIN,WIN),BF),
+      scratch_shapes=[v((nW,SLAB,D),F32),v((nW,SLAB,D),F32),v((2,D,2*cf),BF),v((nW,D,WIN),F32),v((D,WIN),BF),v((D,WIN),BF),v((2,WIN,PER*Q),BF),v((PER*SLAB,2*GROUP),BF),
         v((2,D,cq+2*cf),F32),v((2,D,cq),BF),v((WIN,D),BF),v((D,WIN),BF),v((WIN,D),BF),v((D,WIN),BF),v((WIN,D),F32),v((WIN,D),F32),v((nW,SLAB,D),BF),
         v((WIN,2*nW),F32),dma((2,)),dma((2,2*nW)),dma((2,2))]+gather_sems()+[dma((nW,)),dma((nW,)),dma((nW,)),dma((2,))],
       compiler_params=pltpu.CompilerParams(vmem_limit_bytes=63*1024*1024,dimension_semantics=("arbitrary",),collective_id=2,has_side_effects=True),
-      name="kernel_a2")(inputs,og,wf,lab,bias,W1,gains,shifts)
+      name="kernel_a2")(inputs,og,wf,lab,bias,brem,W1,gains,shifts)
 
 class Reduce:
     def __init__(self,src,out,own,r1,bufs,ss,rs,ls):
@@ -794,10 +819,10 @@
                 @pl.when(self.other(k,yy))
                 def _(): self.part(k,yy).wait_send()
 
-def kernel_bc(nheads,x_ref,gln2_ref,qkv_ref,g_ref,gT_ref,D_ref,P_ref,W1,gains_ref,shifts_ref,sm_ref,pos_ref,dcat_hbm,dlast_hbm,
+def kernel_bc(nheads,x_ref,gln2_ref,qkv_ref,g_ref,gT_ref,D_ref,P_ref,pr_ref,W1,gains_ref,shifts_ref,sm_ref,pos_ref,pose_ref,dcat_hbm,dlast_hbm,
               ev_hbm,hd_hbm,evl_hbm,hdl_hbm,redq_ref,redm_ref,tab_ref,sum_ref,
-              G_s,Gx,aq,dq_s,kT_s,gq_s,gqT_s,dd_s,small_ref,acc,slabs,got,res,
-              gs,gr_,dl,ds,dr,es,er,us,ss0,rs0,ts0,us0,
+              G_s,Gx,Gr_s,Gxr,vst_s,dS_s,dsr_s,gbd_s,qbd_s,aq,dq_s,kT_s,gq_s,gqT_s,dd_s,small_ref,acc,slabs,got,res,
+              gs,gr_,ge,dl,ds,dr,es,er,us,ss0,rs0,ts0,us0,
               *more):
     w=pl.program_id(0); nw=dd_s.shape[0]
     z,xc,c,y=place_of()
@@ -806,7 +831,7 @@
     D=x_ref.shape[-1]; WIN=x_ref.shape[-2]; SLAB=dd_s.shape[1]
     cq=D//2
     groups=nheads//PER
-    tiles=G_s.shape[0]; part=Gx.shape[1]//nheads
+    tiles=G_s.shape[0]; Q=tiles*128; R=WIN-Q; part=Gx.shape[1]//nheads
     big=Reduce(dcat_hbm,redm_ref,more[9],more[10],more[11:15],*more[15:18])
     red=Reduce(dq_s,redq_ref,more[0],more[1],more[2:6],*more[6:9])
     def slab(k,to=None):
@@ -821,6 +846,8 @@
         if k==0: return pltpu.make_async_copy(dlast_hbm,evl_hbm.at[y],us.at[0])
         if k==1: return send(dlast_hbm,evl_hbm.at[y],us.at[1],us.at[2],mate)
         return send(dlast_hbm.at[pl.ds(lead,hdl_hbm.shape[0])],hdl_hbm,us.at[k+1],us.at[5],((s+1)%16,k-2))
+    def edge_trade():
+        return send(Gr_s,Gxr,ge.at[0],ge.at[1],sib)
     def trade(h):
         r=pl.multiple_of(h*WIN+(1-c)*(WIN-part),8)
         return send(G_s.at[:,pl.ds(r,part)],Gx.at[:,pl.ds(pl.multiple_of(h*part,8),part)],gs.at[h],gr_.at[h],sib)
@@ -828,8 +855,9 @@
     @pl.when(w==0)
     def _():
         hail(everyone)
-        aq[...]=jnp.zeros_like(aq); G_s[...]=jnp.zeros_like(G_s); small_ref[...]=sm_ref[...]
+        aq[...]=jnp.zeros_like(aq); G_s[...]=jnp.zeros_like(G_s); Gr_s[...]=jnp.zeros_like(Gr_s); small_ref[...]=sm_ref[...]
         dd_s[:,SLAB-16:,:]=jnp.zeros((nw,16,D),BF)
+        for hh in range(PER): vst_s[(hh+1)*SLAB-16:(hh+1)*SLAB,:]=jnp.zeros((16,GROUP),BF)
     def met():
         heard(everyone)
         big.start()
@@ -841,26 +869,37 @@
     kT_s[...]=qkv_ref[0,1].T
     lane=lax.broadcasted_iota(jnp.int32,(WIN,GROUP),1)
     hl=lane//HD
+    lift=pick((GROUP,R),lambda r,c: r%R==c).astype(BF)
+    own_cols=pick((GROUP,D),lambda r,c: r//R==c//HD)
+    gbd_s[...]=(mm(lift,g_ref[0,Q:WIN,:])*own_cols).astype(BF)
+    qbd_s[...]=(mm(lift,qkv_ref[0,0,Q:WIN,:])*own_cols).astype(BF)
+    Dr=exact(D_ref[0,:,Q:WIN],pick((R,GROUP),lambda r,c: c%R==r))
+    Dr=jnp.sum(Dr*pick((nheads,GROUP),lambda r,c: c//R==r),axis=0,keepdims=True)
+    dsr=pr_ref[0].astype(F32)*(mm_nt(qkv_ref[0,2],gbd_s[...])-Dr)
+    Gr_s[...]+=dsr
+    dsr_s[...]=dsr.astype(BF)
+    gqT_s[:,Q:WIN]=exact(mm(kT_s[...],dsr_s[...])*pick((D,GROUP),lambda r,c: r//HD==c//R),pick((GROUP,R),lambda r,c: r%R==c))
     def group(gi,_):
         o=pl.multiple_of(gi*GROUP,GROUP)
-        gTg=gT_ref[0,pl.ds(o,GROUP),:]
+        gTg=gT_ref[0,pl.ds(o,GROUP),0:Q]
         vg=qkv_ref[0,2,:,pl.ds(o,GROUP)]
-        qg=qkv_ref[0,0,:,pl.ds(o,GROUP)]
-        gg=g_ref[0,:,pl.ds(o,GROUP)]
-        dv=jnp.zeros((WIN,GROUP),F32); dk=jnp.zeros((WIN,GROUP),F32)
-        zero=jnp.zeros_like(vg)
+        qg=qkv_ref[0,0,0:Q,pl.ds(o,GROUP)]
+        gg=g_ref[0,0:Q,pl.ds(o,GROUP)]
+        for hh in range(PER): vst_s[hh*SLAB:hh*SLAB+WIN,:]=jnp.where(hl==hh,vg,jnp.zeros_like(vg))
+        dp4=mm(vst_s[...],gTg)
         for hh in range(PER):
             h=gi*PER+hh
-            p=P_ref[0,h]
-            dp=mm(jnp.where(hl==hh,vg,zero),gTg)
-            dsc=p.astype(F32)*(dp-D_ref[0,pl.ds(h,1),:])
+            dsc=P_ref[0,gi,:,hh*Q:(hh+1)*Q].astype(F32)*(dp4[hh*SLAB:hh*SLAB+WIN]-D_ref[0,pl.ds(h,1),0:Q])
             for k in range(tiles):
-                wd=min(128,WIN-k*128)
-                G_s[k,pl.ds(pl.multiple_of(h*WIN,8),WIN),:wd]+=dsc[:,k*128:k*128+wd]
+                G_s[k,pl.ds(pl.multiple_of(h*WIN,8),WIN),:]+=dsc[:,k*128:(k+1)*128]
             dsl=dsc.astype(BF)
-            dv+=mm(p,jnp.where(hl==hh,gg,zero))
-            dk+=mm(dsl,jnp.where(hl==hh,qg,zero))
-            gqT_s[pl.ds(o+hh*HD,HD),:]=mm(kT_s[pl.ds(o+hh*HD,HD),:],dsl)
+            dS_s[:,hh*Q:(hh+1)*Q]=dsl
+            gqT_s[pl.ds(o+hh*HD,HD),0:Q]=mm(kT_s[pl.ds(o+hh*HD,HD),:],dsl)
+        zero=jnp.zeros_like(gg); hq=hl[0:Q]
+        gst=jnp.concatenate([jnp.where(hq==hh,gg,zero) for hh in range(PER)],axis=0)
+        qst=jnp.concatenate([jnp.where(hq==hh,qg,zero) for hh in range(PER)],axis=0)
+        dv=mm(P_ref[0,gi],gst)+mm(pr_ref[0],gbd_s[:,pl.ds(o,GROUP)])
+        dk=mm(dS_s[...],qst)+mm(dsr_s[...],qbd_s[:,pl.ds(o,GROUP)])
         gq_s[1,:,pl.ds(o,GROUP)]=(dk*(1.0/SQ)).astype(BF)
         gq_s[2,:,pl.ds(o,GROUP)]=dv.astype(BF)
         for when,what in plan:
@@ -868,6 +907,8 @@
         @pl.when(w==nw-1)
         def _():
             for hh in range(PER): trade(gi*PER+hh).start()
+            @pl.when(gi==0)
+            def _(): edge_trade().start()
         return 0
     lax.fori_loop(0,groups,group,0)
     gq_s[0]=(gqT_s[...]*(1.0/SQ)).astype(BF).T
@@ -895,24 +936,33 @@
     @pl.when(w==nw-1)
     def _():
         for h in range(nheads): trade(h).wait()
+        edge_trade().wait()
         acc[...]=jnp.zeros_like(acc)
         nh=acc.shape[0]; LW=tiles*128
         base=c*(WIN-part)
+        def one_hots(g,hr,lr,width):
+            iota=lax.broadcasted_iota(jnp.int32,(256,width),0).astype(F32).astype(BF)
+            A=jnp.concatenate([jnp.where(hr==m,g,0.0) for m in range(nh)],axis=0).astype(BF)
+            oh=jnp.where(iota==lr.astype(F32).astype(BF),jnp.ones((),BF),jnp.zeros((),BF))
+            return mm_nt(A,oh)
         def rows(r,_):
             r8=pl.multiple_of(r*8,8)
             f8=pl.multiple_of(base+r*8,8)
-            pos=pos_ref[pl.ds(f8,8),:]
+            pos=pos_ref[pl.ds(f8,8),0:LW]
             hi8=pos>>8; lo8=pos&255
             tot=jnp.zeros((nh*nheads,256),F32)
-            iota=lax.broadcasted_iota(jnp.int32,(256,LW),0).astype(F32).astype(BF)
             for k in range(8):
                 g=jnp.concatenate([G_s[q,pl.ds(f8+k,nheads,stride=WIN),:]+Gx[q,pl.ds(r8+k,nheads,stride=part),:] for q in range(tiles)],axis=1)
-                hr=hi8[k:k+1,:]; lr=lo8[k:k+1,:].astype(F32).astype(BF)
-                A=jnp.concatenate([jnp.where(hr==m,g,0.0) for m in range(nh)],axis=0).astype(BF)
-                oh=jnp.where(iota==lr,jnp.ones((),BF),jnp.zeros((),BF))
-                tot=tot+mm_nt(A,oh)
+                tot=tot+one_hots(g,hi8[k:k+1,:],lo8[k:k+1,:],LW)
             acc[...]+=tot.reshape(acc.shape)
             return 0
+        turned=mm_nt(pick((GROUP,GROUP),lambda r,c: c==(r%nheads)*R+r//nheads).astype(BF),(Gr_s[...]+Gxr[...]).astype(BF))
+        tot=jnp.zeros((nh*nheads,256),F32)
+        for k in range(R):
+            pos=pose_ref[k:k+1,:]
+            hi=jnp.where(c==k//(R//2),pos>>8,-1)
+            tot=tot+one_hots(turned[k*nheads:(k+1)*nheads],hi,pos&255,WIN)
+        acc[...]+=tot.reshape(acc.shape)
         n=part//8
         cuts=[c]+[n*f//25 for f in (4,9,14,19)]+[n]
         after=(red.one,lambda: red.turn(0),lambda: red.turn(1),lambda: red.turn(2),None)
@@ -940,23 +990,23 @@
         tail(0).wait_recv(); early(2).wait_recv()
         early(0).wait(); early(1).wait()
 
-def call_bc(x,gln2,qkv,g,gT,Dd,Pp,W1,gains,shifts,sm,pp,dcat,dlast,T):
+def call_bc(x,gln2,qkv,g,gT,Dd,Pp,Pr,W1,gains,shifts,sm,pp,pos_index,dcat,dlast,T):
     nW,WIN,D=x.shape; NH=Dd.shape[1]
-    cq=D//2; tiles=-(-WIN//128); SLAB=-(-WIN//16)*16; EDGE=-(-(SLAB-WIN//2)//16)*16
+    cq=D//2; tiles=WIN//128; Q=tiles*128; SLAB=-(-WIN//16)*16; EDGE=-(-(SLAB-WIN//2)//16)*16
     part=-(-WIN//16)*8
     nh=-(-T//256)
     rows,more=dcat.shape[-2:]; cols=3*cq
     sd=jax.ShapeDtypeStruct; dma=pltpu.SemaphoreType.DMA; v=pltpu.VMEM
     return pl.pallas_call(functools.partial(kernel_bc,NH),grid=(nW,),
-      in_specs=[per((WIN,D)),per((WIN,D),pipeline_mode=ONE),per((3,WIN,D)),per((WIN,D)),per((D,WIN)),per((NH,WIN)),per((NH,WIN,WIN)),
-        full((2,D,cols),pipeline_mode=ONE),full(gains.shape),full(shifts.shape),full(sm.shape),full(pp.shape,pipeline_mode=ONE),ANY,ANY],
+      in_specs=[per((WIN,D)),per((WIN,D),pipeline_mode=ONE),per((3,WIN,D)),per((WIN,D)),per((D,WIN)),per((NH,WIN)),per(Pp.shape[1:]),per((WIN,GROUP)),
+        full((2,D,cols),pipeline_mode=ONE),full(gains.shape),full(shifts.shape),full(sm.shape),full(pp.shape,pipeline_mode=ONE),pl.BlockSpec((WIN-Q,WIN),lambda w:(Q//(WIN-Q),0)),ANY,ANY],
       out_specs=[ANY,ANY,ANY,ANY,full((rows,cols),pipeline_mode=ONE),full((rows,more),pipeline_mode=ONE),full((NH//2,nh*256),pipeline_mode=ONE),full(sm.shape)],
       out_shape=[sd((2*nW,SLAB,D),BF),sd((EDGE,D),BF),sd((2,SLAB,D),BF),sd((EDGE,D),BF),sd((rows,cols),F32),sd((rows,more),F32),sd((NH//2,nh*256),F32),sd(sm.shape,F32)],
-      scratch_shapes=[v((tiles,NH*WIN,128),F32),v((tiles,NH*part,128),F32),v((2,D,cols),F32),v((2,2,2,2,2,rows,cols),BF),v((D,WIN),BF),v((3,WIN,D),BF),v((D,WIN),F32),
+      scratch_shapes=[v((tiles,NH*WIN,128),F32),v((tiles,NH*part,128),F32),v((WIN,GROUP),F32),v((WIN,GROUP),F32),v((PER*SLAB,GROUP),BF),v((WIN,PER*Q),BF),v((WIN,GROUP),BF),v((GROUP,D),BF),v((GROUP,D),BF),v((2,D,cols),F32),v((2,2,2,2,2,rows,cols),BF),v((D,WIN),BF),v((3,WIN,D),BF),v((D,WIN),F32),
         v((nW,SLAB,D),BF),v(sm.shape,F32),v((nh,NH,256),F32),v((2,nh+2,8,256),F32),v((32,8,256),F32),v((nh+2,8,256),F32),
-        dma((NH,)),dma((NH,)),dma((nW,)),dma((nW,)),dma((nW,)),dma((2,)),dma,dma((6,)),dma((2*nh+4,)),dma((32,)),dma((16,)),dma((nh+2,))]+reduce_scratch(rows,cols)+reduce_scratch(rows,more),
+        dma((NH,)),dma((NH,)),dma((2,)),dma((nW,)),dma((nW,)),dma((nW,)),dma((2,)),dma,dma((6,)),dma((2*nh+4,)),dma((32,)),dma((16,)),dma((nh+2,))]+reduce_scratch(rows,cols)+reduce_scratch(rows,more),
       compiler_params=pltpu.CompilerParams(vmem_limit_bytes=63*1024*1024,dimension_semantics=("arbitrary",),collective_id=3,has_side_effects=True),
-      name="kernel_bc")(x,gln2,qkv,g,gT,Dd,Pp,W1,gains,shifts,sm,pp,dcat,dlast)
+      name="kernel_bc")(x,gln2,qkv,g,gT,Dd,Pp,Pr,W1,gains,shifts,sm,pp,pos_index,dcat,dlast)
 
 
 def kernel_f(in_ref,og_ref,ev_ref,evl_ref,ev2_ref,hd_ref,hd2_ref,redq_ref,redm_ref,tab_ref,sum_ref,
@@ -1037,9 +1087,9 @@
     rows=w_qkv.shape[1]; cq=w_qkv.shape[2]; cf=w_fc1.shape[1]
     lab=region.reshape(-1,WIN)
     if linked:
-        W1,bias,wf,posT=call_w(w_qkv,w_proj.T,w_fc1,w_fc2.T,pos_index,rel_table)
-        qkv,x,Pp,gln2,g,gT,Dd,ev,dlast,dcat,sm=call_a2(inputs,out_grad,wf,lab,bias,W1,gains,shifts)
-        ev2,hd2,evl,hd,redq,redm,d_table,small=call_bc(x,gln2,qkv,g,gT,Dd,Pp,W1,gains,shifts,sm,posT,dcat.reshape(2,2,2,2,2,rows,-1),dlast,T)
+        W1,bias,brem,wf,posT=call_w(w_qkv,w_proj.T,w_fc1,w_fc2.T,pos_index,rel_table)
+        qkv,x,Pp,Pr,gln2,g,gT,Dd,ev,dlast,dcat,sm=call_a2(inputs,out_grad,wf,lab,bias,brem,W1,gains,shifts)
+        ev2,hd2,evl,hd,redq,redm,d_table,small=call_bc(x,gln2,qkv,g,gT,Dd,Pp,Pr,W1,gains,shifts,sm,posT,pos_index,dcat.reshape(2,2,2,2,2,rows,-1),dlast,T)
         out,din,dq,dp,d1,d2,dg,dsh,dt=call_f(inputs,out_grad,ev,evl,ev2,hd,hd2,redq,redm,d_table,small,cq,cf,T)
         return (out,din,dq,dp.T,d1,d2.T,dg,dsh,dt)
     posT=pos_index.T

time: 258 us -> 263 us (1.019)
  Pallas kernels: 256 us -> 261 us
    pallas_call x1, Pallas kernels: 35.8 us -> 46.1 us  [call_w(): pl.pallas_call(kernel_w, grid=(1,), out_shape=[sd((2, 16 * rows, 4 * cq),...]
    pallas_call x1, Pallas kernels: 103 us -> 100 us  [call_a2(): pl.pallas_call(functools.partial(kernel_a2, NH), grid=(2 * nW,), in_specs...]
    pallas_call x1, Pallas kernels: 103 us -> 101 us  [call_bc(): pl.pallas_call(functools.partial(kernel_bc, NH), grid=(nW,), in_specs=[pe...]
where the time goes in v7:
time: 263 us
  Pallas kernels  261 us (99%)
    pallas_call x1, Pallas kernels, call_bc(): pl.pallas_call(functools.partial(kernel_bc, NH), grid=(nW,), in_specs=[pe...  101 us
    pallas_call x1, Pallas kernels, call_a2(): pl.pallas_call(functools.partial(kernel_a2, NH), grid=(2 * nW,), in_specs...  100 us
    pallas_call x1, Pallas kernels, call_w(): pl.pallas_call(kernel_w, grid=(1,), out_shape=[sd((2, 16 * rows, 4 * cq),...  46.1 us
    pallas_call x1, Pallas kernels, call_f(): pl.pallas_call(kernel_f, grid=(n,), in_specs=[blk, blk, slab, pl.BlockSpe...  13.4 us

profile of v7, /device:TPU:0, one launch (start us, length us, event | category | flops | bytes accessed | tf_op | source)
XLA Modules:
  0.0 262.8 jit_solution(16347588000763164665)
XLA Ops:
  0.6 1.4 reshape.24.lab_ref
  2.0 46.1 %kernel_w.1 = (bf16[2,512,1024]{2,1,0:T(8,128)(2,1)}, f32[16,392,384]{2,1,0:T(8,128)}, f32[2,392,64]{2,1,0:T(8,128)}, bf16[32,2048]{1,0:T(8,128)(2,1)}, s32[392,512]{1,0:T(8,128)}) custom-call(f32[3,32,256]{2,1,0:T(8,128)} %qkv_ref.1, f32[32,256]{1,0:T(8,128)} %bitcast.7, f32[32,1024]{1,0:T(8,128)} %fc1_ref.1, f32[32,1024]{1,0:T(8,128)} %bitcast.6, ...), custom_call_target="tpu_custom_call" | custom-call | tf_op jit(solution)/shard_map/kernel_w/pallas_call | solution.py:474
  48.1 100.4 %kernel_a2.1 = (bf16[4,3,392,512]{3,2,1,0:T(8,128)(2,1)}, f32[4,392,512]{2,1,0:T(8,128)}, bf16[4,4,392,1536]{3,2,1,0:T(8,128)(2,1)}, bf16[4,392,128]{2,1,0:T(8,1...) custom-call(f32[3136,512]{1,0:T(8,128)} %in_ref.1, ...), custom_call_target="tpu_custom_call" | custom-call | tf_op jit(solution)/shard_map/kernel_a2/pallas_call | solution.py:697
  148.6 100.6 %kernel_bc.1 = (bf16[8,400,512]{2,1,0:T(8,128)(2,1)}, bf16[208,512]{1,0:T(8,128)(2,1)}, bf16[2,400,512]{2,1,0:T(8,128)(2,1)}, bf16[208,512]{1,0:T(8,128)(2,1)}, ...) custom-call(f32[4,392,512]{2,1,0:T(8,128)} %get-tuple-element.48.x_ref, ...), custom_call_target="tpu_custom_call" | custom-call | tf_op jit(solution)/shard_map/kernel_bc/pallas_call | solution.py:1000
  249.1 13.4 %kernel_f.1 = (f32[3136,512]{1,0:T(8,128)}, f32[3136,512]{1,0:T(8,128)}, f32[3,32,256]{2,1,0:T(8,128)}, f32[32,256]{1,0:T(8,128)}, f32[32,1024]{1,0:T(8,128)}, /...) custom-call(f32[3136,512]{1,0:T(8,128)} %in_ref.1, f32[3136,512]{1,0:T(8,128)} %og_ref.1, ...), custom_call_target="tpu_custom_call" | custom-call | tf_op jit(solution)/shard_map/kernel_f/pallas_call | solution.py:1039

commit v8 on v7

--- a/solution.py
+++ b/solution.py
@@ -394,11 +394,13 @@
 
 STEPS=7
 def kernel_w(qkv_ref,proj_ref,fc1_ref,fc2_ref,pos_ref,tab_ref,W_hbm,bias_hbm,brem_hbm,wf_ref,posT_ref,
-             bias_s,brem_s,wq_s,tb,tq,ss,rs,own,bs,br,bl,tsem,ed):
+             bias_s,brem_s,tail_s,wq_s,tb,tq,ss,rs,own,bs,br,bl,tsem,ed):
     z,x,c,y=place_of()
     cq=qkv_ref.shape[2]; cf=fc1_ref.shape[1]
     for k in range(3): wq_s[:,k*cq:(k+1)*cq]=qkv_ref[k].astype(BF)
     wq_s[:,3*cq:4*cq]=proj_ref[...].astype(BF)
+    lead=wq_s.shape[1]-4*cq
+    wq_s[:,4*cq:]=fc1_ref[:,0:lead].astype(BF)
     half,T=tab_ref.shape
     tb[2]=jnp.zeros(tb.shape[1:],F32)
     tb[2,:,0:T]=tab_ref[...]
@@ -408,8 +410,8 @@
     swap.start()
     gather.start()
     tb[y]=tb[2]
-    wf_ref[:,0:cf]=fc1_ref[...].astype(BF)
-    wf_ref[:,cf:2*cf]=fc2_ref[...].astype(BF)
+    wf_ref[:,0:cf-lead]=fc1_ref[:,lead:].astype(BF)
+    wf_ref[:,cf-lead:]=fc2_ref[...].astype(BF)
     WIN,Q=bias_s.shape[-2:]; tiles=-(-WIN//128); n=tb.shape[2]//128
     posT_ref[...]=jnp.full(posT_ref.shape,1<<15,jnp.int32)
     posT_ref[:,0:WIN]=pos_ref[...].astype(F32).T.astype(jnp.int32)
@@ -441,24 +443,27 @@
                     b=((acc<<16)>>16).astype(F32)*(SQ/FIX)
                     for h,v in ((2*p,a),(2*p+1,b)):
                         if width==128: bias_s[h,pl.ds(r8,8),t*128:(t+1)*128]=v
-                        else: brem_s[pl.ds(r8,8),h*width:(h+1)*width]=v[:,:width]
+                        else: tail_s[h,pl.ds(r8,8),:]=v
             return 0
         lax.fori_loop(cuts[k],cuts[k+1],row,0)
         kept(k).start(); sent(k,c).start()
     rows(0)
+    rows(1)
     for i in (1,3,2): gather.turn_z(i)
-    rows(1)
     for i in (0,): gather.turn_a(i); gather.turn_b(i)
     rows(2)
-    for i in (1,3): gather.turn_a(i); gather.turn_b(i)
     rows(3)
-    for i in (2,): gather.turn_a(i); gather.turn_b(i)
+    for i in (1,3,2): gather.turn_a(i); gather.turn_b(i)
     gather.turn_ab(0)
     rows(4)
-    for i in (1,3): gather.turn_ab(i)
     rows(5)
-    gather.turn_ab(2)
+    for i in (1,3,2): gather.turn_ab(i)
     rows(6)
+    R=WIN-Q
+    owner=lax.broadcasted_iota(jnp.int32,brem_s.shape,1)//R
+    joined=tail_s[0]
+    for h in range(1,half): joined=jnp.where(owner==h,pltpu.roll(tail_s[h],h*R,1),joined)
+    brem_s[...]=joined
     edges=[pltpu.make_async_copy(brem_s,brem_hbm.at[c],ed.at[0]),send(brem_s,brem_hbm.at[c],ed.at[1],ed.at[2],sib)]
     for e in edges: e.start()
     gather.last()
@@ -470,11 +475,12 @@
 def call_w(w_qkv,w_proj,w_fc1,w_fc2,pos_index,rel_table):
     rows,cq=w_qkv.shape[1:]; cf=w_fc1.shape[1]; WIN=pos_index.shape[0]; half,T=rel_table.shape; dma=pltpu.SemaphoreType.DMA
     wide=-(-WIN//128)*128; Q=WIN//128*128; n=-(-T//128); mem=pltpu.VMEM
+    early=4*cq+min(512,cf); late=4*cq+2*cf-early
     sd=jax.ShapeDtypeStruct
     return pl.pallas_call(kernel_w,grid=(1,),
-      out_shape=[sd((2,16*rows,4*cq),BF),sd((2*half,WIN,Q),F32),sd((2,WIN,half*(WIN-Q)),F32),sd((rows,2*cf),BF),sd((WIN,wide),jnp.int32)],
-      in_specs=[full(v.shape) for v in (w_qkv,w_proj,w_fc1,w_fc2,pos_index,rel_table)],out_specs=[ANY,ANY,ANY,full((rows,2*cf)),full((WIN,wide))],
-      scratch_shapes=[mem((half,WIN,Q),F32),mem((WIN,half*(WIN-Q)),F32),mem((rows,4*cq),BF),mem((3,half,n*128),F32),mem((half//2,n*128),jnp.int32)]
+      out_shape=[sd((2,16*rows,early),BF),sd((2*half,WIN,Q),F32),sd((2,WIN,128),F32),sd((rows,late),BF),sd((WIN,wide),jnp.int32)],
+      in_specs=[full(v.shape) for v in (w_qkv,w_proj,w_fc1,w_fc2,pos_index,rel_table)],out_specs=[ANY,ANY,ANY,full((rows,late)),full((WIN,wide))],
+      scratch_shapes=[mem((half,WIN,Q),F32),mem((WIN,128),F32),mem((half,WIN,128),F32),mem((rows,early),BF),mem((3,half,n*128),F32),mem((half//2,n*128),jnp.int32)]
         +gather_sems()+[dma((STEPS,)),dma((STEPS,)),dma((STEPS,)),dma((2,)),dma((3,))],
       compiler_params=pltpu.CompilerParams(vmem_limit_bytes=63*1024*1024,collective_id=1,has_side_effects=True),name="kernel_w")(w_qkv,w_proj,w_fc1,w_fc2,pos_index,rel_table)
 
@@ -499,7 +505,7 @@
     s=(z*2+xc)*2+c
     D=x_s.shape[-1]; WIN=qkv_ref.shape[-2]; SLAB=x_s.shape[1]; HALF=SLAB//2
     OFF=(SLAB-WIN)//2
-    cq=D//2; cf=W2.shape[2]//2
+    cq=D//2; lead=W1.shape[2]-4*cq; cf=(W2.shape[2]+lead)//2
     groups=nheads//PER; Q=bias_ref.shape[2]; R=WIN-Q
     gather=Gather(wf_hbm,W2,ss,rs,own)
     mate=dev(z,xc,c,1-y)
@@ -522,19 +528,30 @@
         at=ev_hbm.at[y*nw+k]
         if to is None: return pltpu.make_async_copy(dl_s.at[k],at,dl.at[k])
         return send(dl_s.at[k],at,ds.at[k],dr.at[k],to)
+    everyone=peers_of(z,xc,c,y)+neighbours(z,xc,c,y)
+    def met():
+        heard(everyone)
+        gather.start()
+        @pl.when(y==1)
+        def _():
+            for t in range(2): edge(t).start()
+    def first():
+        for k in (1,3,2): gather.turn_z(k)
+    def second():
+        for k in (0,1,3,2): gather.turn_a(k); gather.turn_b(k)
+    def third():
+        for k in (0,1,3,2): gather.turn_ab(k)
+    plan=((0,met),(6,first),(10,second),(14,third))
     @pl.when(i==0)
     def _():
-        greet(peers_of(z,xc,c,y)+neighbours(z,xc,c,y))
+        hail(everyone)
         for k in range(nw):
             for t in range(2):
                 local(k,0,t).start()
                 if k<nw-1: local(k,1,t).start()
         for t in range(2):
-            @pl.when(y==1)
-            def _(): edge(t).start()
             @pl.when(y==0)
             def _(): local(nw-1,1,t).start()
-        gather.start()
         lab_s[...]=lab_ref[...].astype(F32).T
         acc[...]=jnp.zeros_like(acc)
         for hh in range(PER): kst_s[(hh+1)*SLAB-16:(hh+1)*SLAB,:]=jnp.zeros((16,2*GROUP),BF)
@@ -587,26 +604,19 @@
                 P_s[slot,:,hh*Q:(hh+1)*Q]=p
                 OT_s[w,pl.ds(o+hh*HD,HD),0:Q]=mm(vT_s[pl.ds(o+hh*HD,HD),:],p)
             pltpu.make_async_copy(P_s.at[slot],P_hbm.at[w,gi],psem.at[slot]).start()
+            for when,what in plan:
+                pl.when(w*groups+gi==min(when,nw*groups-1))(what)
             return 0
         lax.fori_loop(0,groups,group,0)
         spread=pick((R,GROUP),lambda r,c: c%R==r).astype(BF)
         own_rows=pick((D,GROUP),lambda r,c: r//HD==c//R)
         qbd=(mm(qT_s[:,Q:WIN],spread)*own_rows).astype(BF)
         nmr=mm(nm[:,Q:WIN],spread).astype(BF)
-        brem=jnp.concatenate([brem_ref[0],brem_ref[1]],axis=1)
+        brem=jnp.concatenate([brem_ref[0,:,0:GROUP//2],brem_ref[1,:,0:GROUP//2]],axis=1)
         pr=soften(mm(qkv_ref[0,1],qbd)+mm(oh,nmr)+brem)
         pr_ref[0]=pr
         OT_s[w,:,Q:WIN]=exact(mm(vT_s[...],pr)*own_rows,pick((GROUP,R),lambda r,c: r%R==c))
 
-    @pl.when(i==0)
-    def _():
-        for k in (1,3,2): gather.turn_z(k)
-    @pl.when(i==1)
-    def _():
-        for k in (0,1,3,2): gather.turn_a(k); gather.turn_b(k)
-    @pl.when(i==2)
-    def _():
-        for k in (0,1,3,2): gather.turn_ab(k)
     @pl.when(i==nw-1)
     def _():
         gather.last(); gather.drain()
@@ -627,21 +637,21 @@
         tg=og.astype(BF)
         xn2_s[...]=xn2; xn2T_s[...]=xn2.T; tg_s[...]=tg; tgT_s[...]=tg.T
         up_s[...]=jnp.zeros_like(up_s); gn2_s[...]=jnp.zeros_like(gn2_s)
-        CH=512; each=cf//CH
-        def chunk(k,_):
-            m=k//each
-            o=pl.multiple_of((k%each)*CH,CH)
-            f1=W2[m,:,pl.ds(o,CH)]; f2=W2[m,:,pl.ds(cf+o,CH)]
-            hid=mm(xn2_s[...],f1)
-            act,dact=gelu_both(hid)
-            a=act.astype(BF)
-            up_s[...]+=mm_nt(a,f2)
-            gh=(mm(tg_s[...],f2)*dact).astype(BF)
-            gn2_s[...]+=mm_nt(gh,f1)
-            acc[m,:,pl.ds(cq+o,CH)]+=mm(xn2T_s[...],gh)
-            acc[m,:,pl.ds(cq+cf+o,CH)]+=mm(tgT_s[...],a)
+        CH=lead
+        def side(m,_):
+            for o in range(0,cf,CH):
+                f1=W1[m,:,4*cq:] if o==0 else W2[m,:,o-lead:o-lead+CH]
+                f2=W2[m,:,cf-lead+o:cf-lead+o+CH]
+                hid=mm(xn2_s[...],f1)
+                act,dact=gelu_both(hid)
+                a=act.astype(BF)
+                up_s[...]+=mm_nt(a,f2)
+                gh=(mm(tg_s[...],f2)*dact).astype(BF)
+                gn2_s[...]+=mm_nt(gh,f1)
+                acc[m,:,cq+o:cq+o+CH]+=mm(xn2T_s[...],gh)
+                acc[m,:,cq+cf+o:cq+cf+o+CH]+=mm(tgT_s[...],a)
             return 0
-        lax.fori_loop(0,2*each,chunk,0)
+        lax.fori_loop(0,2,side,0)
         dl_s[w,0:WIN,:]=(branch+up_s[...]+shifts_ref[3:4,:]).astype(BF)
         @pl.when(w<nw-1)
         def _():
@@ -670,10 +680,10 @@
 
     @pl.when(i==2*nw-1)
     def _():
-        W2[...]=acc[:,:,cq:].astype(BF)
-        pst[...]=acc[:,:,:cq].astype(BF)
-        a=pltpu.make_async_copy(W2,dcat_hbm.at[:,:,pl.ds(cq,2*cf)],fin.at[0])
-        b=pltpu.make_async_copy(pst,dcat_hbm.at[:,:,pl.ds(0,cq)],fin.at[1])
+        W2[...]=acc[:,:,cq+lead:].astype(BF)
+        pst[...]=acc[:,:,:cq+lead].astype(BF)
+        a=pltpu.make_async_copy(W2,dcat_hbm.at[:,:,pl.ds(cq+lead,W2.shape[2])],fin.at[0])
+        b=pltpu.make_async_copy(pst,dcat_hbm.at[:,:,pl.ds(0,cq+lead)],fin.at[1])
         a.start(); b.start()
         for k in range(2):
             pltpu.make_async_copy(P_s.at[k],P_hbm.at[0,0],psem.at[k]).wait()
@@ -687,7 +697,7 @@
 
 def call_a2(inputs,og,wf,lab,bias,brem,W1,gains,shifts):
     nW=lab.shape[0]//2; WIN=lab.shape[1]; D=inputs.shape[1]; NH=bias.shape[0]
-    cf=wf.shape[1]//2; cq=D//2; SLAB=-(-WIN//16)*16
+    cq=D//2; lead=W1.shape[2]-4*cq; cf=(wf.shape[1]+lead)//2; SLAB=-(-WIN//16)*16
     Q=bias.shape[2]
     sd=jax.ShapeDtypeStruct; dma=pltpu.SemaphoreType.DMA; v=pltpu.VMEM
     early=lambda shape: pl.BlockSpec((1,)+shape,lambda i:(jnp.minimum(i,nW-1),)+(0,)*len(shape))
@@ -698,8 +708,8 @@
       in_specs=[ANY,ANY,ANY,full(lab.shape),full(bias.shape,pipeline_mode=ONE),full(brem.shape),full(W1.shape,pipeline_mode=ONE),full(gains.shape),full(shifts.shape)],
       out_specs=[early((3,WIN,D)),early((WIN,D)),ANY,early((WIN,GROUP)),late((WIN,D)),late((WIN,D)),late((D,WIN)),late((NH,WIN)),ANY,ANY,ANY,full((8,D))],
       out_shape=outs,
-      scratch_shapes=[v((nW,SLAB,D),F32),v((nW,SLAB,D),F32),v((2,D,2*cf),BF),v((nW,D,WIN),F32),v((D,WIN),BF),v((D,WIN),BF),v((2,WIN,PER*Q),BF),v((PER*SLAB,2*GROUP),BF),
-        v((2,D,cq+2*cf),F32),v((2,D,cq),BF),v((WIN,D),BF),v((D,WIN),BF),v((WIN,D),BF),v((D,WIN),BF),v((WIN,D),F32),v((WIN,D),F32),v((nW,SLAB,D),BF),
+      scratch_shapes=[v((nW,SLAB,D),F32),v((nW,SLAB,D),F32),v((2,D,2*cf-lead),BF),v((nW,D,WIN),F32),v((D,WIN),BF),v((D,WIN),BF),v((2,WIN,PER*Q),BF),v((PER*SLAB,2*GROUP),BF),
+        v((2,D,cq+2*cf),F32),v((2,D,cq+lead),BF),v((WIN,D),BF),v((D,WIN),BF),v((WIN,D),BF),v((D,WIN),BF),v((WIN,D),F32),v((WIN,D),F32),v((nW,SLAB,D),BF),
         v((WIN,2*nW),F32),dma((2,)),dma((2,2*nW)),dma((2,2))]+gather_sems()+[dma((nW,)),dma((nW,)),dma((nW,)),dma((2,))],
       compiler_params=pltpu.CompilerParams(vmem_limit_bytes=63*1024*1024,dimension_semantics=("arbitrary",),collective_id=2,has_side_effects=True),
       name="kernel_a2")(inputs,og,wf,lab,bias,brem,W1,gains,shifts)
@@ -964,21 +974,22 @@
             tot=tot+one_hots(turned[k*nheads:(k+1)*nheads],hi,pos&255,WIN)
         acc[...]+=tot.reshape(acc.shape)
         n=part//8
-        cuts=[c]+[n*f//25 for f in (4,9,14,19)]+[n]
-        after=(red.one,lambda: red.turn(0),lambda: red.turn(1),lambda: red.turn(2),None)
-        for f in range(5):
+        cuts=[c,n*5//25,n*15//25,n]
+        for f,after in enumerate((red.one,lambda: red.turn(0),None)):
             lax.fori_loop(cuts[f],cuts[f+1],rows,0)
-            if after[f]: after[f]()
+            if after: after()
         half=nheads//2
         for yy in range(2):
             for k in range(nh): slabs[yy,k]=acc[k,yy*half:(yy+1)*half]
             for k in range(2): slabs[yy,nh+k]=small_ref[:,k*256:(k+1)*256]
         sums=Sums(slabs,got,res,ss0,rs0,ts0,us0)
         sums.scatter()
-        red.four()
+        red.turn(1)
         sums.collect()
+        red.turn(2)
         big.four()
         sums.finish()
+        red.four()
         for m in range(nh):
             tab_ref[:,m*256:(m+1)*256]=res[m]
         for k in range(2): sum_ref[:,k*256:(k+1)*256]=res[nh+k]

time: 263 us -> 245 us (0.932)
  Pallas kernels: 261 us -> 243 us
    pallas_call x1, Pallas kernels: 100 us -> 88 us  [call_a2(): pl.pallas_call(functools.partial(kernel_a2, NH), grid=(2 * nW,), in_specs...]
    pallas_call x1, Pallas kernels: 46.1 us -> 39.7 us  [call_w(): pl.pallas_call(kernel_w, grid=(1,), out_shape=[sd((2, 16 * rows, early),...]
where the time goes in v8:
time: 245 us
  Pallas kernels  243 us (99%)
    pallas_call x1, Pallas kernels, call_bc(): pl.pallas_call(functools.partial(kernel_bc, NH), grid=(nW,), in_specs=[pe...  101 us
    pallas_call x1, Pallas kernels, call_a2(): pl.pallas_call(functools.partial(kernel_a2, NH), grid=(2 * nW,), in_specs...  88 us
    pallas_call x1, Pallas kernels, call_w(): pl.pallas_call(kernel_w, grid=(1,), out_shape=[sd((2, 16 * rows, early),...  39.7 us
    pallas_call x1, Pallas kernels, call_f(): pl.pallas_call(kernel_f, grid=(n,), in_specs=[blk, blk, slab, pl.BlockSpe...  13.4 us

profile of v8, /device:TPU:0, one launch (start us, length us, event | category | flops | bytes accessed | tf_op | source)
XLA Modules:
  0.0 244.9 jit_solution(18416415105827067159)
XLA Ops:
  0.6 1.4 reshape.24.lab_ref
  2.0 39.7 %kernel_w.1 = (bf16[2,512,1536]{2,1,0:T(8,128)(2,1)}, f32[16,392,384]{2,1,0:T(8,128)}, f32[2,392,128]{2,1,0:T(8,128)}, bf16[32,1536]{1,0:T(8,128)(2,1)}, s32[392,512]{1,0:T(8,128)}) custom-call(f32[3,32,256]{2,1,0:T(8,128)} %qkv_ref.1, f32[32,256]{1,0:T(8,128)} %bitcast.7, f32[32,1024]{1,0:T(8,128)} %fc1_ref.1, f32[32,1024]{1,0:T(8,128)} %bitcast.6, ...), custom_call_target="tpu_custom_call" | custom-call | tf_op jit(solution)/shard_map/kernel_w/pallas_call | solution.py:480
  41.8 88.0 %kernel_a2.1 = (bf16[4,3,392,512]{3,2,1,0:T(8,128)(2,1)}, f32[4,392,512]{2,1,0:T(8,128)}, bf16[4,4,392,1536]{3,2,1,0:T(8,128)(2,1)}, bf16[4,392,128]{2,1,0:T(8,1...) custom-call(f32[3136,512]{1,0:T(8,128)} %in_ref.1, ...), custom_call_target="tpu_custom_call" | custom-call | tf_op jit(solution)/shard_map/kernel_a2/pallas_call | solution.py:707
  129.8 101.4 %kernel_bc.1 = (bf16[8,400,512]{2,1,0:T(8,128)(2,1)}, bf16[208,512]{1,0:T(8,128)(2,1)}, bf16[2,400,512]{2,1,0:T(8,128)(2,1)}, bf16[208,512]{1,0:T(8,128)(2,1)}, ...) custom-call(f32[4,392,512]{2,1,0:T(8,128)} %get-tuple-element.48.x_ref, ...), custom_call_target="tpu_custom_call" | custom-call | tf_op jit(solution)/shard_map/kernel_bc/pallas_call | solution.py:1011
  231.3 13.4 %kernel_f.1 = (f32[3136,512]{1,0:T(8,128)}, f32[3136,512]{1,0:T(8,128)}, f32[3,32,256]{2,1,0:T(8,128)}, f32[32,256]{1,0:T(8,128)}, f32[32,1024]{1,0:T(8,128)}, /...) custom-call(f32[3136,512]{1,0:T(8,128)} %in_ref.1, f32[3136,512]{1,0:T(8,128)} %og_ref.1, ...), custom_call_target="tpu_custom_call" | custom-call | tf_op jit(solution)/shard_map/kernel_f/pallas_call | solution.py:1050

commit v9 on v8

--- a/solution.py
+++ b/solution.py
@@ -336,15 +336,16 @@
 
 
 class Gather:
-    def __init__(self,src,dst,ss,rs,own):
+    def __init__(self,src,dst,ss,rs,own,cols=None):
         self.src,self.dst,self.ss,self.rs,self.own=src,dst,ss,rs,own
+        self.cols=pl.ds(0,dst.shape[2]) if cols is None else cols
         z,x,c,y=self.at=place_of()
         self.xa=x+(1-2*x)*(1-c); self.ya=y+(1-2*y)*c
         self.xb=x+(1-2*x)*c; self.yb=y+(1-2*y)*(1-c)
         self.sib=dev(z,x,1-c,y); self.pa=dev(z,self.xa,c,self.ya); self.pb=dev(z,self.xb,c,self.yb)
     def slot(self,zz,xx,cc,yy):
         n=self.src.shape[0]
-        return self.dst.at[yy,pl.ds(pl.multiple_of(((zz*2+xx)*2+cc)*n,n),n)]
+        return self.dst.at[yy,pl.ds(pl.multiple_of(((zz*2+xx)*2+cc)*n,n),n),self.cols]
     def copy(self,src,where,k,to):
         return send(src,self.slot(*where),self.ss.at[k],self.rs.at[k],to)
     def go(self,where,k,to,src=None):
@@ -389,12 +390,40 @@
             self.copy(self.src,(z,x,c,y),k,self.sib).wait_send()
         self.keep().wait()
 
+class GatherLate(Gather):
+    def start(self):
+        z,x,c,y=self.at
+        me=(z,x,c,y)
+        self.keep().start()
+        self.go(me,0,self.pa,self.src)
+        for i in (1,2,3):
+            self.go(me,i,dev((z+i)%4,x,c,y),self.src)
+        self.go(me,7,self.pb,self.src); self.go(me,15,self.sib,self.src)
+    def pair(self):
+        z,x,c,y=self.at
+        at=(z,self.xa,c,self.ya); self.came(at,0)
+        for i in (1,2,3):
+            self.go(at,3+i,dev((z+i)%4,x,c,y))
+        self.go(at,11,self.pb); self.go(at,19,self.sib)
+    def along(self,i):
+        z,x,c,y=self.at
+        at=(self.z(i),x,c,y); self.came(at,i)
+        self.go(at,7+i,self.pb); self.go(at,15+i,self.sib)
+        at=(self.z(i),self.xa,c,self.ya); self.came(at,3+i)
+        self.go(at,11+i,self.pb); self.go(at,19+i,self.sib)
+    def over(self,i):
+        z,x,c,y=self.at
+        at=(self.z(i),self.xb,c,self.yb); self.came(at,7+i)
+        self.go(at,23+i,self.sib)
+        at=(self.z(i),1-x,c,1-y); self.came(at,11+i)
+        self.go(at,27+i,self.sib)
+
 def gather_sems():
     return [pltpu.SemaphoreType.DMA((31,)),pltpu.SemaphoreType.DMA((31,)),pltpu.SemaphoreType.DMA]
 
 STEPS=7
 def kernel_w(qkv_ref,proj_ref,fc1_ref,fc2_ref,pos_ref,tab_ref,W_hbm,bias_hbm,brem_hbm,wf_ref,posT_ref,
-             bias_s,brem_s,tail_s,wq_s,tb,tq,ss,rs,own,bs,br,bl,tsem,ed):
+             bias_s,brem_s,short_s,found_s,wq_s,tb,tq,ss,rs,own,bs,br,bl,tsem,ed):
     z,x,c,y=place_of()
     cq=qkv_ref.shape[2]; cf=fc1_ref.shape[1]
     for k in range(3): wq_s[:,k*cq:(k+1)*cq]=qkv_ref[k].astype(BF)
@@ -405,14 +434,16 @@
     tb[2]=jnp.zeros(tb.shape[1:],F32)
     tb[2,:,0:T]=tab_ref[...]
     greet(peers_of(z,x,c,y))
-    gather=Gather(wq_s,W_hbm,ss,rs,own)
+    mid=wq_s.shape[1]//2
+    gather=Gather(wq_s.at[:,pl.ds(0,mid)],W_hbm,ss.at[0],rs.at[0],own.at[0],pl.ds(0,mid))
+    other=GatherLate(wq_s.at[:,pl.ds(mid,mid)],W_hbm,ss.at[1],rs.at[1],own.at[1],pl.ds(mid,mid))
     swap=send(tb.at[2],tb.at[y],tsem.at[0],tsem.at[1],dev(z,x,c,1-y))
     swap.start()
-    gather.start()
+    gather.start(); other.start()
     tb[y]=tb[2]
     wf_ref[:,0:cf-lead]=fc1_ref[:,lead:].astype(BF)
     wf_ref[:,cf-lead:]=fc2_ref[...].astype(BF)
-    WIN,Q=bias_s.shape[-2:]; tiles=-(-WIN//128); n=tb.shape[2]//128
+    WIN,Q=bias_s.shape[-2:]; tiles=Q//128; n=tb.shape[2]//128; R=WIN-Q; per_row=128//R; nr=found_s.shape[1]
     posT_ref[...]=jnp.full(posT_ref.shape,1<<15,jnp.int32)
     posT_ref[:,0:WIN]=pos_ref[...].astype(F32).T.astype(jnp.int32)
     swap.wait()
@@ -426,62 +457,77 @@
     def rows_of(k): return pl.ds(cuts[k]*8,(cuts[k+1]-cuts[k])*8)
     def kept(k): return pltpu.make_async_copy(bias_s.at[:,rows_of(k)],bias_hbm.at[pl.ds(c*half,half),rows_of(k)],bl.at[k])
     def sent(k,cc): return send(bias_s.at[:,rows_of(k)],bias_hbm.at[pl.ds(cc*half,half),rows_of(k)],bs.at[k],br.at[k],sib)
+    def look(idx):
+        lo=idx&127; hi=idx>>7
+        masks=[hi==q for q in range(n)]
+        for p in range(npair):
+            acc=jnp.zeros((8,128),jnp.int32)
+            for q in range(n):
+                src=jnp.broadcast_to(tq[p:p+1,q*128:(q+1)*128],(8,128))
+                acc=jnp.where(masks[q],jnp.take_along_axis(src,lo,axis=1),acc)
+            yield 2*p,(acc>>16).astype(F32)*(SQ/FIX)
+            yield 2*p+1,((acc<<16)>>16).astype(F32)*(SQ/FIX)
+    slots=lax.broadcasted_iota(jnp.int32,(nr,128),1)//R
+    def short_in():
+        short_s[...]=jnp.full(short_s.shape,1<<15,jnp.int32)
+        short_s[0:WIN,:]=posT_ref[:,Q:Q+128]
+        packed=jnp.zeros((nr,128),jnp.int32)
+        for u in range(per_row):
+            v=short_s[pl.ds(u,nr,stride=per_row),:]
+            packed=jnp.where(slots==u,pltpu.roll(v,u*R,1) if u else v,packed)
+        for t in range(nr//8):
+            for h,v in look(packed[t*8:(t+1)*8]): found_s[h,t*8:(t+1)*8,:]=v
+    def short_out():
+        for u in range(per_row):
+            row=jnp.zeros((nr,128),F32)
+            for h in range(half):
+                by=((h-u)*R)%128
+                v=found_s[h]
+                row=jnp.where(slots==h,pltpu.roll(v,by,1) if by else v,row)
+            brem_s[pl.ds(u,nr,stride=per_row),:]=row
     def rows(k):
         def row(r,_):
             r8=pl.multiple_of(r*8,8)
             for t in range(tiles):
-                width=min(128,WIN-t*128)
-                idx=posT_ref[pl.ds(r8,8),t*128:(t+1)*128]
-                lo=idx&127; hi=idx>>7
-                masks=[hi==q for q in range(n)]
-                for p in range(npair):
-                    acc=jnp.zeros((8,128),jnp.int32)
-                    for q in range(n):
-                        src=jnp.broadcast_to(tq[p:p+1,q*128:(q+1)*128],(8,128))
-                        acc=jnp.where(masks[q],jnp.take_along_axis(src,lo,axis=1),acc)
-                    a=(acc>>16).astype(F32)*(SQ/FIX)
-                    b=((acc<<16)>>16).astype(F32)*(SQ/FIX)
-                    for h,v in ((2*p,a),(2*p+1,b)):
-                        if width==128: bias_s[h,pl.ds(r8,8),t*128:(t+1)*128]=v
-                        else: tail_s[h,pl.ds(r8,8),:]=v
+                for h,v in look(posT_ref[pl.ds(r8,8),t*128:(t+1)*128]):
+                    bias_s[h,pl.ds(r8,8),t*128:(t+1)*128]=v
             return 0
         lax.fori_loop(cuts[k],cuts[k+1],row,0)
         kept(k).start(); sent(k,c).start()
     rows(0)
+    short_in()
+    short_out()
+    other.pair()
     rows(1)
     for i in (1,3,2): gather.turn_z(i)
     for i in (0,): gather.turn_a(i); gather.turn_b(i)
     rows(2)
+    for i in (1,3,2): other.along(i)
     rows(3)
     for i in (1,3,2): gather.turn_a(i); gather.turn_b(i)
-    gather.turn_ab(0)
     rows(4)
+    for i in (0,1,3,2): gather.turn_ab(i); other.over(i)
     rows(5)
-    for i in (1,3,2): gather.turn_ab(i)
     rows(6)
-    R=WIN-Q
-    owner=lax.broadcasted_iota(jnp.int32,brem_s.shape,1)//R
-    joined=tail_s[0]
-    for h in range(1,half): joined=jnp.where(owner==h,pltpu.roll(tail_s[h],h*R,1),joined)
-    brem_s[...]=joined
-    edges=[pltpu.make_async_copy(brem_s,brem_hbm.at[c],ed.at[0]),send(brem_s,brem_hbm.at[c],ed.at[1],ed.at[2],sib)]
+    edges=[pltpu.make_async_copy(brem_s.at[pl.ds(0,WIN)],brem_hbm.at[c],ed.at[0]),send(brem_s.at[pl.ds(0,WIN)],brem_hbm.at[c],ed.at[1],ed.at[2],sib)]
     for e in edges: e.start()
-    gather.last()
+    gather.last(); other.last()
     for e in edges: e.wait()
     for k in range(STEPS):
         kept(k).wait(); sent(k,c).wait_send(); sent(k,1-c).wait_recv()
-    gather.drain()
+    gather.drain(); other.drain()
 
 def call_w(w_qkv,w_proj,w_fc1,w_fc2,pos_index,rel_table):
     rows,cq=w_qkv.shape[1:]; cf=w_fc1.shape[1]; WIN=pos_index.shape[0]; half,T=rel_table.shape; dma=pltpu.SemaphoreType.DMA
     wide=-(-WIN//128)*128; Q=WIN//128*128; n=-(-T//128); mem=pltpu.VMEM
+    keys=-(-WIN//(1024//(WIN-Q)))*(1024//(WIN-Q))
     early=4*cq+min(512,cf); late=4*cq+2*cf-early
     sd=jax.ShapeDtypeStruct
     return pl.pallas_call(kernel_w,grid=(1,),
       out_shape=[sd((2,16*rows,early),BF),sd((2*half,WIN,Q),F32),sd((2,WIN,128),F32),sd((rows,late),BF),sd((WIN,wide),jnp.int32)],
       in_specs=[full(v.shape) for v in (w_qkv,w_proj,w_fc1,w_fc2,pos_index,rel_table)],out_specs=[ANY,ANY,ANY,full((rows,late)),full((WIN,wide))],
-      scratch_shapes=[mem((half,WIN,Q),F32),mem((WIN,128),F32),mem((half,WIN,128),F32),mem((rows,early),BF),mem((3,half,n*128),F32),mem((half//2,n*128),jnp.int32)]
-        +gather_sems()+[dma((STEPS,)),dma((STEPS,)),dma((STEPS,)),dma((2,)),dma((3,))],
+      scratch_shapes=[mem((half,WIN,Q),F32),mem((keys,128),F32),mem((keys,128),jnp.int32),mem((half,keys*(WIN-Q)//128,128),F32),mem((rows,early),BF),mem((3,half,n*128),F32),mem((half//2,n*128),jnp.int32)]
+        +[dma((2,31)),dma((2,31)),dma((2,))]+[dma((STEPS,)),dma((STEPS,)),dma((STEPS,)),dma((2,)),dma((3,))],
       compiler_params=pltpu.CompilerParams(vmem_limit_bytes=63*1024*1024,collective_id=1,has_side_effects=True),name="kernel_w")(w_qkv,w_proj,w_fc1,w_fc2,pos_index,rel_table)
 
 def neighbours(z,x,c,y):

time: 245 us -> 243 us (level)
    pallas_call x1, Pallas kernels: 39.7 us -> 36.3 us  [call_w(): pl.pallas_call(kernel_w, grid=(1,), out_shape=[sd((2, 16 * rows, early),...]
where the time goes in v9:
time: 243 us
  Pallas kernels  241 us (99%)
    pallas_call x1, Pallas kernels, call_bc(): pl.pallas_call(functools.partial(kernel_bc, NH), grid=(nW,), in_specs=[pe...  103 us
    pallas_call x1, Pallas kernels, call_a2(): pl.pallas_call(functools.partial(kernel_a2, NH), grid=(2 * nW,), in_specs...  88.2 us
    pallas_call x1, Pallas kernels, call_w(): pl.pallas_call(kernel_w, grid=(1,), out_shape=[sd((2, 16 * rows, early),...  36.3 us
    pallas_call x1, Pallas kernels, call_f(): pl.pallas_call(kernel_f, grid=(n,), in_specs=[blk, blk, slab, pl.BlockSpe...  13.4 us

profile of v9, /device:TPU:0, one launch (start us, length us, event | category | flops | bytes accessed | tf_op | source)
XLA Modules:
  0.0 243.0 jit_solution(5960477255837613312)
XLA Ops:
  0.6 1.4 reshape.24.lab_ref
  2.0 36.3 %kernel_w.1 = (bf16[2,512,1536]{2,1,0:T(8,128)(2,1)}, f32[16,392,384]{2,1,0:T(8,128)}, f32[2,392,128]{2,1,0:T(8,128)}, bf16[32,1536]{1,0:T(8,128)(2,1)}, s32[392,512]{1,0:T(8,128)}) custom-call(f32[3,32,256]{2,1,0:T(8,128)} %qkv_ref.1, f32[32,256]{1,0:T(8,128)} %bitcast.7, f32[32,1024]{1,0:T(8,128)} %fc1_ref.1, f32[32,1024]{1,0:T(8,128)} %bitcast.6, ...), custom_call_target="tpu_custom_call" | custom-call | tf_op jit(solution)/shard_map/kernel_w/pallas_call | solution.py:526
  38.4 88.2 %kernel_a2.1 = (bf16[4,3,392,512]{3,2,1,0:T(8,128)(2,1)}, f32[4,392,512]{2,1,0:T(8,128)}, bf16[4,4,392,1536]{3,2,1,0:T(8,128)(2,1)}, bf16[4,392,128]{2,1,0:T(8,1...) custom-call(f32[3136,512]{1,0:T(8,128)} %in_ref.1, ...), custom_call_target="tpu_custom_call" | custom-call | tf_op jit(solution)/shard_map/kernel_a2/pallas_call | solution.py:753
  126.6 102.8 %kernel_bc.1 = (bf16[8,400,512]{2,1,0:T(8,128)(2,1)}, bf16[208,512]{1,0:T(8,128)(2,1)}, bf16[2,400,512]{2,1,0:T(8,128)(2,1)}, bf16[208,512]{1,0:T(8,128)(2,1)}, ...) custom-call(f32[4,392,512]{2,1,0:T(8,128)} %get-tuple-element.48.x_ref, ...), custom_call_target="tpu_custom_call" | custom-call | tf_op jit(solution)/shard_map/kernel_bc/pallas_call | solution.py:1057
  229.4 13.4 %kernel_f.1 = (f32[3136,512]{1,0:T(8,128)}, f32[3136,512]{1,0:T(8,128)}, f32[3,32,256]{2,1,0:T(8,128)}, f32[32,256]{1,0:T(8,128)}, f32[32,1024]{1,0:T(8,128)}, /...) custom-call(f32[3136,512]{1,0:T(8,128)} %in_ref.1, f32[3136,512]{1,0:T(8,128)} %og_ref.1, ...), custom_call_target="tpu_custom_call" | custom-call | tf_op jit(solution)/shard_map/kernel_f/pallas_call | solution.py:1096

commit v10 on v9

--- a/solution.py
+++ b/solution.py
@@ -921,7 +921,7 @@
         @pl.when(y==1)
         def _():
             early(2).start(); early(3).start()
-    plan=((0,met),(2,big.one),(6,lambda: big.turn(0)),(10,lambda: big.turn(1)),(13,lambda: big.turn(2)))
+    plan=((0,met),(2,big.one),(7,lambda: big.turn(0)),(11,lambda: big.turn(1)),(14,lambda: big.turn(2)))
     kT_s[...]=qkv_ref[0,1].T
     lane=lax.broadcasted_iota(jnp.int32,(WIN,GROUP),1)
     hl=lane//HD
@@ -1055,7 +1055,7 @@
     rows,more=dcat.shape[-2:]; cols=3*cq
     sd=jax.ShapeDtypeStruct; dma=pltpu.SemaphoreType.DMA; v=pltpu.VMEM
     return pl.pallas_call(functools.partial(kernel_bc,NH),grid=(nW,),
-      in_specs=[per((WIN,D)),per((WIN,D),pipeline_mode=ONE),per((3,WIN,D)),per((WIN,D)),per((D,WIN)),per((NH,WIN)),per(Pp.shape[1:]),per((WIN,GROUP)),
+      in_specs=[per((WIN,D)),per((WIN,D)),per((3,WIN,D)),per((WIN,D)),per((D,WIN)),per((NH,WIN)),per(Pp.shape[1:]),per((WIN,GROUP)),
         full((2,D,cols),pipeline_mode=ONE),full(gains.shape),full(shifts.shape),full(sm.shape),full(pp.shape,pipeline_mode=ONE),pl.BlockSpec((WIN-Q,WIN),lambda w:(Q//(WIN-Q),0)),ANY,ANY],
       out_specs=[ANY,ANY,ANY,ANY,full((rows,cols),pipeline_mode=ONE),full((rows,more),pipeline_mode=ONE),full((NH//2,nh*256),pipeline_mode=ONE),full(sm.shape)],
       out_shape=[sd((2*nW,SLAB,D),BF),sd((EDGE,D),BF),sd((2,SLAB,D),BF),sd((EDGE,D),BF),sd((rows,cols),F32),sd((rows,more),F32),sd((NH//2,nh*256),F32),sd(sm.shape,F32)],

time: 243 us -> 238 us (0.979)
  Pallas kernels: 241 us -> 235 us
    pallas_call x1, Pallas kernels: 103 us -> 97.1 us  [call_bc(): pl.pallas_call(functools.partial(kernel_bc, NH), grid=(nW,), in_specs=[pe...]
where the time goes in v10:
time: 238 us; the launch traced here: 237 us
  Pallas kernels  235 us (99%)
    pallas_call x1, Pallas kernels, call_bc(): pl.pallas_call(functools.partial(kernel_bc, NH), grid=(nW,), in_specs=[pe...  97.1 us
    pallas_call x1, Pallas kernels, call_a2(): pl.pallas_call(functools.partial(kernel_a2, NH), grid=(2 * nW,), in_specs...  88.2 us
    pallas_call x1, Pallas kernels, call_w(): pl.pallas_call(kernel_w, grid=(1,), out_shape=[sd((2, 16 * rows, early),...  36.3 us
    pallas_call x1, Pallas kernels, call_f(): pl.pallas_call(kernel_f, grid=(n,), in_specs=[blk, blk, slab, pl.BlockSpe...  13.4 us

profile of v10, /device:TPU:0, one launch (start us, length us, event | category | flops | bytes accessed | tf_op | source)
XLA Modules:
  0.0 237.3 jit_solution(14379160933920687681)
XLA Ops:
  0.6 1.4 reshape.24.lab_ref
  2.0 36.3 %kernel_w.1 = (bf16[2,512,1536]{2,1,0:T(8,128)(2,1)}, f32[16,392,384]{2,1,0:T(8,128)}, f32[2,392,128]{2,1,0:T(8,128)}, bf16[32,1536]{1,0:T(8,128)(2,1)}, s32[392,512]{1,0:T(8,128)}) custom-call(f32[3,32,256]{2,1,0:T(8,128)} %qkv_ref.1, f32[32,256]{1,0:T(8,128)} %bitcast.7, f32[32,1024]{1,0:T(8,128)} %fc1_ref.1, f32[32,1024]{1,0:T(8,128)} %bitcast.6, ...), custom_call_target="tpu_custom_call" | custom-call | tf_op jit(solution)/shard_map/kernel_w/pallas_call | solution.py:526
  38.4 88.2 %kernel_a2.1 = (bf16[4,3,392,512]{3,2,1,0:T(8,128)(2,1)}, f32[4,392,512]{2,1,0:T(8,128)}, bf16[4,4,392,1536]{3,2,1,0:T(8,128)(2,1)}, bf16[4,392,128]{2,1,0:T(8,1...) custom-call(f32[3136,512]{1,0:T(8,128)} %in_ref.1, ...), custom_call_target="tpu_custom_call" | custom-call | tf_op jit(solution)/shard_map/kernel_a2/pallas_call | solution.py:753
  126.6 97.1 %kernel_bc.1 = (bf16[8,400,512]{2,1,0:T(8,128)(2,1)}, bf16[208,512]{1,0:T(8,128)(2,1)}, bf16[2,400,512]{2,1,0:T(8,128)(2,1)}, bf16[208,512]{1,0:T(8,128)(2,1)}, ...) custom-call(f32[4,392,512]{2,1,0:T(8,128)} %get-tuple-element.48.x_ref, ...), custom_call_target="tpu_custom_call" | custom-call | tf_op jit(solution)/shard_map/kernel_bc/pallas_call | solution.py:1057
  223.7 13.4 %kernel_f.1 = (f32[3136,512]{1,0:T(8,128)}, f32[3136,512]{1,0:T(8,128)}, f32[3,32,256]{2,1,0:T(8,128)}, f32[32,256]{1,0:T(8,128)}, f32[32,1024]{1,0:T(8,128)}, /...) custom-call(f32[3136,512]{1,0:T(8,128)} %in_ref.1, f32[3136,512]{1,0:T(8,128)} %og_ref.1, ...), custom_call_target="tpu_custom_call" | custom-call | tf_op jit(solution)/shard_map/kernel_f/pallas_call | solution.py:1096

commit v11 on v10

--- a/solution.py
+++ b/solution.py
@@ -921,7 +921,7 @@
         @pl.when(y==1)
         def _():
             early(2).start(); early(3).start()
-    plan=((0,met),(2,big.one),(7,lambda: big.turn(0)),(11,lambda: big.turn(1)),(14,lambda: big.turn(2)))
+    plan=((0,met),(2,big.one),(8,lambda: big.turn(0)),(11,lambda: big.turn(1)),(14,lambda: big.turn(2)))
     kT_s[...]=qkv_ref[0,1].T
     lane=lax.broadcasted_iota(jnp.int32,(WIN,GROUP),1)
     hl=lane//HD

time: 238 us -> 243 us (1.021)
  Pallas kernels: 235 us -> 241 us
    pallas_call x1, Pallas kernels: 97.1 us -> 103 us  [call_bc(): pl.pallas_call(functools.partial(kernel_bc, NH), grid=(nW,), in_specs=[pe...]
where the time goes in v11:
time: 243 us
  Pallas kernels  241 us (99%)
    pallas_call x1, Pallas kernels, call_bc(): pl.pallas_call(functools.partial(kernel_bc, NH), grid=(nW,), in_specs=[pe...  103 us
    pallas_call x1, Pallas kernels, call_a2(): pl.pallas_call(functools.partial(kernel_a2, NH), grid=(2 * nW,), in_specs...  88.2 us
    pallas_call x1, Pallas kernels, call_w(): pl.pallas_call(kernel_w, grid=(1,), out_shape=[sd((2, 16 * rows, early),...  36.3 us
    pallas_call x1, Pallas kernels, call_f(): pl.pallas_call(kernel_f, grid=(n,), in_specs=[blk, blk, slab, pl.BlockSpe...  13.4 us

profile of v11, /device:TPU:0, one launch (start us, length us, event | category | flops | bytes accessed | tf_op | source)
XLA Modules:
  0.0 243.0 jit_solution(15234442424036395771)
XLA Ops:
  0.6 1.4 reshape.24.lab_ref
  2.0 36.3 %kernel_w.1 = (bf16[2,512,1536]{2,1,0:T(8,128)(2,1)}, f32[16,392,384]{2,1,0:T(8,128)}, f32[2,392,128]{2,1,0:T(8,128)}, bf16[32,1536]{1,0:T(8,128)(2,1)}, s32[392,512]{1,0:T(8,128)}) custom-call(f32[3,32,256]{2,1,0:T(8,128)} %qkv_ref.1, f32[32,256]{1,0:T(8,128)} %bitcast.7, f32[32,1024]{1,0:T(8,128)} %fc1_ref.1, f32[32,1024]{1,0:T(8,128)} %bitcast.6, ...), custom_call_target="tpu_custom_call" | custom-call | tf_op jit(solution)/shard_map/kernel_w/pallas_call | solution.py:526
  38.4 88.2 %kernel_a2.1 = (bf16[4,3,392,512]{3,2,1,0:T(8,128)(2,1)}, f32[4,392,512]{2,1,0:T(8,128)}, bf16[4,4,392,1536]{3,2,1,0:T(8,128)(2,1)}, bf16[4,392,128]{2,1,0:T(8,1...) custom-call(f32[3136,512]{1,0:T(8,128)} %in_ref.1, ...), custom_call_target="tpu_custom_call" | custom-call | tf_op jit(solution)/shard_map/kernel_a2/pallas_call | solution.py:753
  126.6 102.7 %kernel_bc.1 = (bf16[8,400,512]{2,1,0:T(8,128)(2,1)}, bf16[208,512]{1,0:T(8,128)(2,1)}, bf16[2,400,512]{2,1,0:T(8,128)(2,1)}, bf16[208,512]{1,0:T(8,128)(2,1)}, ...) custom-call(f32[4,392,512]{2,1,0:T(8,128)} %get-tuple-element.48.x_ref, ...), custom_call_target="tpu_custom_call" | custom-call | tf_op jit(solution)/shard_map/kernel_bc/pallas_call | solution.py:1057
  229.4 13.4 %kernel_f.1 = (f32[3136,512]{1,0:T(8,128)}, f32[3136,512]{1,0:T(8,128)}, f32[3,32,256]{2,1,0:T(8,128)}, f32[32,256]{1,0:T(8,128)}, f32[32,1024]{1,0:T(8,128)}, /...) custom-call(f32[3136,512]{1,0:T(8,128)} %in_ref.1, f32[3136,512]{1,0:T(8,128)} %og_ref.1, ...), custom_call_target="tpu_custom_call" | custom-call | tf_op jit(solution)/shard_map/kernel_f/pallas_call | solution.py:1096
